TPU v7x, 32 devices: a whole 2x2x4 slice. The times are simulated.
32 devices in a mesh: tm: 16 (over z, y, core), pb: 2 (over x).
Axes of the slice: x: 2, y: 2, z: 4, core: 2. Of those that a mesh axis runs over, the one named last changes fastest.
Arguments:
- queries: bfloat16 [4096, 768], P(('tm', 'pb')), may hold values from -64 to 64
- corpus: bfloat16 [262144, 768], P(('tm', 'pb')), may hold values from -40 to 40
- window_start: int32 [4096, 2], P(('tm', 'pb')), may hold values from 0 to 262142, as said below
- window_end: int32 [4096, 2], P(('tm', 'pb')), may hold values from 2 to 262144, as said below
Outputs:
- pooled: bfloat16 [4096, 2, 768], P(('tm', 'pb'))
- log_mass: float32 [4096, 2], P(('tm', 'pb'))
- mean_score: float32 [4096, 2], P(('tm', 'pb'))
Inputs may be any that keep to these rules, and one draw needn't show every extreme that they name: `window_start`: for query q both windows are nonempty and lie within documents (q // 128 - 1) * 8192 to (q // 128 + 2) * 8192 - 1, that is the time block of q and the blocks just before and after it. window_end[q, w] > window_start[q, w], and window_end[q, w] <= (q // 128 + 2) * 8192.
All inputs are finite; a program needn't handle non-finite values.
Results may differ from a plain program's by a relative error of at most 0.0051.
Values may be sent and summed in bfloat16 or wider, within the bound.
No kernel may reach another device: no remote copies, remote signals or barrier semaphores. Data moves between devices by JAX's collectives and lax.ppermute only.
A program may use at most 128 MiB of HBM per device.

v0:
```python
from functools import reduce
import math

import jax
import jax.numpy as jnp
from jax import lax
from jax.sharding import PartitionSpec as P

NEG_FILL = -1e30
SCORE_SCALE = 3.0


def shifted(shard, axis, by):
    size = lax.axis_size(axis)
    pairs = [(i, i + by) for i in range(size) if 0 <= i + by < size]
    return lax.ppermute(shard, axis, pairs)


def block_state(query_rows, first_doc, stop_doc, block, start_doc):
    scores = lax.dot_general(
        query_rows, block, (((1,), (1,)), ((), ())), preferred_element_type=jnp.float32
    )
    scores = scores * (SCORE_SCALE / math.sqrt(block.shape[1]))
    doc_index = start_doc + jnp.arange(block.shape[0], dtype=jnp.int32)
    maxima, totals, parts, score_sums, counts = ([], [], [], [], [])
    for window in range(2):
        inside = (doc_index[None, :] >= first_doc[:, window : window + 1]) & (
            doc_index[None, :] < stop_doc[:, window : window + 1]
        )
        window_max = jnp.max(jnp.where(inside, scores, NEG_FILL), axis=1)
        weights = jnp.where(inside, jnp.exp(scores - window_max[:, None]), 0.0)
        maxima.append(window_max)
        totals.append(jnp.sum(weights, axis=1))
        parts.append(
            jnp.dot(weights.astype(jnp.bfloat16), block, preferred_element_type=jnp.float32).astype(
                jnp.bfloat16
            )
        )
        score_sums.append(jnp.sum(jnp.where(inside, scores, 0.0), axis=1))
        counts.append(jnp.sum(inside.astype(jnp.float32), axis=1))
    return (
        jnp.stack(maxima, 1),
        jnp.stack(totals, 1),
        jnp.stack(parts, 1),
        jnp.stack(score_sums, 1),
        jnp.stack(counts, 1),
    )


def combine(states):
    tops = [jnp.where(member[4] > 0, member[0], NEG_FILL) for member in states]
    overall = reduce(jnp.maximum, tops)
    rescale = [jnp.exp(value - overall) for value in tops]
    denominator = reduce(jnp.add, [factor * member[1] for factor, member in zip(rescale, states)])
    weighted = reduce(
        jnp.add,
        [
            factor[..., None] * member[2].astype(jnp.float32)
            for factor, member in zip(rescale, states)
        ],
    )
    pooled = (weighted / denominator[..., None]).astype(jnp.bfloat16)
    log_mass = overall + jnp.log(denominator)
    mean_score = reduce(jnp.add, [member[3] for member in states]) / reduce(
        jnp.add, [member[4] for member in states]
    )
    return (pooled, log_mass, mean_score)


def local(queries, corpus, window_start, window_end):
    block_rows = corpus.shape[0]
    position = lax.axis_index(("tm", "pb"))
    start_doc = position * block_rows
    own_state = block_state(queries, window_start, window_end, corpus, start_doc)
    prior_rows, prior_first, prior_stop = shifted(
        (queries, window_start, window_end), ("tm", "pb"), 1
    )
    next_rows, next_first, next_stop = shifted(
        (queries, window_start, window_end), ("tm", "pb"), -1
    )
    for_prior = block_state(prior_rows, prior_first, prior_stop, corpus, start_doc)
    for_next = block_state(next_rows, next_first, next_stop, corpus, start_doc)
    upper_stats = shifted(
        (for_prior[0], for_prior[1], for_prior[3], for_prior[4]), ("tm", "pb"), -1
    )
    upper_parts = shifted(for_prior[2], ("tm", "pb"), -1)
    lower_stats = shifted((for_next[0], for_next[1], for_next[3], for_next[4]), ("tm", "pb"), 1)
    lower_parts = shifted(for_next[2], ("tm", "pb"), 1)
    upper_state = (upper_stats[0], upper_stats[1], upper_parts, upper_stats[2], upper_stats[3])
    lower_state = (lower_stats[0], lower_stats[1], lower_parts, lower_stats[2], lower_stats[3])
    return combine([lower_state, own_state, upper_state])


def solution(mesh):
    placed = (
        P(("tm", "pb"), None),
        P(("tm", "pb"), None),
        P(("tm", "pb"), None),
        P(("tm", "pb"), None),
    )
    return jax.shard_map(
        local,
        mesh=mesh,
        in_specs=placed,
        out_specs=(P(("tm", "pb"), None, None), P(("tm", "pb"), None), P(("tm", "pb"), None)),
        check_vma=False,
    )
```

profile of v0, /device:TPU:1, one launch (start us, length us, event | category | flops | bytes accessed | tf_op | source)
XLA Modules:
  0.0 125.2 jit_solution(5886967264530635660)
XLA Ops:
  0.6 3.9 %collective-permute-start.5 = (s32[128,2]{0,1:T(2,128)}, s32[128,2]{0,1:T(2,128)S(1)}, u32[]{:S(2)}, u32[]{:S(2)}) collective-permute-start(s32[128,2]{0,1:T(2,128)} %param.6), channel_id=1, source_target_pairs={{0,1},{1,2},{2,3},{3,4},{4,5},{5,6},{6,7},{7,8},{8,9},{9,10},{10,1... | collective-permute-start | bytes 3080 | tf_op jit(solution)/shard_map/ppermute | solution.py:16
  4.6 2.5 %collective-permute-start = (s32[128,2]{0,1:T(2,128)}, s32[128,2]{0,1:T(2,128)S(1)}, u32[]{:S(2)}, u32[]{:S(2)}) collective-permute-start(s32[128,2]{0,1:T(2,128)} %param.6), channel_id=1, source_target_pairs={{1,0},{2,1},{3,2},{4,3},{5,4},{6,5},{7,6},{8,7},{9,8},{10,9},{11,1... | collective-permute-start | bytes 3080 | tf_op jit(solution)/shard_map/ppermute | solution.py:16
  7.1 3.9 %collective-permute-start.1 = (s32[128,2]{0,1:T(2,128)}, s32[128,2]{0,1:T(2,128)S(1)}, u32[]{:S(2)}, u32[]{:S(2)}) collective-permute-start(s32[128,2]{0,1:T(2,128)} %param.7), channel_id=1, source_target_pairs={{1,0},{2,1},{3,2},{4,3},{5,4},{6,5},{7,6},{8,7},{9,8},{10,9},{11,1... | collective-permute-start | bytes 3080 | tf_op jit(solution)/shard_map/ppermute | solution.py:16
  11.0 1.9 %collective-permute-start.6 = (s32[128,2]{0,1:T(2,128)}, s32[128,2]{0,1:T(2,128)S(1)}, u32[]{:S(2)}, u32[]{:S(2)}) collective-permute-start(s32[128,2]{0,1:T(2,128)} %param.7), channel_id=1, source_target_pairs={{0,1},{1,2},{2,3},{3,4},{4,5},{5,6},{6,7},{7,8},{8,9},{9,10},{10,1... | collective-permute-start | bytes 3080 | tf_op jit(solution)/shard_map/ppermute | solution.py:16
  12.9 3.6 %collective-permute-start.3 = (bf16[128,768]{1,0:T(8,128)(2,1)}, bf16[128,768]{1,0:T(8,128)(2,1)S(1)}, u32[]{:S(2)}, u32[]{:S(2)}) collective-permute-start(bf16[128,768]{1,0:T(8,128)(2,1)} %param.4), channel_id=1, source_target_pairs={{1,0},{2,1},{3,2},{4,3},{5,4},{6,5},{7,6},{8,7},{9,8},{10,9},{11,1... | collective-permute-start | bytes 589832 | tf_op jit(solution)/shard_map/ppermute | solution.py:16
  16.6 0.8 slice_bitcast_fusion.4
  17.4 11.6 %select_reduce_fusion.9 = (f32[128]{0:T(128)S(1)}, f32[128]{0:T(128)S(1)}, f32[128]{0:T(128)S(1)}, f32[128,8192]{1,0:T(8,128)}) fusion(s32[128]{0:T(128)S(1)} %get-tuple-element.64, s32[128]{0:T(128)S(1)} %get-tuple-element.67, s32[8192]{0:T(1024)S(1)} %iota_add_fusion, s32[128]{0:T(128)S(1)} %get-tuple-element.63, s32[128]{0:T(128)S(1)} %get-tuple-element.68, ...), kind=kOutput, calls=%fused_computation.20 | convolution fusion | flops 1624243840 | bytes 17010176 | tf_op jit(solution)/shard_map/dot_general | solution.py:20
  29.0 4.5 %fusion.60 = bf16[128,1,768]{2,0,1:T(8,128)(2,1)S(1)} fusion(bf16[8192,768]{1,0:T(8,128)(2,1)S(1)} %copy-done, f32[128,8192]{1,0:T(8,128)} %get-tuple-element.65, f32[128]{0:T(128)S(1)} %get-tuple-element.25, s32[8192]{0:T(1024)S(1)} %iota_add_fusion, s32[128]{0:T(128)S(1)} %get-tuple-element.63, s32[128]{0:T(128)S(1)} %get-tuple-element.68), kind=kOutput, calls=%fused_computation.71 | convolution fusion | flops 1617002496 | bytes 17008128 | tf_op jit(solution)/shard_map/dot_general | solution.py:35
  33.6 2.2 %collective-permute-start.8 = (bf16[128,768]{1,0:T(8,128)(2,1)S(1)}, bf16[128,768]{1,0:T(8,128)(2,1)S(1)}, u32[]{:S(2)}, u32[]{:S(2)}) collective-permute-start(bf16[128,768]{1,0:T(8,128)(2,1)S(1)} %copy-done.3), channel_id=1, source_target_pairs={{0,1},{1,2},{2,3},{3,4},{4,5},{5,6},{6,7},{7,8},{8,9},{9,10},{10,1... | collective-permute-start | bytes 589832 | tf_op jit(solution)/shard_map/ppermute | solution.py:16
  35.8 6.1 %convolution_multiply_fusion.2 = f32[128,8192]{1,0:T(8,128)} fusion(bf16[128,768]{1,0:T(8,128)(2,1)S(1)} %collective-permute-done.3, bf16[8192,768]{1,0:T(8,128)(2,1)S(1)} %copy-done), kind=kOutput, calls=%fused_computation.2 | convolution fusion | flops 1611661312 | bytes 16973824 | tf_op jit(solution)/shard_map/dot_general | solution.py:20
  42.0 14.7 %select_reduce_fusion.3 = (f32[128]{0:T(128)S(1)}, f32[128]{0:T(128)S(1)}, f32[128]{0:T(128)S(1)}, f32[128]{0:T(128)S(1)}, f32[128]{0:T(128)S(1)}, /*index=5*/f3...) fusion(f32[128,8192]{1,0:T(8,128)} %get-tuple-element.65, ...), kind=kOutput, calls=%fused_computation.6 | convolution fusion | flops 1655700096 | bytes 25408000 | tf_op jit(solution)/shard_map/dot_general | solution.py:20
  56.7 4.8 %fusion.69 = bf16[128,1,768]{2,0,1:T(8,128)(2,1)S(1)} fusion(bf16[8192,768]{1,0:T(8,128)(2,1)S(1)} %copy-done, f32[128,8192]{1,0:T(8,128)} %convolution_multiply_fusion.2, f32[128]{0:T(128)S(1)} %get-tuple-element.41, s32[8192]{0:T(1024)S(1)} %iota_add_fusion, s32[128]{0:T(128)S(1)} %get-tuple-element.72, s32[128]{0:T(128)S(1)} %get-tuple-element.70), kind=kOutput, calls=%fused_computation.74 | convolution fusion | flops 1617002496 | bytes 17008128 | tf_op jit(solution)/shard_map/dot_general | solution.py:35
  61.6 2.4 %fusion.66 = bf16[128,1,768]{2,0,1:T(8,128)(2,1)S(1)} fusion(bf16[8192,768]{1,0:T(8,128)(2,1)S(1)} %copy-done, f32[128,8192]{1,0:T(8,128)S(1)} %copy-done.1, f32[128]{0:T(128)S(1)} %get-tuple-element.40, s32[8192]{0:T(1024)S(1)} %iota_add_fusion, s32[128]{0:T(128)S(1)} %get-tuple-element.71, s32[128]{0:T(128)S(1)} %get-tuple-element.69), kind=kOutput, calls=%fused_computation.73 | convolution fusion | flops 1617002496 | bytes 17008128 | tf_op jit(solution)/shard_map/dot_general | solution.py:35
  64.1 2.4 %fusion.57 = bf16[128,1,768]{2,0,1:T(8,128)(2,1)S(1)} fusion(bf16[8192,768]{1,0:T(8,128)(2,1)S(1)} %copy-done, f32[128,8192]{1,0:T(8,128)S(1)} %copy-done.2, f32[128]{0:T(128)S(1)} %get-tuple-element.38, s32[8192]{0:T(1024)S(1)} %iota_add_fusion, s32[128]{0:T(128)S(1)} %get-tuple-element.59, s32[128]{0:T(128)S(1)} %get-tuple-element.57), kind=kOutput, calls=%fused_computation.70 | convolution fusion | flops 1617002496 | bytes 17008128 | tf_op jit(solution)/shard_map/dot_general | solution.py:35
  66.5 8.6 %select_reduce_fusion.5 = (f32[128]{0:T(128)S(1)}, f32[128]{0:T(128)S(1)}, f32[128]{0:T(128)S(1)}, f32[128]{0:T(128)S(1)}, f32[128]{0:T(128)S(1)}, /*index=5*/f3...) fusion(f32[128,8192]{1,0:T(8,128)S(1)} %copy-done.1, ...), kind=kLoop, calls=%fused_computation.8 | loop fusion | flops 37747456 | bytes 8432640 | tf_op jit(solution)/shard_map/reduce_sum | solution.py:39
  75.1 2.4 %fusion.54 = bf16[128,1,768]{2,0,1:T(8,128)(2,1)S(1)} fusion(bf16[8192,768]{1,0:T(8,128)(2,1)S(1)} %copy-done, f32[128,8192]{1,0:T(8,128)S(1)} %copy-done.2, f32[128]{0:T(128)S(1)} %get-tuple-element.37, s32[8192]{0:T(1024)S(1)} %iota_add_fusion, s32[128]{0:T(128)S(1)} %get-tuple-element.60, s32[128]{0:T(128)S(1)} %get-tuple-element.58), kind=kOutput, calls=%fused_computation.69 | convolution fusion | flops 1617002496 | bytes 17008128 | tf_op jit(solution)/shard_map/dot_general | solution.py:35
  77.6 4.5 %collective-permute-start.14 = (f32[128,2]{0,1:T(2,128)S(1)}, f32[128,2]{0,1:T(2,128)S(1)}, u32[]{:S(2)}, u32[]{:S(2)}) collective-permute-start(f32[128,2]{0,1:T(2,128)S(1)} %pad_maximum_fusion.9), channel_id=1, source_target_pairs={{0,1},{1,2},{2,3},{3,4},{4,5},{5,6},{6,7},{7,8},{8,9},{9,10},{10,1... | collective-permute-start | bytes 3080 | tf_op jit(solution)/shard_map/ppermute | solution.py:16
  82.1 1.9 %collective-permute-start.15 = (f32[128,2]{0,1:T(2,128)S(1)}, f32[128,2]{0,1:T(2,128)S(1)}, u32[]{:S(2)}, u32[]{:S(2)}) collective-permute-start(f32[128,2]{0,1:T(2,128)S(1)} %pad_maximum_fusion.10), channel_id=1, source_target_pairs={{1,0},{2,1},{3,2},{4,3},{5,4},{6,5},{7,6},{8,7},{9,8},{10,9},{11,1... | collective-permute-start | bytes 3080 | tf_op jit(solution)/shard_map/ppermute | solution.py:16
  84.1 2.9 %collective-permute-start.7 = (f32[128,2]{0,1:T(2,128)S(1)}, f32[128,2]{0,1:T(2,128)S(1)}, u32[]{:S(2)}, u32[]{:S(2)}) collective-permute-start(f32[128,2]{0,1:T(2,128)S(1)} %pad_maximum_fusion.5), channel_id=1, source_target_pairs={{1,0},{2,1},{3,2},{4,3},{5,4},{6,5},{7,6},{8,7},{9,8},{10,9},{11,1... | collective-permute-start | bytes 3080 | tf_op jit(solution)/shard_map/ppermute | solution.py:16
  87.0 1.9 %collective-permute-start.9 = (f32[128,2]{0,1:T(2,128)S(1)}, f32[128,2]{0,1:T(2,128)S(1)}, u32[]{:S(2)}, u32[]{:S(2)}) collective-permute-start(f32[128,2]{0,1:T(2,128)S(1)} %pad_maximum_fusion.6), channel_id=1, source_target_pairs={{1,0},{2,1},{3,2},{4,3},{5,4},{6,5},{7,6},{8,7},{9,8},{10,9},{11,1... | collective-permute-start | bytes 3080 | tf_op jit(solution)/shard_map/ppermute | solution.py:16
  89.0 3.4 %collective-permute-start.2 = (f32[128,2]{0,1:T(2,128)S(1)}, f32[128,2]{0,1:T(2,128)S(1)}, u32[]{:S(2)}, u32[]{:S(2)}) collective-permute-start(f32[128,2]{0,1:T(2,128)S(1)} %pad_maximum_fusion.2), channel_id=1, source_target_pairs={{0,1},{1,2},{2,3},{3,4},{4,5},{5,6},{6,7},{7,8},{8,9},{9,10},{10,1... | collective-permute-start | bytes 3080 | tf_op jit(solution)/shard_map/ppermute | solution.py:16
  92.5 3.6 %collective-permute-start.4 = (f32[128,2]{0,1:T(2,128)S(1)}, f32[128,2]{0,1:T(2,128)S(1)}, u32[]{:S(2)}, u32[]{:S(2)}) collective-permute-start(f32[128,2]{0,1:T(2,128)S(1)} %pad_maximum_fusion.3), channel_id=1, source_target_pairs={{0,1},{1,2},{2,3},{3,4},{4,5},{5,6},{6,7},{7,8},{8,9},{9,10},{10,1... | collective-permute-start | bytes 3080 | tf_op jit(solution)/shard_map/ppermute | solution.py:16
  96.1 3.9 %collective-permute-start.12 = (f32[128,2]{0,1:T(2,128)S(1)}, f32[128,2]{0,1:T(2,128)S(1)}, u32[]{:S(2)}, u32[]{:S(2)}) collective-permute-start(f32[128,2]{0,1:T(2,128)S(1)} %pad_maximum_fusion.7), channel_id=1, source_target_pairs={{0,1},{1,2},{2,3},{3,4},{4,5},{5,6},{6,7},{7,8},{8,9},{9,10},{10,1... | collective-permute-start | bytes 3080 | tf_op jit(solution)/shard_map/ppermute | solution.py:16
  100.0 1.9 %collective-permute-start.13 = (f32[128,2]{0,1:T(2,128)S(1)}, f32[128,2]{0,1:T(2,128)S(1)}, u32[]{:S(2)}, u32[]{:S(2)}) collective-permute-start(f32[128,2]{0,1:T(2,128)S(1)} %pad_maximum_fusion.8), channel_id=1, source_target_pairs={{1,0},{2,1},{3,2},{4,3},{5,4},{6,5},{7,6},{8,7},{9,8},{10,9},{11,1... | collective-permute-start | bytes 3080 | tf_op jit(solution)/shard_map/ppermute | solution.py:16
  101.9 3.6 %collective-permute-start.10 = (bf16[128,2,768]{2,0,1:T(8,128)(2,1)S(1)}, bf16[128,2,768]{2,0,1:T(8,128)(2,1)S(1)}, u32[]{:S(2)}, u32[]{:S(2)}) collective-permute-start(bf16[128,2,768]{2,0,1:T(8,128)(2,1)S(1)} %pad_maximum_fusion), channel_id=1, source_target_pairs={{0,1},{1,2},{2,3},{3,4},{4,5},{5,6},{6,7},{7,8},{8,9},{9,10},{10,1... | collective-permute-start | bytes 1179656 | tf_op jit(solution)/shard_map/ppermute | solution.py:16
  105.5 2.0 %collective-permute-start.11 = (bf16[128,2,768]{2,0,1:T(8,128)(2,1)S(1)}, bf16[128,2,768]{2,0,1:T(8,128)(2,1)S(1)}, u32[]{:S(2)}, u32[]{:S(2)}) collective-permute-start(bf16[128,2,768]{2,0,1:T(8,128)(2,1)S(1)} %pad_maximum_fusion.1), channel_id=1, source_target_pairs={{1,0},{2,1},{3,2},{4,3},{5,4},{6,5},{7,6},{8,7},{9,8},{10,9},{11,1... | collective-permute-start | bytes 1179656 | tf_op jit(solution)/shard_map/ppermute | solution.py:16
  107.5 2.4 %fusion.63 = bf16[128,1,768]{2,0,1:T(8,128)(2,1)S(1)} fusion(bf16[8192,768]{1,0:T(8,128)(2,1)S(1)} %copy-done, f32[128,8192]{1,0:T(8,128)S(1)} %copy-done.4, f32[128]{0:T(128)S(1)} %get-tuple-element.24, s32[8192]{0:T(1024)S(1)} %iota_add_fusion, s32[128]{0:T(128)S(1)} %get-tuple-element.64, s32[128]{0:T(128)S(1)} %get-tuple-element.67), kind=kOutput, calls=%fused_computation.72 | convolution fusion | flops 1617002496 | bytes 17008128 | tf_op jit(solution)/shard_map/dot_general | solution.py:35
  110.0 0.6 log_add_fusion
  110.6 2.8 %collective-permute-done.10 = bf16[128,2,768]{2,0,1:T(8,128)(2,1)S(1)} collective-permute-done((bf16[128,2,768]{2,0,1:T(8,128)(2,1)S(1)}, bf16[128,2,768]{2,0,1:T(8,128)(2,1)S(1)}, u32[]{:S(2)}, u32[]{:S(2)}) %collective-permute-start.10) | collective-permute-done | bytes 393248 | tf_op jit(solution)/shard_map/ppermute | solution.py:16
  113.4 10.2 %collective-permute-done.11 = bf16[128,2,768]{2,0,1:T(8,128)(2,1)S(1)} collective-permute-done((bf16[128,2,768]{2,0,1:T(8,128)(2,1)S(1)}, bf16[128,2,768]{2,0,1:T(8,128)(2,1)S(1)}, u32[]{:S(2)}, u32[]{:S(2)}) %collective-permute-start.11) | collective-permute-done | bytes 393248 | tf_op jit(solution)/shard_map/ppermute | solution.py:16
  123.7 0.3 divide_convert_fusion
  124.0 1.2 copy.7
  (37 shorter events, 0.3 us)
Async XLA Ops:
  0.6 35.1 %collective-permute-start.5 = (s32[128,2]{0,1:T(2,128)}, s32[128,2]{0,1:T(2,128)S(1)}, u32[]{:S(2)}, u32[]{:S(2)}) collective-permute-start(s32[128,2]{0,1:T(2,128)} %param.6), channel_id=1, source_target_pairs={{0,1},{1,2},{2,3},{3,4},{4,5},{5,6},{6,7},{7,8},{8,9},{9,10},{10,1... | collective-permute-start | bytes 3080 | tf_op jit(solution)/shard_map/ppermute | solution.py:16
  4.6 31.2 %collective-permute-start = (s32[128,2]{0,1:T(2,128)}, s32[128,2]{0,1:T(2,128)S(1)}, u32[]{:S(2)}, u32[]{:S(2)}) collective-permute-start(s32[128,2]{0,1:T(2,128)} %param.6), channel_id=1, source_target_pairs={{1,0},{2,1},{3,2},{4,3},{5,4},{6,5},{7,6},{8,7},{9,8},{10,9},{11,1... | collective-permute-start | bytes 3080 | tf_op jit(solution)/shard_map/ppermute | solution.py:16
  7.1 26.5 %collective-permute-start.1 = (s32[128,2]{0,1:T(2,128)}, s32[128,2]{0,1:T(2,128)S(1)}, u32[]{:S(2)}, u32[]{:S(2)}) collective-permute-start(s32[128,2]{0,1:T(2,128)} %param.7), channel_id=1, source_target_pairs={{1,0},{2,1},{3,2},{4,3},{5,4},{6,5},{7,6},{8,7},{9,8},{10,9},{11,1... | collective-permute-start | bytes 3080 | tf_op jit(solution)/shard_map/ppermute | solution.py:16
  11.0 24.8 %collective-permute-start.6 = (s32[128,2]{0,1:T(2,128)}, s32[128,2]{0,1:T(2,128)S(1)}, u32[]{:S(2)}, u32[]{:S(2)}) collective-permute-start(s32[128,2]{0,1:T(2,128)} %param.7), channel_id=1, source_target_pairs={{0,1},{1,2},{2,3},{3,4},{4,5},{5,6},{6,7},{7,8},{8,9},{9,10},{10,1... | collective-permute-start | bytes 3080 | tf_op jit(solution)/shard_map/ppermute | solution.py:16
  12.9 22.9 %collective-permute-start.3 = (bf16[128,768]{1,0:T(8,128)(2,1)}, bf16[128,768]{1,0:T(8,128)(2,1)S(1)}, u32[]{:S(2)}, u32[]{:S(2)}) collective-permute-start(bf16[128,768]{1,0:T(8,128)(2,1)} %param.4), channel_id=1, source_target_pairs={{1,0},{2,1},{3,2},{4,3},{5,4},{6,5},{7,6},{8,7},{9,8},{10,9},{11,1... | collective-permute-start | bytes 589832 | tf_op jit(solution)/shard_map/ppermute | solution.py:16
  17.4 11.7 %copy-start = (bf16[8192,768]{1,0:T(8,128)(2,1)S(1)}, bf16[8192,768]{1,0:T(8,128)(2,1)}, u32[]{:S(2)}) copy-start(bf16[8192,768]{1,0:T(8,128)(2,1)} %param.5) | copy-start | bytes 37748740
  29.0 4.5 %copy-start.3 = (bf16[128,768]{1,0:T(8,128)(2,1)S(1)}, bf16[128,768]{1,0:T(8,128)(2,1)}, u32[]{:S(2)}) copy-start(bf16[128,768]{1,0:T(8,128)(2,1)} %param.4) | copy-start | bytes 589828
  33.6 8.4 %collective-permute-start.8 = (bf16[128,768]{1,0:T(8,128)(2,1)S(1)}, bf16[128,768]{1,0:T(8,128)(2,1)S(1)}, u32[]{:S(2)}, u32[]{:S(2)}) collective-permute-start(bf16[128,768]{1,0:T(8,128)(2,1)S(1)} %copy-done.3), channel_id=1, source_target_pairs={{0,1},{1,2},{2,3},{3,4},{4,5},{5,6},{6,7},{7,8},{8,9},{9,10},{10,1... | collective-permute-start | bytes 589832 | tf_op jit(solution)/shard_map/ppermute | solution.py:16
  56.7 4.9 %copy-start.1 = (f32[128,8192]{1,0:T(8,128)S(1)}, f32[128,8192]{1,0:T(8,128)}, u32[]{:S(2)}) copy-start(f32[128,8192]{1,0:T(8,128)} %convolution_multiply_fusion.2) | copy-start | bytes 12582916
  61.6 2.5 %copy-start.2 = (f32[128,8192]{1,0:T(8,128)S(1)}, f32[128,8192]{1,0:T(8,128)}, u32[]{:S(2)}) copy-start(f32[128,8192]{1,0:T(8,128)} %get-tuple-element.66) | copy-start | bytes 12582916
  75.1 32.4 %copy-start.4 = (f32[128,8192]{1,0:T(8,128)S(1)}, f32[128,8192]{1,0:T(8,128)}, u32[]{:S(2)}) copy-start(f32[128,8192]{1,0:T(8,128)} %get-tuple-element.65) | copy-start | bytes 12582916
  77.6 14.9 %collective-permute-start.14 = (f32[128,2]{0,1:T(2,128)S(1)}, f32[128,2]{0,1:T(2,128)S(1)}, u32[]{:S(2)}, u32[]{:S(2)}) collective-permute-start(f32[128,2]{0,1:T(2,128)S(1)} %pad_maximum_fusion.9), channel_id=1, source_target_pairs={{0,1},{1,2},{2,3},{3,4},{4,5},{5,6},{6,7},{7,8},{8,9},{9,10},{10,1... | collective-permute-start | bytes 3080 | tf_op jit(solution)/shard_map/ppermute | solution.py:16
  82.1 13.9 %collective-permute-start.15 = (f32[128,2]{0,1:T(2,128)S(1)}, f32[128,2]{0,1:T(2,128)S(1)}, u32[]{:S(2)}, u32[]{:S(2)}) collective-permute-start(f32[128,2]{0,1:T(2,128)S(1)} %pad_maximum_fusion.10), channel_id=1, source_target_pairs={{1,0},{2,1},{3,2},{4,3},{5,4},{6,5},{7,6},{8,7},{9,8},{10,9},{11,1... | collective-permute-start | bytes 3080 | tf_op jit(solution)/shard_map/ppermute | solution.py:16
  84.1 15.9 %collective-permute-start.7 = (f32[128,2]{0,1:T(2,128)S(1)}, f32[128,2]{0,1:T(2,128)S(1)}, u32[]{:S(2)}, u32[]{:S(2)}) collective-permute-start(f32[128,2]{0,1:T(2,128)S(1)} %pad_maximum_fusion.5), channel_id=1, source_target_pairs={{1,0},{2,1},{3,2},{4,3},{5,4},{6,5},{7,6},{8,7},{9,8},{10,9},{11,1... | collective-permute-start | bytes 3080 | tf_op jit(solution)/shard_map/ppermute | solution.py:16
  87.0 14.9 %collective-permute-start.9 = (f32[128,2]{0,1:T(2,128)S(1)}, f32[128,2]{0,1:T(2,128)S(1)}, u32[]{:S(2)}, u32[]{:S(2)}) collective-permute-start(f32[128,2]{0,1:T(2,128)S(1)} %pad_maximum_fusion.6), channel_id=1, source_target_pairs={{1,0},{2,1},{3,2},{4,3},{5,4},{6,5},{7,6},{8,7},{9,8},{10,9},{11,1... | collective-permute-start | bytes 3080 | tf_op jit(solution)/shard_map/ppermute | solution.py:16
  89.0 16.6 %collective-permute-start.2 = (f32[128,2]{0,1:T(2,128)S(1)}, f32[128,2]{0,1:T(2,128)S(1)}, u32[]{:S(2)}, u32[]{:S(2)}) collective-permute-start(f32[128,2]{0,1:T(2,128)S(1)} %pad_maximum_fusion.2), channel_id=1, source_target_pairs={{0,1},{1,2},{2,3},{3,4},{4,5},{5,6},{6,7},{7,8},{8,9},{9,10},{10,1... | collective-permute-start | bytes 3080 | tf_op jit(solution)/shard_map/ppermute | solution.py:16
  92.5 17.5 %collective-permute-start.4 = (f32[128,2]{0,1:T(2,128)S(1)}, f32[128,2]{0,1:T(2,128)S(1)}, u32[]{:S(2)}, u32[]{:S(2)}) collective-permute-start(f32[128,2]{0,1:T(2,128)S(1)} %pad_maximum_fusion.3), channel_id=1, source_target_pairs={{0,1},{1,2},{2,3},{3,4},{4,5},{5,6},{6,7},{7,8},{8,9},{9,10},{10,1... | collective-permute-start | bytes 3080 | tf_op jit(solution)/shard_map/ppermute | solution.py:16
  96.1 13.9 %collective-permute-start.12 = (f32[128,2]{0,1:T(2,128)S(1)}, f32[128,2]{0,1:T(2,128)S(1)}, u32[]{:S(2)}, u32[]{:S(2)}) collective-permute-start(f32[128,2]{0,1:T(2,128)S(1)} %pad_maximum_fusion.7), channel_id=1, source_target_pairs={{0,1},{1,2},{2,3},{3,4},{4,5},{5,6},{6,7},{7,8},{8,9},{9,10},{10,1... | collective-permute-start | bytes 3080 | tf_op jit(solution)/shard_map/ppermute | solution.py:16
  100.0 10.0 %collective-permute-start.13 = (f32[128,2]{0,1:T(2,128)S(1)}, f32[128,2]{0,1:T(2,128)S(1)}, u32[]{:S(2)}, u32[]{:S(2)}) collective-permute-start(f32[128,2]{0,1:T(2,128)S(1)} %pad_maximum_fusion.8), channel_id=1, source_target_pairs={{1,0},{2,1},{3,2},{4,3},{5,4},{6,5},{7,6},{8,7},{9,8},{10,9},{11,1... | collective-permute-start | bytes 3080 | tf_op jit(solution)/shard_map/ppermute | solution.py:16
  101.9 11.5 %collective-permute-start.10 = (bf16[128,2,768]{2,0,1:T(8,128)(2,1)S(1)}, bf16[128,2,768]{2,0,1:T(8,128)(2,1)S(1)}, u32[]{:S(2)}, u32[]{:S(2)}) collective-permute-start(bf16[128,2,768]{2,0,1:T(8,128)(2,1)S(1)} %pad_maximum_fusion), channel_id=1, source_target_pairs={{0,1},{1,2},{2,3},{3,4},{4,5},{5,6},{6,7},{7,8},{8,9},{9,10},{10,1... | collective-permute-start | bytes 1179656 | tf_op jit(solution)/shard_map/ppermute | solution.py:16
  105.5 18.1 %collective-permute-start.11 = (bf16[128,2,768]{2,0,1:T(8,128)(2,1)S(1)}, bf16[128,2,768]{2,0,1:T(8,128)(2,1)S(1)}, u32[]{:S(2)}, u32[]{:S(2)}) collective-permute-start(bf16[128,2,768]{2,0,1:T(8,128)(2,1)S(1)} %pad_maximum_fusion.1), channel_id=1, source_target_pairs={{1,0},{2,1},{3,2},{4,3},{5,4},{6,5},{7,6},{8,7},{9,8},{10,9},{11,1... | collective-permute-start | bytes 1179656 | tf_op jit(solution)/shard_map/ppermute | solution.py:16
where the time goes:
time: 128 us; the launch traced here: 125 us
  matrix products  51.7 us (40%)
  starting transfers between devices  47.7 us (37%)
  waiting for transfers between devices  13.1 us (10%)
  other arithmetic  9.66 us (8%)
  local copies, waits for them, and re-layouts  1.95 us (2%)
    ppermute x16, starting transfers between devices, shifted(): return lax.ppermute(shard, axis, pairs)  47.7 us
    dot_general x3, matrix products, block_state(): lax.dot_general(query_rows, block, (((1,), (1,)), ((), ())), preferred_el...  32.5 us
    dot_general x6, matrix products, block_state(): jnp.dot(weights.astype(jnp.bfloat16), block, preferred_element_type=jnp.f...  19.2 us
    ppermute x16, waiting for transfers between devices, shifted(): return lax.ppermute(shard, axis, pairs)  13.1 us
    reduce_sum x1, other arithmetic, block_state(): score_sums.append(jnp.sum(jnp.where(inside, scores, 0.0), axis=1))  8.58 us
  transfers between devices with their start and end apart: 16, of which 2 were waited for; matrix products, arithmetic and copies ran while one was open for 21% of the time, Pallas kernels for 0%

commit v1 on v0

v1 whole, which is shorter than its diff:
```python
import functools
import math

import jax
import jax.numpy as jnp
from jax import lax
from jax.experimental import pallas as pl
from jax.experimental.pallas import tpu as pltpu
from jax.sharding import PartitionSpec as P

SCORE_SCALE = 3.0
NEG = -1e30
LOG2E = math.log2(math.e)
AXES = ("tm", "pb")
BF16 = jnp.bfloat16
F32 = jnp.float32
NT = (((1,), (1,)), ((), ()))
TN = (((0,), (0,)), ((), ()))
META = 16
LANES = 128
DOC_TILE = 1024
DOT_TILE = 256
ROW_TILE = 16

VMEM = pl.BlockSpec(memory_space=pltpu.VMEM)
SMEM = pl.BlockSpec(memory_space=pltpu.SMEM)


def params(mebibytes):
    return pltpu.CompilerParams(vmem_limit_bytes=mebibytes * 2**20)


def identity(n):
    rows = lax.broadcasted_iota(jnp.int32, (n, n), 0)
    return (rows == lax.broadcasted_iota(jnp.int32, (n, n), 1)).astype(BF16)


def split_int(value):
    return (value >> 8).astype(F32), (value & 255).astype(F32)


def split_float(value):
    high = value.astype(BF16).astype(F32)
    rest = value - high
    middle = rest.astype(BF16).astype(F32)
    return high, middle, rest - middle


def row_scratch(rows, docs, width, tile):
    return [
        pltpu.VMEM((rows, width), BF16),
        pltpu.VMEM((2, rows, LANES), jnp.int32),
        pltpu.VMEM((rows, LANES), F32),
        pltpu.VMEM((rows, LANES), F32),
        pltpu.VMEM((rows, LANES), F32),
        pltpu.VMEM((rows, tile), F32),
        pltpu.VMEM((rows, tile), F32),
        pltpu.VMEM((docs // tile, rows, tile), F32),
        pltpu.VMEM((rows, tile), BF16),
        pltpu.VMEM((rows, tile), BF16),
        pltpu.VMEM((rows, width), F32),
    ]


def attend_rows(docs, scratch):
    rows_q, bounds, peak, score_sum, mass, s_a, s_b, masked, p_a, p_b, acc = scratch
    n_docs, width = docs.shape
    rows, tile = s_a.shape
    tiles = n_docs // tile
    scale = SCORE_SCALE / math.sqrt(width)
    starts = range(0, rows, ROW_TILE)

    def share(part, parts):
        each = -(-len(starts) // parts)
        return starts[part * each : (part + 1) * each]

    def score(t, out, part):
        first = pl.multiple_of(t * tile + part * DOT_TILE, DOT_TILE)
        out[:, part * DOT_TILE : (part + 1) * DOT_TILE] = lax.dot_general(
            rows_q[...], docs[pl.ds(first, DOT_TILE), :], NT, preferred_element_type=F32
        )

    def scan(t, scores, some):
        for r in some:
            at = slice(r, r + ROW_TILE)
            offset = t * tile - bounds[0, at, :]
            length = bounds[1, at, :].astype(jnp.uint32)
            top, total = peak[at, :], score_sum[at, :]
            for c in range(0, tile, LANES):
                value = scores[at, c : c + LANES]
                inside = (offset + c).astype(jnp.uint32) < length
                kept = jnp.where(inside, value, NEG)
                top = jnp.maximum(top, kept)
                total = total + jnp.where(inside, value, 0.0)
                masked[t, at, c : c + LANES] = kept
            peak[at, :] = top
            score_sum[at, :] = total

    def score_and_scan(t_score, out, t_scan, scores):
        parts = tile // DOT_TILE
        for part in range(parts):
            score(t_score, out, part)
            scan(t_scan, scores, share(part, parts))

    peak[...] = jnp.full(peak.shape, NEG, F32)
    score_sum[...] = jnp.zeros(score_sum.shape, F32)
    mass[...] = jnp.zeros(mass.shape, F32)
    for part in range(tile // DOT_TILE):
        score(0, s_a, part)

    def first_step(i, carry):
        t = 2 * i
        score_and_scan(t + 1, s_b, t, s_a)
        score_and_scan(jnp.minimum(t + 2, tiles - 1), s_a, t + 1, s_b)
        return carry

    lax.fori_loop(0, tiles // 2, first_step, 0)
    top = jnp.max(peak[...], axis=1, keepdims=True)
    peak[...] = jnp.broadcast_to(jnp.maximum(top, 0.5 * NEG), peak.shape)
    acc[...] = jnp.zeros(acc.shape, F32)

    def weigh(t, out, some):
        for r in some:
            at = slice(r, r + ROW_TILE)
            shift, total = peak[at, :], mass[at, :]
            for c in range(0, tile, LANES):
                p = jnp.exp2((masked[t, at, c : c + LANES] - shift) * (scale * LOG2E))
                total = total + p
                out[at, c : c + LANES] = p.astype(BF16)
            mass[at, :] = total

    def pool(t, weights, part):
        at = slice(part * DOT_TILE, (part + 1) * DOT_TILE)
        block = docs[pl.ds(pl.multiple_of(t * tile, tile), tile), at]
        acc[:, at] += jnp.dot(weights[...], block, preferred_element_type=F32)

    def pool_and_weigh(t, weights, t_weigh, out):
        parts = width // DOT_TILE
        for part in range(parts):
            pool(t, weights, part)
            weigh(t_weigh, out, share(part, parts))

    weigh(0, p_a, starts)

    def second_step(i, carry):
        t = 2 * i + 1
        pool_and_weigh(t - 1, p_a, t, p_b)
        pool_and_weigh(t, p_b, t + 1, p_a)
        return carry

    lax.fori_loop(0, tiles // 2 - 1, second_step, 0)
    pool_and_weigh(tiles - 2, p_a, tiles - 1, p_b)
    for part in range(width // DOT_TILE):
        pool(tiles - 1, p_b, part)
    return (
        top * scale,
        jnp.sum(mass[...], axis=1, keepdims=True),
        jnp.sum(score_sum[...], axis=1, keepdims=True) * scale,
    )


def stats_matrix(stats):
    rows = stats[0].shape[0]
    lane = lax.broadcasted_iota(jnp.int32, (rows, META), 1)
    matrix = jnp.zeros((rows, META), F32)
    for k, value in enumerate(stats):
        for j, part in enumerate(split_float(value)):
            matrix = jnp.where(lane == 3 * k + j, part, matrix)
    return matrix.astype(BF16)


def set_bounds(bounds, at, low, length):
    shape = (low.shape[0], LANES)
    bounds[0, at, :] = low - lax.broadcasted_iota(jnp.int32, shape, 1)
    bounds[1, at, :] = jnp.broadcast_to(length, shape)


def own_kernel(shift, message, docs, out, *scratch):
    queries = message.shape[0] - META
    rows_q, bounds = scratch[:2]
    unit = identity(queries)
    columns = lax.dot_general(
        unit, message[queries:, 0:queries], NT, preferred_element_type=F32
    )

    def bound(k):
        value = columns[:, 2 * k : 2 * k + 1] * 256.0 + columns[:, 2 * k + 1 : 2 * k + 2]
        return jnp.clip(value.astype(jnp.int32) - shift[0], 0, docs.shape[0])

    for w in range(2):
        at = slice(w * queries, (w + 1) * queries)
        low = bound(w)
        set_bounds(bounds, at, low, jnp.maximum(bound(2 + w) - low, 0))
        rows_q[at, :] = message[0:queries, :]
    stats = stats_matrix(attend_rows(docs, scratch))
    out[0 : 2 * queries, :] = scratch[-1][...].astype(BF16)
    out[2 * queries :, :] = jnp.zeros((META, out.shape[1]), BF16)
    for w in range(2):
        at = slice(w * queries, (w + 1) * queries)
        out[2 * queries :, at] = lax.dot_general(
            stats[at, :], unit, TN, preferred_element_type=F32
        ).astype(BF16)


def own(shift, message, corpus):
    docs, width = corpus.shape
    queries = message.shape[0] - META
    tile = min(DOC_TILE, docs // 2)
    return pl.pallas_call(
        own_kernel,
        out_shape=jax.ShapeDtypeStruct((2 * queries + META, width), BF16),
        in_specs=[SMEM, VMEM, VMEM],
        out_specs=VMEM,
        scratch_shapes=row_scratch(2 * queries, docs, width, tile),
        compiler_params=params(20),
        cost_estimate=pl.CostEstimate(
            flops=8 * queries * docs * width,
            bytes_accessed=docs * width * 2,
            transcendentals=2 * queries * docs,
        ),
        name="own_block",
    )(shift, message, corpus)


def neighbour_kernel(shifts, near, far_a, far_b, docs, near_out, far_out, both_q, *scratch):
    queries = near.shape[0] - META
    rows_q, bounds = scratch[:2]
    group = rows_q.shape[0]
    both_q[0:queries, :] = near[0:queries, :]
    both_q[queries:, :] = far_a[0:queries, :] + far_b[0:queries, :]

    lows, lengths = [], []
    for side, meta in enumerate((near[queries:, 0:queries], far_a[queries:, 0:queries] + far_b[queries:, 0:queries])):
        meta = meta.astype(F32)

        def bound(k):
            value = meta[2 * k : 2 * k + 1, :] * 256.0 + meta[2 * k + 1 : 2 * k + 2, :]
            return jnp.clip(value.astype(jnp.int32) - shifts[side], 0, docs.shape[0])

        for w in range(2):
            low = bound(w)
            lows.append(low)
            lengths.append(jnp.maximum(bound(2 + w) - low, 0))
    blocks = len(lows)
    parts = []
    for low, length in zip(lows, lengths):
        rows = [*split_int(low), *split_int(length)]
        parts.append(jnp.concatenate(rows + [jnp.zeros((META - 4, queries), F32)], axis=0).astype(BF16))
    flags = [(length > 0).astype(F32) for length in lengths]
    stacked = jnp.concatenate(flags + [jnp.zeros((META - blocks, queries), F32)], axis=0).astype(BF16)
    before = lax.broadcasted_iota(jnp.int32, (queries, queries), 0) < lax.broadcasted_iota(
        jnp.int32, (queries, queries), 1
    )
    ranks = jnp.dot(stacked, before.astype(BF16), preferred_element_type=F32)
    places, first = [], jnp.zeros((1, 1), F32)
    for b in range(blocks):
        places.append(jnp.where(flags[b] > 0, ranks[b : b + 1, :] + first, -1.0).astype(jnp.int32))
        first = first + jnp.sum(flags[b], axis=1, keepdims=True)
    active = jnp.max(first).astype(jnp.int32)

    near_out[...] = jnp.zeros(near_out.shape, BF16)
    far_out[...] = jnp.zeros(far_out.shape, BF16)

    def work(g, carry):
        row = lax.broadcasted_iota(jnp.int32, (group, queries), 0) + g * group
        pick = [(row == place).astype(F32).astype(BF16) for place in places]
        of_query = jnp.concatenate([pick[0] + pick[1], pick[2] + pick[3]], axis=1)
        rows_q[...] = jnp.dot(of_query, both_q[...], preferred_element_type=F32).astype(BF16)
        columns = jnp.zeros((group, META), F32)
        for chosen, part in zip(pick, parts):
            columns = columns + lax.dot_general(chosen, part, NT, preferred_element_type=F32)
        low = (columns[:, 0:1] * 256.0 + columns[:, 1:2]).astype(jnp.int32)
        length = (columns[:, 2:3] * 256.0 + columns[:, 3:4]).astype(jnp.int32)
        set_bounds(bounds, slice(0, group), low, length)
        stats = stats_matrix(attend_rows(docs, scratch))
        pooled = scratch[-1][...].astype(BF16)
        for b, chosen in enumerate(pick):
            out = (near_out, far_out)[b // 2]
            at = slice((b % 2) * queries, (b % 2 + 1) * queries)
            out[at, :] += lax.dot_general(chosen, pooled, TN, preferred_element_type=F32).astype(BF16)
            out[2 * queries :, at] += lax.dot_general(
                stats, chosen, TN, preferred_element_type=F32
            ).astype(BF16)
        return carry

    lax.fori_loop(0, (active + group - 1) // group, work, 0)


def neighbours(shifts, near, far_a, far_b, corpus):
    docs, width = corpus.shape
    queries = near.shape[0] - META
    tile = min(DOC_TILE, docs // 2)
    group = min(4 * queries, (2 * queries + 3 * queries // 8) // ROW_TILE * ROW_TILE)
    result = jax.ShapeDtypeStruct((2 * queries + META, width), BF16)
    return pl.pallas_call(
        neighbour_kernel,
        out_shape=(result, result),
        in_specs=[SMEM, VMEM, VMEM, VMEM, VMEM],
        out_specs=(VMEM, VMEM),
        scratch_shapes=[pltpu.VMEM((2 * queries, width), BF16)] + row_scratch(group, docs, width, tile),
        compiler_params=params(24),
        cost_estimate=pl.CostEstimate(
            flops=8 * queries * docs * width,
            bytes_accessed=docs * width * 2,
            transcendentals=2 * queries * docs,
        ),
        name="neighbour_blocks",
    )(shifts, near, far_a, far_b, corpus)


def pack_kernel(queries, relative, out):
    rows, width = queries.shape
    out[0:rows, :] = queries[...]
    out[rows:, :] = jnp.zeros((META, width), BF16)
    high, low = split_int(relative[...])
    lines = [part[k : k + 1, :] for k in range(4) for part in (high, low)]
    lines.append(jnp.zeros((META - 8, rows), F32))
    out[rows:, 0:rows] = jnp.concatenate(lines, axis=0).astype(BF16)


def pack(queries, relative):
    rows, width = queries.shape
    return pl.pallas_call(
        pack_kernel,
        out_shape=jax.ShapeDtypeStruct((rows + META, width), BF16),
        in_specs=[VMEM, VMEM],
        out_specs=VMEM,
        name="pack",
    )(queries, relative)


def columns_of(state, unit, w):
    queries = unit.shape[0]
    lines = state[2 * queries :, w * queries : (w + 1) * queries]
    columns = lax.dot_general(unit, lines, NT, preferred_element_type=F32)
    top, total, score_sum = (
        columns[:, 3 * k : 3 * k + 1] + columns[:, 3 * k + 1 : 3 * k + 2] + columns[:, 3 * k + 2 : 3 * k + 3]
        for k in range(3)
    )
    return jnp.where(total > 0, top, NEG), total, score_sum


def weigh_states(tops):
    best = functools.reduce(jnp.maximum, tops)
    return best, [jnp.exp(top - best) for top in tops]


def merge_kernel(first, second, out):
    queries = (first.shape[0] - META) // 2
    unit = identity(queries)
    out[2 * queries :, :] = jnp.zeros((META, out.shape[1]), BF16)
    for w in range(2):
        at = slice(w * queries, (w + 1) * queries)
        states = [columns_of(state, unit, w) for state in (first, second)]
        best, factors = weigh_states([state[0] for state in states])
        total = functools.reduce(jnp.add, [f * state[1] for f, state in zip(factors, states)])
        score_sum = states[0][2] + states[1][2]
        out[at, :] = (
            factors[0] * first[at, :].astype(F32) + factors[1] * second[at, :].astype(F32)
        ).astype(BF16)
        stats = stats_matrix((best, total, score_sum))
        out[2 * queries :, at] = lax.dot_general(
            stats, unit, TN, preferred_element_type=F32
        ).astype(BF16)


def merge(first, second):
    return pl.pallas_call(
        merge_kernel,
        out_shape=jax.ShapeDtypeStruct(first.shape, BF16),
        in_specs=[VMEM, VMEM],
        out_specs=VMEM,
        name="merge",
    )(first, second)


def finish_kernel(window_start, window_end, first, second, third, pooled, log_mass, mean_score):
    queries = window_start.shape[1]
    unit = identity(queries)
    members = (first, second, third)
    for w in range(2):
        at = slice(w * queries, (w + 1) * queries)
        states = [columns_of(member, unit, w) for member in members]
        _, factors = weigh_states([state[0] for state in states])
        total = functools.reduce(jnp.add, [f * state[1] for f, state in zip(factors, states)])
        weighted = functools.reduce(
            jnp.add, [f * member[at, :].astype(F32) for f, member in zip(factors, members)]
        )
        pooled[at, :] = (weighted / total).astype(BF16)

        lines = [member[2 * queries :, at].astype(F32) for member in members]
        tops, totals, sums = (
            [line[3 * k : 3 * k + 1, :] + line[3 * k + 1 : 3 * k + 2, :] + line[3 * k + 2 : 3 * k + 3, :] for line in lines]
            for k in range(3)
        )
        best, factors = weigh_states([jnp.where(t > 0, top, NEG) for top, t in zip(tops, totals)])
        total = functools.reduce(jnp.add, [f * t for f, t in zip(factors, totals)])
        log_mass[w : w + 1, :] = best + jnp.log(total)
        count = (window_end[w : w + 1, :] - window_start[w : w + 1, :]).astype(F32)
        mean_score[w : w + 1, :] = functools.reduce(jnp.add, sums) / count


def finish(window_start, window_end, *members):
    queries = window_start.shape[1]
    width = members[0].shape[1]
    line = jax.ShapeDtypeStruct((2, queries), F32)
    return pl.pallas_call(
        finish_kernel,
        out_shape=(jax.ShapeDtypeStruct((2 * queries, width), BF16), line, line),
        in_specs=[VMEM] * 5,
        out_specs=(VMEM, VMEM, VMEM),
        name="finish",
    )(window_start, window_end, *members)


def local(queries, corpus, window_start, window_end):
    rows, width = queries.shape
    docs = corpus.shape[0]
    size = lax.axis_size(AXES)
    position = lax.axis_index(AXES)
    across = [(i, i ^ 1) for i in range(size)]
    between = [(i, i + 1) for i in range(3, size - 1, 4)] + [(i + 1, i) for i in range(3, size - 1, 4)]
    relay = [(i, i + 2) for i in range(0, size, 4)] + [(i + 3, i + 1) for i in range(0, size, 4)]
    relay_back = [(target, source) for source, target in relay]
    odd = position % 2

    starts, ends = window_start.T, window_end.T
    relative = jnp.concatenate([starts, ends], axis=0) - (position - 1) * docs
    message = pack(queries, relative)
    near = lax.ppermute(message, AXES, across)
    far_a = lax.ppermute(message, AXES, between)
    far_b = lax.ppermute(near, AXES, relay)
    shifts = jnp.stack([2 * docs * odd, 2 * docs * (1 - odd)]).astype(jnp.int32)
    near_part, far_part = neighbours(shifts, near, far_a, far_b, corpus)
    far_back = lax.ppermute(far_part, AXES, between)
    relayed = lax.ppermute(far_part, AXES, relay_back)
    near_back = lax.ppermute(merge(near_part, relayed), AXES, across)
    message, _ = lax.optimization_barrier((message, far_part))
    own_part = own(jnp.full((1,), docs, jnp.int32), message, corpus)
    pooled, log_mass, mean_score = finish(starts, ends, own_part, near_back, far_back)
    pooled = pooled.reshape(2, rows, width).transpose(1, 0, 2)
    return pooled, log_mass.T, mean_score.T


def solution(mesh):
    placed = P(AXES, None)
    return jax.shard_map(
        local,
        mesh=mesh,
        in_specs=(placed,) * 4,
        out_specs=(P(AXES, None, None), placed, placed),
        check_vma=False,
    )
```

time: 128 us -> 69.4 us (0.54); the launches traced: 125 us -> 68.7 us
  matrix products: 51.7 us -> 0 us
  starting transfers between devices: 47.7 us -> 11.5 us
  Pallas kernels: 0 us -> 32.5 us
  local copies, waits for them, and re-layouts: 1.95 us -> 15.1 us
  other arithmetic: 9.66 us -> 1.35 us
  waiting for transfers between devices: 13.1 us -> 7.5 us
    dot_general x9 -> x0, matrix products: 51.7 us -> none  [the longest x3 32.5 us: block_state(): lax.dot_general(query_rows, block, (((1,), (1,)), ((), ())), preferred_el...]
    ppermute x16 -> x6, starting transfers between devices: 47.7 us -> 11.5 us  [the longest x1 4.75 us: local(): near_back = lax.ppermute(merge(near_part, relayed), AXES, across)]
    pallas_call x0 -> x5, Pallas kernels: none -> 32.5 us  [the longest x1 14.1 us: neighbours(): pl.pallas_call(neighbour_kernel, out_shape=(result, result), in_specs=[SM...]
    unnamed x11 -> x16, local copies, waits for them, and re-layouts: 1.17 us -> 13 us
    reduce_sum x1 -> x0, other arithmetic: 8.58 us -> none  [block_state(): score_sums.append(jnp.sum(jnp.where(inside, scores, 0.0), axis=1))]
    ppermute x16 -> x6, waiting for transfers between devices: 13.1 us -> 7.5 us  [the longest x1 4.76 us: local(): near = lax.ppermute(message, AXES, across)]
    reshape x0 -> x1, local copies, waits for them, and re-layouts: none -> 2.15 us  [local(): pooled = pooled.reshape(2, rows, width).transpose(1, 0, 2)]
  transfers between devices with their start and end apart: 16 -> 6, of which waited for: 2 -> 3; matrix products, arithmetic and copies ran while one was open for 21% -> 0% of each run, Pallas kernels for 0% -> 20%
where the time goes in v1:
time: 69.4 us; the launch traced here: 68.7 us
  Pallas kernels  32.5 us (47%)
  local copies, waits for them, and re-layouts  15.1 us (22%)
  starting transfers between devices  11.5 us (17%)
  waiting for transfers between devices  7.5 us (11%)
  other arithmetic  1.35 us (2%)
  between operations  0.72 us (1%)
    pallas_call x1, Pallas kernels, neighbours(): pl.pallas_call(neighbour_kernel, out_shape=(result, result), in_specs=[SM...  14.1 us
    unnamed x16, local copies, waits for them, and re-layouts  13 us
    pallas_call x1, Pallas kernels, own(): pl.pallas_call(own_kernel, out_shape=jax.ShapeDtypeStruct((2 * queries +...  10.8 us
    ppermute x1, waiting for transfers between devices, local(): near = lax.ppermute(message, AXES, across)  4.76 us
    ppermute x1, starting transfers between devices, local(): near_back = lax.ppermute(merge(near_part, relayed), AXES, across)  4.75 us
    pallas_call x1, Pallas kernels, merge(): pl.pallas_call(merge_kernel, out_shape=jax.ShapeDtypeStruct(first.shape,...  2.99 us
    pallas_call x1, Pallas kernels, finish(): pl.pallas_call(finish_kernel, out_shape=(jax.ShapeDtypeStruct((2 * querie...  2.98 us
    reshape x1, local copies, waits for them, and re-layouts, local(): pooled = pooled.reshape(2, rows, width).transpose(1, 0, 2)  2.15 us
  transfers between devices with their start and end apart: 6, of which 3 were waited for; matrix products, arithmetic and copies ran while one was open for 0% of the time, Pallas kernels for 20%

profile of v1, /device:TPU:1, one launch (start us, length us, event | category | flops | bytes accessed | tf_op | source)
XLA Modules:
  0.0 68.7 jit_solution(7380493755920311161)
XLA Ops:
  0.6 1.3 %add_subtract_fusion.relative = s32[4,128]{1,0:T(4,128)} fusion(s32[2,128]{1,0:T(2,128)} %bitcast.14, s32[2,128]{1,0:T(2,128)} %bitcast.12, s32[]{:T(128)S(6)} %mul.13), kind=kLoop, calls=%fused_computation.1 | loop fusion | flops 1024 | bytes 4100 | tf_op jit(solution)/shard_map/sub | solution.py:428
  1.9 1.6 %pack.1.message = bf16[144,768]{1,0:T(8,128)(2,1)} custom-call(bf16[128,768]{1,0:T(8,128)(2,1)} %queries.1, s32[4,128]{1,0:T(4,128)} %add_subtract_fusion.relative), custom_call_target="tpu_custom_call" | custom-call | tf_op jit(solution)/shard_map/pack/pallas_call | solution.py:323
  3.5 0.0 copy-start.2
  3.6 2.0 %collective-permute-start = (bf16[144,768]{1,0:T(8,128)(2,1)}, bf16[144,768]{1,0:T(8,128)(2,1)S(1)}, u32[]{:S(2)}, u32[]{:S(2)}) collective-permute-start(bf16[144,768]{1,0:T(8,128)(2,1)} %pack.1.message), channel_id=1, source_target_pairs={{0,1},{1,0},{2,3},{3,2},{4,5},{5,4},{6,7},{7,6},{8,9},{9,8},{10,11... | collective-permute-start | bytes 663560 | tf_op jit(solution)/shard_map/ppermute | solution.py:430
  5.6 0.7 collective-permute-start.1
  6.3 4.8 %collective-permute-done.near = bf16[144,768]{1,0:T(8,128)(2,1)S(1)} collective-permute-done((bf16[144,768]{1,0:T(8,128)(2,1)}, bf16[144,768]{1,0:T(8,128)(2,1)S(1)}, u32[]{:S(2)}, u32[]{:S(2)}) %collective-permute-start) | collective-permute-done | bytes 221216 | tf_op jit(solution)/shard_map/ppermute | solution.py:430
  11.0 1.3 %collective-permute-start.2 = (bf16[144,768]{1,0:T(8,128)(2,1)S(1)}, bf16[144,768]{1,0:T(8,128)(2,1)S(1)}, u32[]{:S(2)}, u32[]{:S(2)}) collective-permute-start(bf16[144,768]{1,0:T(8,128)(2,1)S(1)} %collective-permute-done.near), channel_id=1, source_target_pairs={{0,2},{4,6},{8,10},{12,14},{16,18},{20,22},{24,26},{28,30},{3,1},{... | collective-permute-start | bytes 663560 | tf_op jit(solution)/shard_map/ppermute | solution.py:432
  12.3 0.1 pad_add_fusion.shifts
  12.4 0.0 collective-permute-done.1.far_a
  12.4 2.1 %collective-permute-done.2.far_b = bf16[144,768]{1,0:T(8,128)(2,1)S(1)} collective-permute-done((bf16[144,768]{1,0:T(8,128)(2,1)S(1)}, bf16[144,768]{1,0:T(8,128)(2,1)S(1)}, u32[]{:S(2)}, u32[]{:S(2)}) %collective-permute-start.2) | collective-permute-done | bytes 221216 | tf_op jit(solution)/shard_map/ppermute | solution.py:432
  14.5 0.0 copy-start.3
  14.5 4.6 %copy-done.3 = bf16[8192,768]{1,0:T(8,128)(2,1)S(1)} copy-done((bf16[8192,768]{1,0:T(8,128)(2,1)S(1)}, bf16[8192,768]{1,0:T(8,128)(2,1)}, u32[]{:S(2)}) %copy-start.3) | copy-done | bytes 12582936
  19.1 14.1 %neighbour_blocks.1 = (bf16[272,768]{1,0:T(8,128)(2,1)S(1)}, bf16[272,768]{1,0:T(8,128)(2,1)S(1)}) custom-call(s32[2]{0:T(128)S(1)} %pad_add_fusion.shifts, bf16[144,768]{1,0:T(8,128)(2,1)S(1)} %collective-permute-done.near, bf16[144,768]{1,0:T(8,128)(2,1)S(1)} %collective-permute-done.1.far_a, bf16[144,768]{1,0:T(8,128)(2,1)S(1)} %collective-permute-done.2.far_b, ...), custom_call_target="tpu_custom_call" | custom-call | flops 6442450944 | bytes 12582912 | tf_op jit(solution)/shard_map/neighbour_blocks/pallas_call | solution.py:295
  33.2 0.0 copy-start
  33.2 0.8 %copy-done = bf16[272,768]{1,0:T(8,128)(2,1)} copy-done((bf16[272,768]{1,0:T(8,128)(2,1)}, bf16[272,768]{1,0:T(8,128)(2,1)S(1)}, u32[]{:S(2)}) %copy-start) | copy-done | bytes 417816
  34.0 2.1 %collective-permute-start.3 = (bf16[272,768]{1,0:T(8,128)(2,1)S(1)}, bf16[272,768]{1,0:T(8,128)(2,1)S(1)}, u32[]{:S(2)}, u32[]{:S(2)}) collective-permute-start(bf16[272,768]{1,0:T(8,128)(2,1)S(1)} %get-tuple-element.9), channel_id=1, source_target_pairs={{2,0},{6,4},{10,8},{14,12},{18,16},{22,20},{26,24},{30,28},{1,3},{... | collective-permute-start | bytes 1253384 | tf_op jit(solution)/shard_map/ppermute | solution.py:436
  36.0 0.7 %collective-permute-start.5 = (bf16[272,768]{1,0:T(8,128)(2,1)S(1)}, bf16[272,768]{1,0:T(8,128)(2,1)S(1)}, u32[]{:S(2)}, u32[]{:S(2)}) collective-permute-start(bf16[272,768]{1,0:T(8,128)(2,1)S(1)} %get-tuple-element.9), channel_id=1, source_target_pairs={{3,4},{7,8},{11,12},{15,16},{19,20},{23,24},{27,28},{4,3},{8,7},{1... | collective-permute-start | bytes 1253384 | tf_op jit(solution)/shard_map/ppermute | solution.py:435
  36.7 0.6 collective-permute-done.3.second
  37.4 0.8 %copy-done.7 = bf16[272,768]{1,0:T(8,128)(2,1)} copy-done((bf16[272,768]{1,0:T(8,128)(2,1)}, bf16[272,768]{1,0:T(8,128)(2,1)S(1)}, u32[]{:S(2)}) %copy-start.7) | copy-done | bytes 417816
  38.1 3.0 %merge.1 = bf16[272,768]{1,0:T(8,128)(2,1)} custom-call(bf16[272,768]{1,0:T(8,128)(2,1)} %copy-done, bf16[272,768]{1,0:T(8,128)(2,1)} %copy-done.7), custom_call_target="tpu_custom_call" | custom-call | tf_op jit(solution)/shard_map/merge/pallas_call | solution.py:368
  41.1 4.7 %collective-permute-start.4 = (bf16[272,768]{1,0:T(8,128)(2,1)}, bf16[272,768]{1,0:T(8,128)(2,1)S(1)}, u32[]{:S(2)}, u32[]{:S(2)}) collective-permute-start(bf16[272,768]{1,0:T(8,128)(2,1)} %merge.1), channel_id=1, source_target_pairs={{0,1},{1,0},{2,3},{3,2},{4,5},{5,4},{6,7},{7,6},{8,9},{9,8},{10,11... | collective-permute-start | bytes 1253384 | tf_op jit(solution)/shard_map/ppermute | solution.py:437
  45.9 0.0 copy-done.2
  45.9 4.6 %copy-done.4 = bf16[8192,768]{1,0:T(8,128)(2,1)S(1)} copy-done((bf16[8192,768]{1,0:T(8,128)(2,1)S(1)}, bf16[8192,768]{1,0:T(8,128)(2,1)}, u32[]{:S(2)}) %copy-start.4) | copy-done | bytes 12582936
  50.5 10.8 %own_block.1.first = bf16[272,768]{1,0:T(8,128)(2,1)S(1)} custom-call(s32[1]{0:T(128)} %constant.21.clone.1.shift, bf16[144,768]{1,0:T(8,128)(2,1)S(1)} %copy-done.2, bf16[8192,768]{1,0:T(8,128)(2,1)S(1)} %copy-done.4), custom_call_target="tpu_custom_call" | custom-call | flops 6442450944 | bytes 12582912 | tf_op jit(solution)/shard_map/own_block/pallas_call | solution.py:209
  61.3 0.0 copy-start.1
  61.3 0.8 %copy-done.1 = bf16[272,768]{1,0:T(8,128)(2,1)} copy-done((bf16[272,768]{1,0:T(8,128)(2,1)}, bf16[272,768]{1,0:T(8,128)(2,1)S(1)}, u32[]{:S(2)}) %copy-start.1) | copy-done | bytes 417816
  62.0 0.0 collective-permute-done.5.third
  62.0 0.0 collective-permute-done.4.second
  62.1 0.8 %copy-done.5 = bf16[272,768]{1,0:T(8,128)(2,1)} copy-done((bf16[272,768]{1,0:T(8,128)(2,1)}, bf16[272,768]{1,0:T(8,128)(2,1)S(1)}, u32[]{:S(2)}) %copy-start.5) | copy-done | bytes 417816
  62.8 0.7 %copy-done.6 = bf16[272,768]{1,0:T(8,128)(2,1)} copy-done((bf16[272,768]{1,0:T(8,128)(2,1)}, bf16[272,768]{1,0:T(8,128)(2,1)S(1)}, u32[]{:S(2)}) %copy-start.6) | copy-done | bytes 417816
  63.6 3.0 %finish.1 = (bf16[256,768]{1,0:T(8,128)(2,1)}, f32[2,128]{1,0:T(2,128)}, f32[2,128]{1,0:T(2,128)}) custom-call(s32[2,128]{1,0:T(2,128)} %bitcast.13, s32[2,128]{1,0:T(2,128)} %bitcast.15, bf16[272,768]{1,0:T(8,128)(2,1)} %copy-done.1, bf16[272,768]{1,0:T(8,128)(2,1)} %copy-done.6, bf16[272,768]{1,0:T(8,128)(2,1)} %copy-done.5), custom_call_target="tpu_custom_call" | custom-call | tf_op jit(solution)/shard_map/finish/pallas_call | solution.py:407
  66.6 2.1 %copy.9 = bf16[2,128,768]{2,0,1:T(2,128)(2,1)} copy(bf16[2,128,768]{2,1,0:T(8,128)(2,1)} %bitcast.11) | data formatting | bytes 786432 | tf_op jit(solution)/shard_map/reshape | solution.py:441
  (4 shorter events, 0.0 us)
Async XLA Ops:
  3.5 42.3 %copy-start.2 = (bf16[144,768]{1,0:T(8,128)(2,1)S(1)}, bf16[144,768]{1,0:T(8,128)(2,1)}, u32[]{:S(2)}) copy-start(bf16[144,768]{1,0:T(8,128)(2,1)} %pack.1.message) | copy-start | bytes 663556
  3.6 7.5 %collective-permute-start = (bf16[144,768]{1,0:T(8,128)(2,1)}, bf16[144,768]{1,0:T(8,128)(2,1)S(1)}, u32[]{:S(2)}, u32[]{:S(2)}) collective-permute-start(bf16[144,768]{1,0:T(8,128)(2,1)} %pack.1.message), channel_id=1, source_target_pairs={{0,1},{1,0},{2,3},{3,2},{4,5},{5,4},{6,7},{7,6},{8,9},{9,8},{10,11... | collective-permute-start | bytes 663560 | tf_op jit(solution)/shard_map/ppermute | solution.py:430
  5.6 6.8 %collective-permute-start.1 = (bf16[144,768]{1,0:T(8,128)(2,1)}, bf16[144,768]{1,0:T(8,128)(2,1)S(1)}, u32[]{:S(2)}, u32[]{:S(2)}) collective-permute-start(bf16[144,768]{1,0:T(8,128)(2,1)} %pack.1.message), channel_id=1, source_target_pairs={{3,4},{7,8},{11,12},{15,16},{19,20},{23,24},{27,28},{4,3},{8,7},{1... | collective-permute-start | bytes 663560 | tf_op jit(solution)/shard_map/ppermute | solution.py:431
  11.0 3.5 %collective-permute-start.2 = (bf16[144,768]{1,0:T(8,128)(2,1)S(1)}, bf16[144,768]{1,0:T(8,128)(2,1)S(1)}, u32[]{:S(2)}, u32[]{:S(2)}) collective-permute-start(bf16[144,768]{1,0:T(8,128)(2,1)S(1)} %collective-permute-done.near), channel_id=1, source_target_pairs={{0,2},{4,6},{8,10},{12,14},{16,18},{20,22},{24,26},{28,30},{3,1},{... | collective-permute-start | bytes 663560 | tf_op jit(solution)/shard_map/ppermute | solution.py:432
  14.5 4.6 %copy-start.3 = (bf16[8192,768]{1,0:T(8,128)(2,1)S(1)}, bf16[8192,768]{1,0:T(8,128)(2,1)}, u32[]{:S(2)}) copy-start(bf16[8192,768]{1,0:T(8,128)(2,1)} %docs.3) | copy-start | bytes 37748740
  33.2 0.8 %copy-start = (bf16[272,768]{1,0:T(8,128)(2,1)}, bf16[272,768]{1,0:T(8,128)(2,1)S(1)}, u32[]{:S(2)}) copy-start(bf16[272,768]{1,0:T(8,128)(2,1)S(1)} %get-tuple-element.11.first) | copy-start | bytes 1253380
  34.0 3.4 %collective-permute-start.3 = (bf16[272,768]{1,0:T(8,128)(2,1)S(1)}, bf16[272,768]{1,0:T(8,128)(2,1)S(1)}, u32[]{:S(2)}, u32[]{:S(2)}) collective-permute-start(bf16[272,768]{1,0:T(8,128)(2,1)S(1)} %get-tuple-element.9), channel_id=1, source_target_pairs={{2,0},{6,4},{10,8},{14,12},{18,16},{22,20},{26,24},{30,28},{1,3},{... | collective-permute-start | bytes 1253384 | tf_op jit(solution)/shard_map/ppermute | solution.py:436
  36.0 26.0 %collective-permute-start.5 = (bf16[272,768]{1,0:T(8,128)(2,1)S(1)}, bf16[272,768]{1,0:T(8,128)(2,1)S(1)}, u32[]{:S(2)}, u32[]{:S(2)}) collective-permute-start(bf16[272,768]{1,0:T(8,128)(2,1)S(1)} %get-tuple-element.9), channel_id=1, source_target_pairs={{3,4},{7,8},{11,12},{15,16},{19,20},{23,24},{27,28},{4,3},{8,7},{1... | collective-permute-start | bytes 1253384 | tf_op jit(solution)/shard_map/ppermute | solution.py:435
  37.4 0.8 %copy-start.7 = (bf16[272,768]{1,0:T(8,128)(2,1)}, bf16[272,768]{1,0:T(8,128)(2,1)S(1)}, u32[]{:S(2)}) copy-start(bf16[272,768]{1,0:T(8,128)(2,1)S(1)} %collective-permute-done.3.second) | copy-start | bytes 1253380
  41.1 20.9 %collective-permute-start.4 = (bf16[272,768]{1,0:T(8,128)(2,1)}, bf16[272,768]{1,0:T(8,128)(2,1)S(1)}, u32[]{:S(2)}, u32[]{:S(2)}) collective-permute-start(bf16[272,768]{1,0:T(8,128)(2,1)} %merge.1), channel_id=1, source_target_pairs={{0,1},{1,0},{2,3},{3,2},{4,5},{5,4},{6,7},{7,6},{8,9},{9,8},{10,11... | collective-permute-start | bytes 1253384 | tf_op jit(solution)/shard_map/ppermute | solution.py:437
  45.9 4.6 %copy-start.4 = (bf16[8192,768]{1,0:T(8,128)(2,1)S(1)}, bf16[8192,768]{1,0:T(8,128)(2,1)}, u32[]{:S(2)}) copy-start(bf16[8192,768]{1,0:T(8,128)(2,1)} %docs.3) | copy-start | bytes 37748740
  61.3 0.8 %copy-start.1 = (bf16[272,768]{1,0:T(8,128)(2,1)}, bf16[272,768]{1,0:T(8,128)(2,1)S(1)}, u32[]{:S(2)}) copy-start(bf16[272,768]{1,0:T(8,128)(2,1)S(1)} %own_block.1.first) | copy-start | bytes 1253380
  62.0 0.8 %copy-start.5 = (bf16[272,768]{1,0:T(8,128)(2,1)}, bf16[272,768]{1,0:T(8,128)(2,1)S(1)}, u32[]{:S(2)}) copy-start(bf16[272,768]{1,0:T(8,128)(2,1)S(1)} %collective-permute-done.5.third) | copy-start | bytes 1253380
  62.8 0.7 %copy-start.6 = (bf16[272,768]{1,0:T(8,128)(2,1)}, bf16[272,768]{1,0:T(8,128)(2,1)S(1)}, u32[]{:S(2)}) copy-start(bf16[272,768]{1,0:T(8,128)(2,1)S(1)} %collective-permute-done.4.second) | copy-start | bytes 1253380

commit v2 on v1

--- a/solution.py
+++ b/solution.py
@@ -21,6 +21,7 @@
 DOC_TILE = 1024
 DOT_TILE = 256
 ROW_TILE = 16
+LOADS = 8
 
 VMEM = pl.BlockSpec(memory_space=pltpu.VMEM)
 SMEM = pl.BlockSpec(memory_space=pltpu.SMEM)
@@ -308,25 +309,51 @@
     )(shifts, near, far_a, far_b, corpus)
 
 
-def pack_kernel(queries, relative, out):
+def load_kernel(corpus, out, arrived):
+    step = corpus.shape[0] // LOADS
+    copies = [
+        pltpu.make_async_copy(corpus.at[pl.ds(k * step, step)], out.at[pl.ds(k * step, step)], arrived.at[k])
+        for k in range(LOADS)
+    ]
+    for copy in copies:
+        copy.start()
+    for copy in copies:
+        copy.wait()
+
+
+def load(corpus):
+    return pl.pallas_call(
+        load_kernel,
+        out_shape=jax.ShapeDtypeStruct(corpus.shape, corpus.dtype),
+        in_specs=[pl.BlockSpec(memory_space=pltpu.HBM)],
+        out_specs=VMEM,
+        scratch_shapes=[pltpu.SemaphoreType.DMA((LOADS,))],
+        compiler_params=params(44),
+        cost_estimate=pl.CostEstimate(flops=0, bytes_accessed=2 * corpus.size * 2, transcendentals=0),
+        name="load",
+    )(corpus)
+
+
+def pack_kernel(base, queries, starts, ends, out):
     rows, width = queries.shape
     out[0:rows, :] = queries[...]
     out[rows:, :] = jnp.zeros((META, width), BF16)
-    high, low = split_int(relative[...])
-    lines = [part[k : k + 1, :] for k in range(4) for part in (high, low)]
+    parts = [split_int(lines[...] - base[0]) for lines in (starts, ends)]
+    lines = [part[w : w + 1, :] for pair in parts for w in range(2) for part in pair]
     lines.append(jnp.zeros((META - 8, rows), F32))
     out[rows:, 0:rows] = jnp.concatenate(lines, axis=0).astype(BF16)
 
 
-def pack(queries, relative):
+def pack(base, queries, starts, ends):
     rows, width = queries.shape
     return pl.pallas_call(
         pack_kernel,
         out_shape=jax.ShapeDtypeStruct((rows + META, width), BF16),
-        in_specs=[VMEM, VMEM],
+        in_specs=[SMEM, VMEM, VMEM, VMEM],
         out_specs=VMEM,
+        compiler_params=params(4),
         name="pack",
-    )(queries, relative)
+    )(base, queries, starts, ends)
 
 
 def columns_of(state, unit, w):
@@ -370,6 +397,7 @@
         out_shape=jax.ShapeDtypeStruct(first.shape, BF16),
         in_specs=[VMEM, VMEM],
         out_specs=VMEM,
+        compiler_params=params(8),
         name="merge",
     )(first, second)
 
@@ -386,7 +414,7 @@
         weighted = functools.reduce(
             jnp.add, [f * member[at, :].astype(F32) for f, member in zip(factors, members)]
         )
-        pooled[at, :] = (weighted / total).astype(BF16)
+        pooled[:, w, :] = (weighted / total).astype(BF16)
 
         lines = [member[2 * queries :, at].astype(F32) for member in members]
         tops, totals, sums = (
@@ -406,15 +434,15 @@
     line = jax.ShapeDtypeStruct((2, queries), F32)
     return pl.pallas_call(
         finish_kernel,
-        out_shape=(jax.ShapeDtypeStruct((2 * queries, width), BF16), line, line),
+        out_shape=(jax.ShapeDtypeStruct((queries, 2, width), BF16), line, line),
         in_specs=[VMEM] * 5,
         out_specs=(VMEM, VMEM, VMEM),
+        compiler_params=params(8),
         name="finish",
     )(window_start, window_end, *members)
 
 
 def local(queries, corpus, window_start, window_end):
-    rows, width = queries.shape
     docs = corpus.shape[0]
     size = lax.axis_size(AXES)
     position = lax.axis_index(AXES)
@@ -425,10 +453,11 @@
     odd = position % 2
 
     starts, ends = window_start.T, window_end.T
-    relative = jnp.concatenate([starts, ends], axis=0) - (position - 1) * docs
-    message = pack(queries, relative)
+    base = jnp.full((1,), (position - 1) * docs, jnp.int32)
+    message = pack(base, queries, starts, ends)
     near = lax.ppermute(message, AXES, across)
     far_a = lax.ppermute(message, AXES, between)
+    near, corpus = lax.optimization_barrier((near, load(corpus)))
     far_b = lax.ppermute(near, AXES, relay)
     shifts = jnp.stack([2 * docs * odd, 2 * docs * (1 - odd)]).astype(jnp.int32)
     near_part, far_part = neighbours(shifts, near, far_a, far_b, corpus)
@@ -438,7 +467,6 @@
     message, _ = lax.optimization_barrier((message, far_part))
     own_part = own(jnp.full((1,), docs, jnp.int32), message, corpus)
     pooled, log_mass, mean_score = finish(starts, ends, own_part, near_back, far_back)
-    pooled = pooled.reshape(2, rows, width).transpose(1, 0, 2)
     return pooled, log_mass.T, mean_score.T
 
 

time: 69.4 us -> 61.2 us (0.88)
  local copies, waits for them, and re-layouts: 15.1 us -> 6.87 us
  Pallas kernels: 32.5 us -> 36.3 us
  waiting for transfers between devices: 7.5 us -> 5.49 us
  other arithmetic: 1.35 us -> 0.08 us
  starting transfers between devices: 11.5 us -> 10.6 us
    pallas_call x1 -> x2, Pallas kernels: 2.98 us -> 11.1 us  [the longest x1 9.23 us: load(): pl.pallas_call(load_kernel, out_shape=jax.ShapeDtypeStruct(corpus.shape,...]
    unnamed x16 -> x14, local copies, waits for them, and re-layouts: 13 us -> 6.87 us
    ppermute x1, waiting for transfers between devices: 4.76 us -> 0.01 us  [local(): near = lax.ppermute(message, AXES, across)]
    ppermute x1, waiting for transfers between devices: 0.01 us -> 2.85 us  [local(): near_back = lax.ppermute(merge(near_part, relayed), AXES, across)]
    reshape x1 -> x0, local copies, waits for them, and re-layouts: 2.15 us -> none  [local(): pooled = pooled.reshape(2, rows, width).transpose(1, 0, 2)]
    pallas_call x1, Pallas kernels: 2.99 us -> 1.12 us  [merge(): pl.pallas_call(merge_kernel, out_shape=jax.ShapeDtypeStruct(first.shape,...]
    pallas_call x1, Pallas kernels: 1.63 us -> 0.02 us  [pack(): pl.pallas_call(pack_kernel, out_shape=jax.ShapeDtypeStruct((rows + META,...]
    sub x1 -> x0, other arithmetic: 1.28 us -> none  [local(): relative = jnp.concatenate([starts, ends], axis=0) - (position - 1) * docs]
  transfers between devices with their start and end apart: 6 -> 6, of which waited for: 3 -> 3; matrix products, arithmetic and copies ran while one was open for 0% -> 0% of each run, Pallas kernels for 20% -> 35%
where the time goes in v2:
time: 61.2 us; the launch traced here: 60 us
  Pallas kernels  36.3 us (59%)
  starting transfers between devices  10.6 us (17%)
  local copies, waits for them, and re-layouts  6.87 us (11%)
  waiting for transfers between devices  5.49 us (9%)
  between operations  0.75 us (1%)
    pallas_call x1, Pallas kernels, neighbours(): pl.pallas_call(neighbour_kernel, out_shape=(result, result), in_specs=[SM...  13.6 us
    pallas_call x1, Pallas kernels, own(): pl.pallas_call(own_kernel, out_shape=jax.ShapeDtypeStruct((2 * queries +...  10.5 us
    pallas_call x1, Pallas kernels, load(): pl.pallas_call(load_kernel, out_shape=jax.ShapeDtypeStruct(corpus.shape,...  9.23 us
    unnamed x14, local copies, waits for them, and re-layouts  6.87 us
    ppermute x1, starting transfers between devices, local(): near_back = lax.ppermute(merge(near_part, relayed), AXES, across)  3.74 us
    ppermute x1, waiting for transfers between devices, local(): near_back = lax.ppermute(merge(near_part, relayed), AXES, across)  2.85 us
    ppermute x1, starting transfers between devices, local(): near = lax.ppermute(message, AXES, across)  2.11 us
    ppermute x1, starting transfers between devices, local(): relayed = lax.ppermute(far_part, AXES, relay_back)  2.06 us
  transfers between devices with their start and end apart: 6, of which 3 were waited for; matrix products, arithmetic and copies ran while one was open for 0% of the time, Pallas kernels for 35%

profile of v2, /device:TPU:1, one launch (start us, length us, event | category | flops | bytes accessed | tf_op | source)
XLA Modules:
  0.0 60.0 jit_solution(14975903442795747603)
XLA Ops:
  0.6 0.0 copy-start.2
  0.6 0.9 %copy-done.2 = bf16[128,768]{1,0:T(8,128)(2,1)S(1)} copy-done((bf16[128,768]{1,0:T(8,128)(2,1)S(1)}, bf16[128,768]{1,0:T(8,128)(2,1)}, u32[]{:S(2)}) %copy-start.2) | copy-done | bytes 196632
  1.6 0.0 copy-start.3
  1.6 0.7 %copy-done.3 = s32[128,2]{0,1:T(2,128)S(1)} copy-done((s32[128,2]{0,1:T(2,128)S(1)}, s32[128,2]{0,1:T(2,128)}, u32[]{:S(2)}) %copy-start.3) | copy-done | bytes 1048
  2.2 0.0 copy-start.5
  2.2 0.7 %copy-done.5 = s32[128,2]{0,1:T(2,128)S(1)} copy-done((s32[128,2]{0,1:T(2,128)S(1)}, s32[128,2]{0,1:T(2,128)}, u32[]{:S(2)}) %copy-start.5) | copy-done | bytes 1048
  3.0 2.1 %collective-permute-start = (bf16[144,768]{1,0:T(8,128)(2,1)S(1)}, bf16[144,768]{1,0:T(8,128)(2,1)S(1)}, u32[]{:S(2)}, u32[]{:S(2)}) collective-permute-start(bf16[144,768]{1,0:T(8,128)(2,1)S(1)} %pack.1.message), channel_id=1, source_target_pairs={{0,1},{1,0},{2,3},{3,2},{4,5},{5,4},{6,7},{7,6},{8,9},{9,8},{10,11... | collective-permute-start | bytes 663560 | tf_op jit(solution)/shard_map/ppermute | solution.py:458
  5.1 0.7 %collective-permute-start.1 = (bf16[144,768]{1,0:T(8,128)(2,1)S(1)}, bf16[144,768]{1,0:T(8,128)(2,1)S(1)}, u32[]{:S(2)}, u32[]{:S(2)}) collective-permute-start(bf16[144,768]{1,0:T(8,128)(2,1)S(1)} %pack.1.message), channel_id=1, source_target_pairs={{3,4},{7,8},{11,12},{15,16},{19,20},{23,24},{27,28},{4,3},{8,7},{1... | collective-permute-start | bytes 663560 | tf_op jit(solution)/shard_map/ppermute | solution.py:459
  5.7 9.2 %load.1.docs = bf16[8192,768]{1,0:T(8,128)(2,1)} custom-call(bf16[8192,768]{1,0:T(8,128)(2,1)} %corpus.1), custom_call_target="tpu_custom_call" | custom-call | bytes 25165824 | tf_op jit(solution)/shard_map/load/pallas_call | solution.py:325
  15.0 0.0 collective-permute-done.near
  15.0 1.3 %collective-permute-start.2 = (bf16[144,768]{1,0:T(8,128)(2,1)S(1)}, bf16[144,768]{1,0:T(8,128)(2,1)S(1)}, u32[]{:S(2)}, u32[]{:S(2)}) collective-permute-start(bf16[144,768]{1,0:T(8,128)(2,1)S(1)} %collective-permute-done.near), channel_id=1, source_target_pairs={{0,2},{4,6},{8,10},{12,14},{16,18},{20,22},{24,26},{28,30},{3,1},{... | collective-permute-start | bytes 663560 | tf_op jit(solution)/shard_map/ppermute | solution.py:461
  16.3 0.1 pad_add_fusion.shifts
  16.4 0.0 collective-permute-done.1.far_a
  16.4 2.0 %collective-permute-done.2.far_b = bf16[144,768]{1,0:T(8,128)(2,1)S(1)} collective-permute-done((bf16[144,768]{1,0:T(8,128)(2,1)S(1)}, bf16[144,768]{1,0:T(8,128)(2,1)S(1)}, u32[]{:S(2)}, u32[]{:S(2)}) %collective-permute-start.2) | collective-permute-done | bytes 221216 | tf_op jit(solution)/shard_map/ppermute | solution.py:461
  18.4 0.0 copy-start
  18.4 4.6 %copy-done = bf16[8192,768]{1,0:T(8,128)(2,1)S(1)} copy-done((bf16[8192,768]{1,0:T(8,128)(2,1)S(1)}, bf16[8192,768]{1,0:T(8,128)(2,1)}, u32[]{:S(2)}) %copy-start) | copy-done | bytes 12582936
  22.9 0.0 copy-start.1
  22.9 13.6 %neighbour_blocks.1 = (bf16[272,768]{1,0:T(8,128)(2,1)S(1)}, bf16[272,768]{1,0:T(8,128)(2,1)S(1)}) custom-call(s32[2]{0:T(128)S(1)} %pad_add_fusion.shifts, bf16[144,768]{1,0:T(8,128)(2,1)S(1)} %collective-permute-done.near, bf16[144,768]{1,0:T(8,128)(2,1)S(1)} %collective-permute-done.1.far_a, bf16[144,768]{1,0:T(8,128)(2,1)S(1)} %collective-permute-done.2.far_b, ...), custom_call_target="tpu_custom_call" | custom-call | flops 6442450944 | bytes 12582912 | tf_op jit(solution)/shard_map/neighbour_blocks/pallas_call | solution.py:296
  36.5 0.0 copy-start.4
  36.5 0.0 copy-start.6
  36.6 2.1 %collective-permute-start.3 = (bf16[272,768]{1,0:T(8,128)(2,1)S(1)}, bf16[272,768]{1,0:T(8,128)(2,1)S(1)}, u32[]{:S(2)}, u32[]{:S(2)}) collective-permute-start(bf16[272,768]{1,0:T(8,128)(2,1)S(1)} %get-tuple-element.13), channel_id=1, source_target_pairs={{2,0},{6,4},{10,8},{14,12},{18,16},{22,20},{26,24},{30,28},{1,3},{... | collective-permute-start | bytes 1253384 | tf_op jit(solution)/shard_map/ppermute | solution.py:465
  38.6 0.7 %collective-permute-start.5 = (bf16[272,768]{1,0:T(8,128)(2,1)S(1)}, bf16[272,768]{1,0:T(8,128)(2,1)S(1)}, u32[]{:S(2)}, u32[]{:S(2)}) collective-permute-start(bf16[272,768]{1,0:T(8,128)(2,1)S(1)} %get-tuple-element.13), channel_id=1, source_target_pairs={{3,4},{7,8},{11,12},{15,16},{19,20},{23,24},{27,28},{4,3},{8,7},{1... | collective-permute-start | bytes 1253384 | tf_op jit(solution)/shard_map/ppermute | solution.py:464
  39.3 0.6 %collective-permute-done.3.second = bf16[272,768]{1,0:T(8,128)(2,1)S(1)} collective-permute-done((bf16[272,768]{1,0:T(8,128)(2,1)S(1)}, bf16[272,768]{1,0:T(8,128)(2,1)S(1)}, u32[]{:S(2)}, u32[]{:S(2)}) %collective-permute-start.3) | collective-permute-done | bytes 417824 | tf_op jit(solution)/shard_map/ppermute | solution.py:465
  40.0 1.1 %merge.1 = bf16[272,768]{1,0:T(8,128)(2,1)S(1)} custom-call(bf16[272,768]{1,0:T(8,128)(2,1)S(1)} %get-tuple-element.15.first, bf16[272,768]{1,0:T(8,128)(2,1)S(1)} %collective-permute-done.3.second), custom_call_target="tpu_custom_call" | custom-call | tf_op jit(solution)/shard_map/merge/pallas_call | solution.py:395
  41.1 3.7 %collective-permute-start.4 = (bf16[272,768]{1,0:T(8,128)(2,1)S(1)}, bf16[272,768]{1,0:T(8,128)(2,1)S(1)}, u32[]{:S(2)}, u32[]{:S(2)}) collective-permute-start(bf16[272,768]{1,0:T(8,128)(2,1)S(1)} %merge.1), channel_id=1, source_target_pairs={{0,1},{1,0},{2,3},{3,2},{4,5},{5,4},{6,7},{7,6},{8,9},{9,8},{10,11... | collective-permute-start | bytes 1253384 | tf_op jit(solution)/shard_map/ppermute | solution.py:466
  44.8 0.0 copy-done.1
  44.8 10.5 %own_block.1.first = bf16[272,768]{1,0:T(8,128)(2,1)S(1)} custom-call(s32[1]{0:T(128)} %constant.21.clone.1.shift, bf16[144,768]{1,0:T(8,128)(2,1)S(1)} %pack.1.message, bf16[8192,768]{1,0:T(8,128)(2,1)S(1)} %copy-done.1), custom_call_target="tpu_custom_call" | custom-call | flops 6442450944 | bytes 12582912 | tf_op jit(solution)/shard_map/own_block/pallas_call | solution.py:210
  55.4 0.0 collective-permute-done.5.third
  55.4 2.9 %collective-permute-done.4.second = bf16[272,768]{1,0:T(8,128)(2,1)S(1)} collective-permute-done((bf16[272,768]{1,0:T(8,128)(2,1)S(1)}, bf16[272,768]{1,0:T(8,128)(2,1)S(1)}, u32[]{:S(2)}, u32[]{:S(2)}) %collective-permute-start.4) | collective-permute-done | bytes 417824 | tf_op jit(solution)/shard_map/ppermute | solution.py:466
  58.2 0.0 copy-done.4
  58.2 0.0 copy-done.6
  58.2 1.8 %finish.1 = (bf16[128,2,768]{2,1,0:T(2,128)(2,1)}, f32[2,128]{1,0:T(2,128)}, f32[2,128]{1,0:T(2,128)}) custom-call(s32[2,128]{1,0:T(2,128)S(1)} %bitcast.8, s32[2,128]{1,0:T(2,128)S(1)} %bitcast.10, bf16[272,768]{1,0:T(8,128)(2,1)S(1)} %own_block.1.first, bf16[272,768]{1,0:T(8,128)(2,1)S(1)} %collective-permute-done.4.second, ...), custom_call_target="tpu_custom_call" | custom-call | tf_op jit(solution)/shard_map/finish/pallas_call | solution.py:435
  (1 shorter events, 0.0 us)
Async XLA Ops:
  0.6 0.9 %copy-start.2 = (bf16[128,768]{1,0:T(8,128)(2,1)S(1)}, bf16[128,768]{1,0:T(8,128)(2,1)}, u32[]{:S(2)}) copy-start(bf16[128,768]{1,0:T(8,128)(2,1)} %queries.1) | copy-start | bytes 589828
  1.6 0.7 %copy-start.3 = (s32[128,2]{0,1:T(2,128)S(1)}, s32[128,2]{0,1:T(2,128)}, u32[]{:S(2)}) copy-start(s32[128,2]{0,1:T(2,128)} %param.6) | copy-start | bytes 3076
  2.2 0.7 %copy-start.5 = (s32[128,2]{0,1:T(2,128)S(1)}, s32[128,2]{0,1:T(2,128)}, u32[]{:S(2)}) copy-start(s32[128,2]{0,1:T(2,128)} %param.7) | copy-start | bytes 3076
  3.0 12.0 %collective-permute-start = (bf16[144,768]{1,0:T(8,128)(2,1)S(1)}, bf16[144,768]{1,0:T(8,128)(2,1)S(1)}, u32[]{:S(2)}, u32[]{:S(2)}) collective-permute-start(bf16[144,768]{1,0:T(8,128)(2,1)S(1)} %pack.1.message), channel_id=1, source_target_pairs={{0,1},{1,0},{2,3},{3,2},{4,5},{5,4},{6,7},{7,6},{8,9},{9,8},{10,11... | collective-permute-start | bytes 663560 | tf_op jit(solution)/shard_map/ppermute | solution.py:458
  5.1 11.3 %collective-permute-start.1 = (bf16[144,768]{1,0:T(8,128)(2,1)S(1)}, bf16[144,768]{1,0:T(8,128)(2,1)S(1)}, u32[]{:S(2)}, u32[]{:S(2)}) collective-permute-start(bf16[144,768]{1,0:T(8,128)(2,1)S(1)} %pack.1.message), channel_id=1, source_target_pairs={{3,4},{7,8},{11,12},{15,16},{19,20},{23,24},{27,28},{4,3},{8,7},{1... | collective-permute-start | bytes 663560 | tf_op jit(solution)/shard_map/ppermute | solution.py:459
  15.0 3.4 %collective-permute-start.2 = (bf16[144,768]{1,0:T(8,128)(2,1)S(1)}, bf16[144,768]{1,0:T(8,128)(2,1)S(1)}, u32[]{:S(2)}, u32[]{:S(2)}) collective-permute-start(bf16[144,768]{1,0:T(8,128)(2,1)S(1)} %collective-permute-done.near), channel_id=1, source_target_pairs={{0,2},{4,6},{8,10},{12,14},{16,18},{20,22},{24,26},{28,30},{3,1},{... | collective-permute-start | bytes 663560 | tf_op jit(solution)/shard_map/ppermute | solution.py:461
  18.4 4.6 %copy-start = (bf16[8192,768]{1,0:T(8,128)(2,1)S(1)}, bf16[8192,768]{1,0:T(8,128)(2,1)}, u32[]{:S(2)}) copy-start(bf16[8192,768]{1,0:T(8,128)(2,1)} %load.1.docs) | copy-start | bytes 37748740
  22.9 21.9 %copy-start.1 = (bf16[8192,768]{1,0:T(8,128)(2,1)S(1)}, bf16[8192,768]{1,0:T(8,128)(2,1)}, u32[]{:S(2)}) copy-start(bf16[8192,768]{1,0:T(8,128)(2,1)} %load.1.docs) | copy-start | bytes 37748740
  36.5 21.7 %copy-start.4 = (s32[128,2]{0,1:T(2,128)S(1)}, s32[128,2]{0,1:T(2,128)}, u32[]{:S(2)}) copy-start(s32[128,2]{0,1:T(2,128)} %param.6) | copy-start | bytes 3076
  36.5 21.7 %copy-start.6 = (s32[128,2]{0,1:T(2,128)S(1)}, s32[128,2]{0,1:T(2,128)}, u32[]{:S(2)}) copy-start(s32[128,2]{0,1:T(2,128)} %param.7) | copy-start | bytes 3076
  36.6 3.4 %collective-permute-start.3 = (bf16[272,768]{1,0:T(8,128)(2,1)S(1)}, bf16[272,768]{1,0:T(8,128)(2,1)S(1)}, u32[]{:S(2)}, u32[]{:S(2)}) collective-permute-start(bf16[272,768]{1,0:T(8,128)(2,1)S(1)} %get-tuple-element.13), channel_id=1, source_target_pairs={{2,0},{6,4},{10,8},{14,12},{18,16},{22,20},{26,24},{30,28},{1,3},{... | collective-permute-start | bytes 1253384 | tf_op jit(solution)/shard_map/ppermute | solution.py:465
  38.6 16.7 %collective-permute-start.5 = (bf16[272,768]{1,0:T(8,128)(2,1)S(1)}, bf16[272,768]{1,0:T(8,128)(2,1)S(1)}, u32[]{:S(2)}, u32[]{:S(2)}) collective-permute-start(bf16[272,768]{1,0:T(8,128)(2,1)S(1)} %get-tuple-element.13), channel_id=1, source_target_pairs={{3,4},{7,8},{11,12},{15,16},{19,20},{23,24},{27,28},{4,3},{8,7},{1... | collective-permute-start | bytes 1253384 | tf_op jit(solution)/shard_map/ppermute | solution.py:464
  41.1 17.1 %collective-permute-start.4 = (bf16[272,768]{1,0:T(8,128)(2,1)S(1)}, bf16[272,768]{1,0:T(8,128)(2,1)S(1)}, u32[]{:S(2)}, u32[]{:S(2)}) collective-permute-start(bf16[272,768]{1,0:T(8,128)(2,1)S(1)} %merge.1), channel_id=1, source_target_pairs={{0,1},{1,0},{2,3},{3,2},{4,5},{5,4},{6,7},{7,6},{8,9},{9,8},{10,11... | collective-permute-start | bytes 1253384 | tf_op jit(solution)/shard_map/ppermute | solution.py:466

commit v3 on v2

--- a/solution.py
+++ b/solution.py
@@ -328,7 +328,7 @@
         in_specs=[pl.BlockSpec(memory_space=pltpu.HBM)],
         out_specs=VMEM,
         scratch_shapes=[pltpu.SemaphoreType.DMA((LOADS,))],
-        compiler_params=params(44),
+        compiler_params=params(36),
         cost_estimate=pl.CostEstimate(flops=0, bytes_accessed=2 * corpus.size * 2, transcendentals=0),
         name="load",
     )(corpus)

time: 61.2 us -> 61.2 us (level)
  local copies, waits for them, and re-layouts: 6.87 us -> 11.4 us
  Pallas kernels: 36.3 us -> 31.8 us
    pallas_call x1, Pallas kernels: 9.23 us -> 4.7 us  [load(): pl.pallas_call(load_kernel, out_shape=jax.ShapeDtypeStruct(corpus.shape,...]
    unnamed x14 -> x16, local copies, waits for them, and re-layouts: 6.87 us -> 11.4 us
  transfers between devices with their start and end apart: 6 -> 6, of which waited for: 3 -> 3; matrix products, arithmetic and copies ran while one was open for 0% -> 0% of each run, Pallas kernels for 35% -> 27%
where the time goes in v3:
time: 61.2 us; the launch traced here: 60 us
  Pallas kernels  31.8 us (52%)
  local copies, waits for them, and re-layouts  11.4 us (19%)
  starting transfers between devices  10.6 us (17%)
  waiting for transfers between devices  5.49 us (9%)
  between operations  0.75 us (1%)
    pallas_call x1, Pallas kernels, neighbours(): pl.pallas_call(neighbour_kernel, out_shape=(result, result), in_specs=[SM...  13.6 us
    unnamed x16, local copies, waits for them, and re-layouts  11.4 us
    pallas_call x1, Pallas kernels, own(): pl.pallas_call(own_kernel, out_shape=jax.ShapeDtypeStruct((2 * queries +...  10.5 us
    pallas_call x1, Pallas kernels, load(): pl.pallas_call(load_kernel, out_shape=jax.ShapeDtypeStruct(corpus.shape,...  4.7 us
    ppermute x1, starting transfers between devices, local(): near_back = lax.ppermute(merge(near_part, relayed), AXES, across)  3.75 us
    ppermute x1, waiting for transfers between devices, local(): near_back = lax.ppermute(merge(near_part, relayed), AXES, across)  2.85 us
    ppermute x1, starting transfers between devices, local(): near = lax.ppermute(message, AXES, across)  2.11 us
    ppermute x1, starting transfers between devices, local(): relayed = lax.ppermute(far_part, AXES, relay_back)  2.06 us
  transfers between devices with their start and end apart: 6, of which 3 were waited for; matrix products, arithmetic and copies ran while one was open for 0% of the time, Pallas kernels for 27%

profile of v3, /device:TPU:1, one launch (start us, length us, event | category | flops | bytes accessed | tf_op | source)
XLA Modules:
  0.0 60.0 jit_solution(12384696519300179054)
XLA Ops:
  0.6 0.0 copy-start.3
  0.6 0.9 %copy-done.3 = bf16[128,768]{1,0:T(8,128)(2,1)S(1)} copy-done((bf16[128,768]{1,0:T(8,128)(2,1)S(1)}, bf16[128,768]{1,0:T(8,128)(2,1)}, u32[]{:S(2)}) %copy-start.3) | copy-done | bytes 196632
  1.6 0.0 copy-start.4
  1.6 0.7 %copy-done.4 = s32[128,2]{0,1:T(2,128)S(1)} copy-done((s32[128,2]{0,1:T(2,128)S(1)}, s32[128,2]{0,1:T(2,128)}, u32[]{:S(2)}) %copy-start.4) | copy-done | bytes 1048
  2.2 0.0 copy-start.6
  2.2 0.7 %copy-done.6 = s32[128,2]{0,1:T(2,128)S(1)} copy-done((s32[128,2]{0,1:T(2,128)S(1)}, s32[128,2]{0,1:T(2,128)}, u32[]{:S(2)}) %copy-start.6) | copy-done | bytes 1048
  3.0 2.1 %collective-permute-start = (bf16[144,768]{1,0:T(8,128)(2,1)S(1)}, bf16[144,768]{1,0:T(8,128)(2,1)S(1)}, u32[]{:S(2)}, u32[]{:S(2)}) collective-permute-start(bf16[144,768]{1,0:T(8,128)(2,1)S(1)} %pack.1.message), channel_id=1, source_target_pairs={{0,1},{1,0},{2,3},{3,2},{4,5},{5,4},{6,7},{7,6},{8,9},{9,8},{10,11... | collective-permute-start | bytes 663560 | tf_op jit(solution)/shard_map/ppermute | solution.py:458
  5.1 0.7 %collective-permute-start.1 = (bf16[144,768]{1,0:T(8,128)(2,1)S(1)}, bf16[144,768]{1,0:T(8,128)(2,1)S(1)}, u32[]{:S(2)}, u32[]{:S(2)}) collective-permute-start(bf16[144,768]{1,0:T(8,128)(2,1)S(1)} %pack.1.message), channel_id=1, source_target_pairs={{3,4},{7,8},{11,12},{15,16},{19,20},{23,24},{27,28},{4,3},{8,7},{1... | collective-permute-start | bytes 663560 | tf_op jit(solution)/shard_map/ppermute | solution.py:459
  5.7 4.7 %load.1.docs = bf16[8192,768]{1,0:T(8,128)(2,1)S(1)} custom-call(bf16[8192,768]{1,0:T(8,128)(2,1)} %corpus.1), custom_call_target="tpu_custom_call" | custom-call | bytes 25165824 | tf_op jit(solution)/shard_map/load/pallas_call | solution.py:325
  10.4 0.0 copy-start
  10.4 4.5 %copy-done = bf16[8192,768]{1,0:T(8,128)(2,1)} copy-done((bf16[8192,768]{1,0:T(8,128)(2,1)}, bf16[8192,768]{1,0:T(8,128)(2,1)S(1)}, u32[]{:S(2)}) %copy-start) | copy-done | bytes 12582936
  15.0 0.0 collective-permute-done.near
  15.0 1.3 %collective-permute-start.2 = (bf16[144,768]{1,0:T(8,128)(2,1)S(1)}, bf16[144,768]{1,0:T(8,128)(2,1)S(1)}, u32[]{:S(2)}, u32[]{:S(2)}) collective-permute-start(bf16[144,768]{1,0:T(8,128)(2,1)S(1)} %collective-permute-done.near), channel_id=1, source_target_pairs={{0,2},{4,6},{8,10},{12,14},{16,18},{20,22},{24,26},{28,30},{3,1},{... | collective-permute-start | bytes 663560 | tf_op jit(solution)/shard_map/ppermute | solution.py:461
  16.3 0.1 pad_add_fusion.shifts
  16.3 0.0 collective-permute-done.1.far_a
  16.4 2.0 %collective-permute-done.2.far_b = bf16[144,768]{1,0:T(8,128)(2,1)S(1)} collective-permute-done((bf16[144,768]{1,0:T(8,128)(2,1)S(1)}, bf16[144,768]{1,0:T(8,128)(2,1)S(1)}, u32[]{:S(2)}, u32[]{:S(2)}) %collective-permute-start.2) | collective-permute-done | bytes 221216 | tf_op jit(solution)/shard_map/ppermute | solution.py:461
  18.3 4.6 %copy-done.1 = bf16[8192,768]{1,0:T(8,128)(2,1)S(1)} copy-done((bf16[8192,768]{1,0:T(8,128)(2,1)S(1)}, bf16[8192,768]{1,0:T(8,128)(2,1)}, u32[]{:S(2)}) %copy-start.1) | copy-done | bytes 12582936
  22.9 13.6 %neighbour_blocks.1 = (bf16[272,768]{1,0:T(8,128)(2,1)S(1)}, bf16[272,768]{1,0:T(8,128)(2,1)S(1)}) custom-call(s32[2]{0:T(128)S(1)} %pad_add_fusion.shifts, bf16[144,768]{1,0:T(8,128)(2,1)S(1)} %collective-permute-done.near, bf16[144,768]{1,0:T(8,128)(2,1)S(1)} %collective-permute-done.1.far_a, bf16[144,768]{1,0:T(8,128)(2,1)S(1)} %collective-permute-done.2.far_b, ...), custom_call_target="tpu_custom_call" | custom-call | flops 6442450944 | bytes 12582912 | tf_op jit(solution)/shard_map/neighbour_blocks/pallas_call | solution.py:296
  36.5 0.0 copy-start.5
  36.5 0.0 copy-start.7
  36.5 2.1 %collective-permute-start.3 = (bf16[272,768]{1,0:T(8,128)(2,1)S(1)}, bf16[272,768]{1,0:T(8,128)(2,1)S(1)}, u32[]{:S(2)}, u32[]{:S(2)}) collective-permute-start(bf16[272,768]{1,0:T(8,128)(2,1)S(1)} %get-tuple-element.13), channel_id=1, source_target_pairs={{2,0},{6,4},{10,8},{14,12},{18,16},{22,20},{26,24},{30,28},{1,3},{... | collective-permute-start | bytes 1253384 | tf_op jit(solution)/shard_map/ppermute | solution.py:465
  38.6 0.7 %collective-permute-start.5 = (bf16[272,768]{1,0:T(8,128)(2,1)S(1)}, bf16[272,768]{1,0:T(8,128)(2,1)S(1)}, u32[]{:S(2)}, u32[]{:S(2)}) collective-permute-start(bf16[272,768]{1,0:T(8,128)(2,1)S(1)} %get-tuple-element.13), channel_id=1, source_target_pairs={{3,4},{7,8},{11,12},{15,16},{19,20},{23,24},{27,28},{4,3},{8,7},{1... | collective-permute-start | bytes 1253384 | tf_op jit(solution)/shard_map/ppermute | solution.py:464
  39.3 0.6 %collective-permute-done.3.second = bf16[272,768]{1,0:T(8,128)(2,1)S(1)} collective-permute-done((bf16[272,768]{1,0:T(8,128)(2,1)S(1)}, bf16[272,768]{1,0:T(8,128)(2,1)S(1)}, u32[]{:S(2)}, u32[]{:S(2)}) %collective-permute-start.3) | collective-permute-done | bytes 417824 | tf_op jit(solution)/shard_map/ppermute | solution.py:465
  40.0 1.1 %merge.1 = bf16[272,768]{1,0:T(8,128)(2,1)S(1)} custom-call(bf16[272,768]{1,0:T(8,128)(2,1)S(1)} %get-tuple-element.15.first, bf16[272,768]{1,0:T(8,128)(2,1)S(1)} %collective-permute-done.3.second), custom_call_target="tpu_custom_call" | custom-call | tf_op jit(solution)/shard_map/merge/pallas_call | solution.py:395
  41.1 3.8 %collective-permute-start.4 = (bf16[272,768]{1,0:T(8,128)(2,1)S(1)}, bf16[272,768]{1,0:T(8,128)(2,1)S(1)}, u32[]{:S(2)}, u32[]{:S(2)}) collective-permute-start(bf16[272,768]{1,0:T(8,128)(2,1)S(1)} %merge.1), channel_id=1, source_target_pairs={{0,1},{1,0},{2,3},{3,2},{4,5},{5,4},{6,7},{7,6},{8,9},{9,8},{10,11... | collective-permute-start | bytes 1253384 | tf_op jit(solution)/shard_map/ppermute | solution.py:466
  44.8 0.0 copy-done.2
  44.8 10.5 %own_block.1.first = bf16[272,768]{1,0:T(8,128)(2,1)S(1)} custom-call(s32[1]{0:T(128)} %constant.21.clone.1.shift, bf16[144,768]{1,0:T(8,128)(2,1)S(1)} %pack.1.message, bf16[8192,768]{1,0:T(8,128)(2,1)S(1)} %copy-done.2), custom_call_target="tpu_custom_call" | custom-call | flops 6442450944 | bytes 12582912 | tf_op jit(solution)/shard_map/own_block/pallas_call | solution.py:210
  55.4 0.0 collective-permute-done.5.third
  55.4 2.9 %collective-permute-done.4.second = bf16[272,768]{1,0:T(8,128)(2,1)S(1)} collective-permute-done((bf16[272,768]{1,0:T(8,128)(2,1)S(1)}, bf16[272,768]{1,0:T(8,128)(2,1)S(1)}, u32[]{:S(2)}, u32[]{:S(2)}) %collective-permute-start.4) | collective-permute-done | bytes 417824 | tf_op jit(solution)/shard_map/ppermute | solution.py:466
  58.2 0.0 copy-done.5
  58.2 0.0 copy-done.7
  58.2 1.8 %finish.1 = (bf16[128,2,768]{2,1,0:T(2,128)(2,1)}, f32[2,128]{1,0:T(2,128)}, f32[2,128]{1,0:T(2,128)}) custom-call(s32[2,128]{1,0:T(2,128)S(1)} %bitcast.8, s32[2,128]{1,0:T(2,128)S(1)} %bitcast.10, bf16[272,768]{1,0:T(8,128)(2,1)S(1)} %own_block.1.first, bf16[272,768]{1,0:T(8,128)(2,1)S(1)} %collective-permute-done.4.second, ...), custom_call_target="tpu_custom_call" | custom-call | tf_op jit(solution)/shard_map/finish/pallas_call | solution.py:435
  (3 shorter events, 0.0 us)
Async XLA Ops:
  0.6 0.9 %copy-start.3 = (bf16[128,768]{1,0:T(8,128)(2,1)S(1)}, bf16[128,768]{1,0:T(8,128)(2,1)}, u32[]{:S(2)}) copy-start(bf16[128,768]{1,0:T(8,128)(2,1)} %queries.1) | copy-start | bytes 589828
  1.6 0.7 %copy-start.4 = (s32[128,2]{0,1:T(2,128)S(1)}, s32[128,2]{0,1:T(2,128)}, u32[]{:S(2)}) copy-start(s32[128,2]{0,1:T(2,128)} %param.6) | copy-start | bytes 3076
  2.2 0.7 %copy-start.6 = (s32[128,2]{0,1:T(2,128)S(1)}, s32[128,2]{0,1:T(2,128)}, u32[]{:S(2)}) copy-start(s32[128,2]{0,1:T(2,128)} %param.7) | copy-start | bytes 3076
  3.0 12.0 %collective-permute-start = (bf16[144,768]{1,0:T(8,128)(2,1)S(1)}, bf16[144,768]{1,0:T(8,128)(2,1)S(1)}, u32[]{:S(2)}, u32[]{:S(2)}) collective-permute-start(bf16[144,768]{1,0:T(8,128)(2,1)S(1)} %pack.1.message), channel_id=1, source_target_pairs={{0,1},{1,0},{2,3},{3,2},{4,5},{5,4},{6,7},{7,6},{8,9},{9,8},{10,11... | collective-permute-start | bytes 663560 | tf_op jit(solution)/shard_map/ppermute | solution.py:458
  5.1 11.3 %collective-permute-start.1 = (bf16[144,768]{1,0:T(8,128)(2,1)S(1)}, bf16[144,768]{1,0:T(8,128)(2,1)S(1)}, u32[]{:S(2)}, u32[]{:S(2)}) collective-permute-start(bf16[144,768]{1,0:T(8,128)(2,1)S(1)} %pack.1.message), channel_id=1, source_target_pairs={{3,4},{7,8},{11,12},{15,16},{19,20},{23,24},{27,28},{4,3},{8,7},{1... | collective-permute-start | bytes 663560 | tf_op jit(solution)/shard_map/ppermute | solution.py:459
  10.4 4.5 %copy-start = (bf16[8192,768]{1,0:T(8,128)(2,1)}, bf16[8192,768]{1,0:T(8,128)(2,1)S(1)}, u32[]{:S(2)}) copy-start(bf16[8192,768]{1,0:T(8,128)(2,1)S(1)} %load.1.docs) | copy-start | bytes 37748740
  15.0 3.4 %collective-permute-start.2 = (bf16[144,768]{1,0:T(8,128)(2,1)S(1)}, bf16[144,768]{1,0:T(8,128)(2,1)S(1)}, u32[]{:S(2)}, u32[]{:S(2)}) collective-permute-start(bf16[144,768]{1,0:T(8,128)(2,1)S(1)} %collective-permute-done.near), channel_id=1, source_target_pairs={{0,2},{4,6},{8,10},{12,14},{16,18},{20,22},{24,26},{28,30},{3,1},{... | collective-permute-start | bytes 663560 | tf_op jit(solution)/shard_map/ppermute | solution.py:461
  18.3 4.6 %copy-start.1 = (bf16[8192,768]{1,0:T(8,128)(2,1)S(1)}, bf16[8192,768]{1,0:T(8,128)(2,1)}, u32[]{:S(2)}) copy-start(bf16[8192,768]{1,0:T(8,128)(2,1)} %copy-done) | copy-start | bytes 37748740
  22.9 21.9 %copy-start.2 = (bf16[8192,768]{1,0:T(8,128)(2,1)S(1)}, bf16[8192,768]{1,0:T(8,128)(2,1)}, u32[]{:S(2)}) copy-start(bf16[8192,768]{1,0:T(8,128)(2,1)} %copy-done) | copy-start | bytes 37748740
  36.5 21.7 %copy-start.5 = (s32[128,2]{0,1:T(2,128)S(1)}, s32[128,2]{0,1:T(2,128)}, u32[]{:S(2)}) copy-start(s32[128,2]{0,1:T(2,128)} %param.6) | copy-start | bytes 3076
  36.5 21.7 %copy-start.7 = (s32[128,2]{0,1:T(2,128)S(1)}, s32[128,2]{0,1:T(2,128)}, u32[]{:S(2)}) copy-start(s32[128,2]{0,1:T(2,128)} %param.7) | copy-start | bytes 3076
  36.5 3.4 %collective-permute-start.3 = (bf16[272,768]{1,0:T(8,128)(2,1)S(1)}, bf16[272,768]{1,0:T(8,128)(2,1)S(1)}, u32[]{:S(2)}, u32[]{:S(2)}) collective-permute-start(bf16[272,768]{1,0:T(8,128)(2,1)S(1)} %get-tuple-element.13), channel_id=1, source_target_pairs={{2,0},{6,4},{10,8},{14,12},{18,16},{22,20},{26,24},{30,28},{1,3},{... | collective-permute-start | bytes 1253384 | tf_op jit(solution)/shard_map/ppermute | solution.py:465
  38.6 16.7 %collective-permute-start.5 = (bf16[272,768]{1,0:T(8,128)(2,1)S(1)}, bf16[272,768]{1,0:T(8,128)(2,1)S(1)}, u32[]{:S(2)}, u32[]{:S(2)}) collective-permute-start(bf16[272,768]{1,0:T(8,128)(2,1)S(1)} %get-tuple-element.13), channel_id=1, source_target_pairs={{3,4},{7,8},{11,12},{15,16},{19,20},{23,24},{27,28},{4,3},{8,7},{1... | collective-permute-start | bytes 1253384 | tf_op jit(solution)/shard_map/ppermute | solution.py:464
  41.1 17.1 %collective-permute-start.4 = (bf16[272,768]{1,0:T(8,128)(2,1)S(1)}, bf16[272,768]{1,0:T(8,128)(2,1)S(1)}, u32[]{:S(2)}, u32[]{:S(2)}) collective-permute-start(bf16[272,768]{1,0:T(8,128)(2,1)S(1)} %merge.1), channel_id=1, source_target_pairs={{0,1},{1,0},{2,3},{3,2},{4,5},{5,4},{6,7},{7,6},{8,9},{9,8},{10,11... | collective-permute-start | bytes 1253384 | tf_op jit(solution)/shard_map/ppermute | solution.py:466

commit v4 on v3

--- a/solution.py
+++ b/solution.py
@@ -21,10 +21,10 @@
 DOC_TILE = 1024
 DOT_TILE = 256
 ROW_TILE = 16
-LOADS = 8
 
 VMEM = pl.BlockSpec(memory_space=pltpu.VMEM)
 SMEM = pl.BlockSpec(memory_space=pltpu.SMEM)
+HBM = pl.BlockSpec(memory_space=pltpu.HBM)
 
 
 def params(mebibytes):
@@ -47,112 +47,143 @@
     return high, middle, rest - middle
 
 
-def row_scratch(rows, docs, width, tile):
+def row_scratch(rows, window, items, docs, width, tile):
     return [
+        pltpu.VMEM((docs, width), BF16),
+        pltpu.SemaphoreType.DMA((docs // tile,)),
         pltpu.VMEM((rows, width), BF16),
         pltpu.VMEM((2, rows, LANES), jnp.int32),
         pltpu.VMEM((rows, LANES), F32),
         pltpu.VMEM((rows, LANES), F32),
         pltpu.VMEM((rows, LANES), F32),
-        pltpu.VMEM((rows, tile), F32),
-        pltpu.VMEM((rows, tile), F32),
-        pltpu.VMEM((docs // tile, rows, tile), F32),
-        pltpu.VMEM((rows, tile), BF16),
-        pltpu.VMEM((rows, tile), BF16),
+        pltpu.VMEM((window, tile), F32),
+        pltpu.VMEM((window, tile), F32),
+        pltpu.VMEM((items, window, tile), F32),
+        pltpu.VMEM((window, tile), BF16),
+        pltpu.VMEM((window, tile), BF16),
         pltpu.VMEM((rows, width), F32),
     ]
 
 
-def attend_rows(docs, scratch):
-    rows_q, bounds, peak, score_sum, mass, s_a, s_b, masked, p_a, p_b, acc = scratch
-    n_docs, width = docs.shape
-    rows, tile = s_a.shape
-    tiles = n_docs // tile
+def tile_copy(corpus, docs, arrived, t):
+    tile = docs.shape[0] // arrived.shape[0]
+    at = pl.ds(pl.multiple_of(t * tile, tile), tile)
+    return pltpu.make_async_copy(corpus.at[at], docs.at[at], arrived.at[t])
+
+
+def start_copies(corpus, docs, arrived):
+    for t in range(arrived.shape[0]):
+        tile_copy(corpus, docs, arrived, t).start()
+
+
+def attend_rows(scratch, count, item, ready):
+    docs, _, rows_q, bounds, peak, score_sum, mass, s_a, s_b, masked, p_a, p_b, acc = scratch
+    width = docs.shape[1]
+    window, tile = s_a.shape
     scale = SCORE_SCALE / math.sqrt(width)
-    starts = range(0, rows, ROW_TILE)
+    starts = range(0, window, ROW_TILE)
+
+    def rows_from(first, n):
+        if isinstance(first, int):
+            return slice(first, first + n)
+        return pl.ds(pl.multiple_of(first, ROW_TILE), n)
 
     def share(part, parts):
         each = -(-len(starts) // parts)
         return starts[part * each : (part + 1) * each]
 
-    def score(t, out, part):
+    def score(i, out, part):
+        t, first_row = item(i)
         first = pl.multiple_of(t * tile + part * DOT_TILE, DOT_TILE)
         out[:, part * DOT_TILE : (part + 1) * DOT_TILE] = lax.dot_general(
-            rows_q[...], docs[pl.ds(first, DOT_TILE), :], NT, preferred_element_type=F32
+            rows_q[rows_from(first_row, window), :],
+            docs[pl.ds(first, DOT_TILE), :],
+            NT,
+            preferred_element_type=F32,
         )
 
-    def scan(t, scores, some):
+    def scan(i, scores, some):
+        t, first_row = item(i)
         for r in some:
-            at = slice(r, r + ROW_TILE)
+            at = rows_from(first_row + r, ROW_TILE)
             offset = t * tile - bounds[0, at, :]
             length = bounds[1, at, :].astype(jnp.uint32)
             top, total = peak[at, :], score_sum[at, :]
             for c in range(0, tile, LANES):
-                value = scores[at, c : c + LANES]
+                value = scores[r : r + ROW_TILE, c : c + LANES]
                 inside = (offset + c).astype(jnp.uint32) < length
                 kept = jnp.where(inside, value, NEG)
                 top = jnp.maximum(top, kept)
                 total = total + jnp.where(inside, value, 0.0)
-                masked[t, at, c : c + LANES] = kept
+                masked[i, r : r + ROW_TILE, c : c + LANES] = kept
             peak[at, :] = top
             score_sum[at, :] = total
 
-    def score_and_scan(t_score, out, t_scan, scores):
+    def score_and_scan(i_score, out, i_scan, scores):
         parts = tile // DOT_TILE
         for part in range(parts):
-            score(t_score, out, part)
-            scan(t_scan, scores, share(part, parts))
+            score(i_score, out, part)
+            scan(i_scan, scores, share(part, parts))
 
     peak[...] = jnp.full(peak.shape, NEG, F32)
     score_sum[...] = jnp.zeros(score_sum.shape, F32)
     mass[...] = jnp.zeros(mass.shape, F32)
+    ready(0)
     for part in range(tile // DOT_TILE):
         score(0, s_a, part)
 
-    def first_step(i, carry):
-        t = 2 * i
-        score_and_scan(t + 1, s_b, t, s_a)
-        score_and_scan(jnp.minimum(t + 2, tiles - 1), s_a, t + 1, s_b)
+    def first_step(k, carry):
+        i = 2 * k
+        ready(i + 1)
+
+        @pl.when(i + 2 < count)
+        def _():
+            ready(i + 2)
+
+        score_and_scan(i + 1, s_b, i, s_a)
+        score_and_scan(jnp.minimum(i + 2, count - 1), s_a, i + 1, s_b)
         return carry
 
-    lax.fori_loop(0, tiles // 2, first_step, 0)
+    lax.fori_loop(0, count // 2, first_step, 0)
     top = jnp.max(peak[...], axis=1, keepdims=True)
     peak[...] = jnp.broadcast_to(jnp.maximum(top, 0.5 * NEG), peak.shape)
     acc[...] = jnp.zeros(acc.shape, F32)
 
-    def weigh(t, out, some):
+    def weigh(i, out, some):
+        _, first_row = item(i)
         for r in some:
-            at = slice(r, r + ROW_TILE)
+            at = rows_from(first_row + r, ROW_TILE)
             shift, total = peak[at, :], mass[at, :]
             for c in range(0, tile, LANES):
-                p = jnp.exp2((masked[t, at, c : c + LANES] - shift) * (scale * LOG2E))
+                p = jnp.exp2((masked[i, r : r + ROW_TILE, c : c + LANES] - shift) * (scale * LOG2E))
                 total = total + p
-                out[at, c : c + LANES] = p.astype(BF16)
+                out[r : r + ROW_TILE, c : c + LANES] = p.astype(BF16)
             mass[at, :] = total
 
-    def pool(t, weights, part):
+    def pool(i, weights, part):
+        t, first_row = item(i)
         at = slice(part * DOT_TILE, (part + 1) * DOT_TILE)
         block = docs[pl.ds(pl.multiple_of(t * tile, tile), tile), at]
-        acc[:, at] += jnp.dot(weights[...], block, preferred_element_type=F32)
-
-    def pool_and_weigh(t, weights, t_weigh, out):
+        acc[rows_from(first_row, window), at] += jnp.dot(weights[...], block, preferred_element_type=F32)
+
+    def pool_and_weigh(i, weights, i_weigh, out):
         parts = width // DOT_TILE
         for part in range(parts):
-            pool(t, weights, part)
-            weigh(t_weigh, out, share(part, parts))
+            pool(i, weights, part)
+            weigh(i_weigh, out, share(part, parts))
 
     weigh(0, p_a, starts)
 
-    def second_step(i, carry):
-        t = 2 * i + 1
-        pool_and_weigh(t - 1, p_a, t, p_b)
-        pool_and_weigh(t, p_b, t + 1, p_a)
+    def second_step(k, carry):
+        i = 2 * k + 1
+        pool_and_weigh(i - 1, p_a, i, p_b)
+        pool_and_weigh(i, p_b, i + 1, p_a)
         return carry
 
-    lax.fori_loop(0, tiles // 2 - 1, second_step, 0)
-    pool_and_weigh(tiles - 2, p_a, tiles - 1, p_b)
+    lax.fori_loop(0, count // 2 - 1, second_step, 0)
+    pool_and_weigh(count - 2, p_a, count - 1, p_b)
     for part in range(width // DOT_TILE):
-        pool(tiles - 1, p_b, part)
+        pool(count - 1, p_b, part)
     return (
         top * scale,
         jnp.sum(mass[...], axis=1, keepdims=True),
@@ -176,9 +207,10 @@
     bounds[1, at, :] = jnp.broadcast_to(length, shape)
 
 
-def own_kernel(shift, message, docs, out, *scratch):
+def own_kernel(shift, message, corpus, out, *scratch):
+    docs, arrived, rows_q, bounds = scratch[:4]
+    start_copies(corpus, docs, arrived)
     queries = message.shape[0] - META
-    rows_q, bounds = scratch[:2]
     unit = identity(queries)
     columns = lax.dot_general(
         unit, message[queries:, 0:queries], NT, preferred_element_type=F32
@@ -193,7 +225,14 @@
         low = bound(w)
         set_bounds(bounds, at, low, jnp.maximum(bound(2 + w) - low, 0))
         rows_q[at, :] = message[0:queries, :]
-    stats = stats_matrix(attend_rows(docs, scratch))
+    stats = stats_matrix(
+        attend_rows(
+            scratch,
+            arrived.shape[0],
+            lambda i: (i, 0),
+            lambda i: tile_copy(corpus, docs, arrived, i).wait(),
+        )
+    )
     out[0 : 2 * queries, :] = scratch[-1][...].astype(BF16)
     out[2 * queries :, :] = jnp.zeros((META, out.shape[1]), BF16)
     for w in range(2):
@@ -210,10 +249,10 @@
     return pl.pallas_call(
         own_kernel,
         out_shape=jax.ShapeDtypeStruct((2 * queries + META, width), BF16),
-        in_specs=[SMEM, VMEM, VMEM],
+        in_specs=[SMEM, VMEM, HBM],
         out_specs=VMEM,
-        scratch_shapes=row_scratch(2 * queries, docs, width, tile),
-        compiler_params=params(20),
+        scratch_shapes=row_scratch(2 * queries, 2 * queries, docs // tile, docs, width, tile),
+        compiler_params=params(44),
         cost_estimate=pl.CostEstimate(
             flops=8 * queries * docs * width,
             bytes_accessed=docs * width * 2,
@@ -223,83 +262,139 @@
     )(shift, message, corpus)
 
 
-def neighbour_kernel(shifts, near, far_a, far_b, docs, near_out, far_out, both_q, *scratch):
+def neighbour_kernel(
+    shifts, near, far_a, far_b, corpus, near_out, far_out, both_q, pooled, spans, item_spans, items, span_done, *scratch
+):
+    docs, arrived, rows_q, bounds = scratch[:4]
+    start_copies(corpus, docs, arrived)
     queries = near.shape[0] - META
-    rows_q, bounds = scratch[:2]
-    group = rows_q.shape[0]
+    n_docs = docs.shape[0]
+    tiles = arrived.shape[0]
+    tile = n_docs // tiles
+    window = scratch[7].shape[0]
     both_q[0:queries, :] = near[0:queries, :]
     both_q[queries:, :] = far_a[0:queries, :] + far_b[0:queries, :]
-
-    lows, lengths = [], []
-    for side, meta in enumerate((near[queries:, 0:queries], far_a[queries:, 0:queries] + far_b[queries:, 0:queries])):
+    metas = (near[queries:, 0:queries], far_a[queries:, 0:queries] + far_b[queries:, 0:queries])
+
+    lows, highs = [], []
+    for side, meta in enumerate(metas):
         meta = meta.astype(F32)
 
         def bound(k):
             value = meta[2 * k : 2 * k + 1, :] * 256.0 + meta[2 * k + 1 : 2 * k + 2, :]
-            return jnp.clip(value.astype(jnp.int32) - shifts[side], 0, docs.shape[0])
+            return jnp.clip(value.astype(jnp.int32) - shifts[side], 0, n_docs)
 
         for w in range(2):
-            low = bound(w)
-            lows.append(low)
-            lengths.append(jnp.maximum(bound(2 + w) - low, 0))
+            lows.append(bound(w))
+            highs.append(jnp.maximum(bound(2 + w), lows[-1]))
     blocks = len(lows)
+    rows = blocks * queries
+
+    keys = [
+        jnp.where(high > low, jnp.where(low == 0, high, n_docs + low), 2 * n_docs)
+        for low, high in zip(lows, highs)
+    ]
     parts = []
-    for low, length in zip(lows, lengths):
-        rows = [*split_int(low), *split_int(length)]
-        parts.append(jnp.concatenate(rows + [jnp.zeros((META - 4, queries), F32)], axis=0).astype(BF16))
-    flags = [(length > 0).astype(F32) for length in lengths]
-    stacked = jnp.concatenate(flags + [jnp.zeros((META - blocks, queries), F32)], axis=0).astype(BF16)
-    before = lax.broadcasted_iota(jnp.int32, (queries, queries), 0) < lax.broadcasted_iota(
-        jnp.int32, (queries, queries), 1
-    )
-    ranks = jnp.dot(stacked, before.astype(BF16), preferred_element_type=F32)
-    places, first = [], jnp.zeros((1, 1), F32)
+    for low, high, key in zip(lows, highs, keys):
+        lines = [*split_int(low), *split_int(high - low), *split_int(key)]
+        parts.append(jnp.concatenate(lines + [jnp.zeros((META - 6, queries), F32)], axis=0).astype(BF16))
+    unit = identity(queries)
+    lane = lax.broadcasted_iota(jnp.int32, (1, queries), 1)
+    line = lax.broadcasted_iota(jnp.int32, (queries, 1), 0)
+    places = [jnp.zeros((1, queries), F32)] * blocks
+    ordered = [keys[b] * rows + (lane + b * queries) for b in range(blocks)]
+    for a in range(blocks):
+        columns = lax.dot_general(unit, parts[a], NT, preferred_element_type=F32)
+        key = (columns[:, 4:5] * 256.0 + columns[:, 5:6]).astype(jnp.int32)
+        key = jnp.broadcast_to(key * rows + (line + a * queries), (queries, queries))
+        for b in range(blocks):
+            places[b] = places[b] + jnp.sum((key < ordered[b]).astype(F32), axis=0, keepdims=True)
+    places = [place.astype(jnp.int32) for place in places]
+
+    begin = lax.broadcasted_iota(jnp.int32, (tiles, queries), 0) * tile
+    first = jnp.full((tiles, 1), rows, jnp.int32)
+    last = jnp.zeros((tiles, 1), jnp.int32)
+    for low, high, place in zip(lows, highs, places):
+        met = (high > low) & (low < begin + tile) & (high > begin)
+        first = jnp.minimum(first, jnp.min(jnp.where(met, place, rows), axis=1, keepdims=True))
+        last = jnp.maximum(last, jnp.max(jnp.where(met, place + 1, 0), axis=1, keepdims=True))
+    column = lax.broadcasted_iota(jnp.int32, (tiles, LANES), 1)
+    spans[...] = jnp.where(column == 0, first, last)
+    copy = pltpu.make_async_copy(spans, item_spans, span_done)
+    copy.start()
+
+    pick = []
     for b in range(blocks):
-        places.append(jnp.where(flags[b] > 0, ranks[b : b + 1, :] + first, -1.0).astype(jnp.int32))
-        first = first + jnp.sum(flags[b], axis=1, keepdims=True)
-    active = jnp.max(first).astype(jnp.int32)
-
-    near_out[...] = jnp.zeros(near_out.shape, BF16)
-    far_out[...] = jnp.zeros(far_out.shape, BF16)
-
-    def work(g, carry):
-        row = lax.broadcasted_iota(jnp.int32, (group, queries), 0) + g * group
-        pick = [(row == place).astype(F32).astype(BF16) for place in places]
-        of_query = jnp.concatenate([pick[0] + pick[1], pick[2] + pick[3]], axis=1)
-        rows_q[...] = jnp.dot(of_query, both_q[...], preferred_element_type=F32).astype(BF16)
-        columns = jnp.zeros((group, META), F32)
-        for chosen, part in zip(pick, parts):
-            columns = columns + lax.dot_general(chosen, part, NT, preferred_element_type=F32)
-        low = (columns[:, 0:1] * 256.0 + columns[:, 1:2]).astype(jnp.int32)
-        length = (columns[:, 2:3] * 256.0 + columns[:, 3:4]).astype(jnp.int32)
-        set_bounds(bounds, slice(0, group), low, length)
-        stats = stats_matrix(attend_rows(docs, scratch))
-        pooled = scratch[-1][...].astype(BF16)
-        for b, chosen in enumerate(pick):
-            out = (near_out, far_out)[b // 2]
-            at = slice((b % 2) * queries, (b % 2 + 1) * queries)
-            out[at, :] += lax.dot_general(chosen, pooled, TN, preferred_element_type=F32).astype(BF16)
-            out[2 * queries :, at] += lax.dot_general(
-                stats, chosen, TN, preferred_element_type=F32
-            ).astype(BF16)
-        return carry
-
-    lax.fori_loop(0, (active + group - 1) // group, work, 0)
+        row = lax.broadcasted_iota(jnp.int32, (rows, queries), 0)
+        pick.append((row == places[b]).astype(F32).astype(BF16))
+    of_query = jnp.concatenate([pick[0] + pick[1], pick[2] + pick[3]], axis=1)
+    rows_q[0:rows, :] = jnp.dot(of_query, both_q[...], preferred_element_type=F32).astype(BF16)
+    rows_q[rows:, :] = jnp.zeros((rows_q.shape[0] - rows, rows_q.shape[1]), BF16)
+    columns = jnp.zeros((rows, META), F32)
+    for chosen, part in zip(pick, parts):
+        columns = columns + lax.dot_general(chosen, part, NT, preferred_element_type=F32)
+    low = (columns[:, 0:1] * 256.0 + columns[:, 1:2]).astype(jnp.int32)
+    length = (columns[:, 2:3] * 256.0 + columns[:, 3:4]).astype(jnp.int32)
+    set_bounds(bounds, slice(0, rows), low, length)
+    none = jnp.zeros((bounds.shape[1] - rows, 1), jnp.int32)
+    set_bounds(bounds, slice(rows, bounds.shape[1]), none, none)
+
+    copy.wait()
+    count = jnp.int32(0)
+    for t in range(tiles):
+        head = jnp.minimum(item_spans[t, 0] // ROW_TILE * ROW_TILE, rows - ROW_TILE)
+        for k in range(-(-rows // window)):
+            items[0, count] = t
+            items[1, count] = head + k * window
+            items[2, count] = 1 if k == 0 else 0
+            more = True if k == 0 else head + k * window < item_spans[t, 1]
+            count = count + jnp.where(more, 1, 0)
+    items[0, count] = tiles - 1
+    items[1, count] = rows
+    items[2, count] = 0
+    count = (count + 1) // 2 * 2
+
+    def ready(i):
+        @pl.when(items[2, i] == 1)
+        def _():
+            tile_copy(corpus, docs, arrived, items[0, i]).wait()
+
+    stats = stats_matrix(attend_rows(scratch, count, lambda i: (items[0, i], items[1, i]), ready))[0:rows, :]
+    pooled[...] = scratch[-1][0:rows, :].astype(BF16)
+    for out in (near_out, far_out):
+        out[2 * queries :, :] = jnp.zeros((META, out.shape[1]), BF16)
+    for b, chosen in enumerate(pick):
+        out = (near_out, far_out)[b // 2]
+        at = slice((b % 2) * queries, (b % 2 + 1) * queries)
+        out[at, :] = lax.dot_general(chosen, pooled[...], TN, preferred_element_type=F32).astype(BF16)
+        out[2 * queries :, at] = lax.dot_general(
+            stats, chosen, TN, preferred_element_type=F32
+        ).astype(BF16)
 
 
 def neighbours(shifts, near, far_a, far_b, corpus):
     docs, width = corpus.shape
     queries = near.shape[0] - META
+    rows = 4 * queries
     tile = min(DOC_TILE, docs // 2)
-    group = min(4 * queries, (2 * queries + 3 * queries // 8) // ROW_TILE * ROW_TILE)
+    window = min(rows, (queries + 3 * queries // 8) // ROW_TILE * ROW_TILE)
+    most = docs // tile * -(-rows // window) + 2
     result = jax.ShapeDtypeStruct((2 * queries + META, width), BF16)
     return pl.pallas_call(
         neighbour_kernel,
         out_shape=(result, result),
-        in_specs=[SMEM, VMEM, VMEM, VMEM, VMEM],
+        in_specs=[SMEM, VMEM, VMEM, VMEM, HBM],
         out_specs=(VMEM, VMEM),
-        scratch_shapes=[pltpu.VMEM((2 * queries, width), BF16)] + row_scratch(group, docs, width, tile),
-        compiler_params=params(24),
+        scratch_shapes=[
+            pltpu.VMEM((2 * queries, width), BF16),
+            pltpu.VMEM((rows, width), BF16),
+            pltpu.VMEM((docs // tile, LANES), jnp.int32),
+            pltpu.SMEM((docs // tile, LANES), jnp.int32),
+            pltpu.SMEM((3, most), jnp.int32),
+            pltpu.SemaphoreType.DMA,
+        ]
+        + row_scratch(rows + window, window, most, docs, width, tile),
+        compiler_params=params(44),
         cost_estimate=pl.CostEstimate(
             flops=8 * queries * docs * width,
             bytes_accessed=docs * width * 2,
@@ -307,31 +402,6 @@
         ),
         name="neighbour_blocks",
     )(shifts, near, far_a, far_b, corpus)
-
-
-def load_kernel(corpus, out, arrived):
-    step = corpus.shape[0] // LOADS
-    copies = [
-        pltpu.make_async_copy(corpus.at[pl.ds(k * step, step)], out.at[pl.ds(k * step, step)], arrived.at[k])
-        for k in range(LOADS)
-    ]
-    for copy in copies:
-        copy.start()
-    for copy in copies:
-        copy.wait()
-
-
-def load(corpus):
-    return pl.pallas_call(
-        load_kernel,
-        out_shape=jax.ShapeDtypeStruct(corpus.shape, corpus.dtype),
-        in_specs=[pl.BlockSpec(memory_space=pltpu.HBM)],
-        out_specs=VMEM,
-        scratch_shapes=[pltpu.SemaphoreType.DMA((LOADS,))],
-        compiler_params=params(36),
-        cost_estimate=pl.CostEstimate(flops=0, bytes_accessed=2 * corpus.size * 2, transcendentals=0),
-        name="load",
-    )(corpus)
 
 
 def pack_kernel(base, queries, starts, ends, out):
@@ -457,7 +527,6 @@
     message = pack(base, queries, starts, ends)
     near = lax.ppermute(message, AXES, across)
     far_a = lax.ppermute(message, AXES, between)
-    near, corpus = lax.optimization_barrier((near, load(corpus)))
     far_b = lax.ppermute(near, AXES, relay)
     shifts = jnp.stack([2 * docs * odd, 2 * docs * (1 - odd)]).astype(jnp.int32)
     near_part, far_part = neighbours(shifts, near, far_a, far_b, corpus)

time: 61.2 us -> 52 us (0.85); the launches traced: 60 us -> 51.7 us
  local copies, waits for them, and re-layouts: 11.4 us -> 2.29 us
  Pallas kernels: 31.8 us -> 28.9 us
  waiting for transfers between devices: 5.49 us -> 8.1 us
  starting transfers between devices: 10.6 us -> 11.6 us
    unnamed x16 -> x10, local copies, waits for them, and re-layouts: 11.4 us -> 2.29 us
    pallas_call x1 -> x0, Pallas kernels: 4.7 us -> none  [load(): pl.pallas_call(load_kernel, out_shape=jax.ShapeDtypeStruct(corpus.shape,...]
    ppermute x1, waiting for transfers between devices: 0.01 us -> 4.48 us  [local(): near = lax.ppermute(message, AXES, across)]
    ppermute x1, waiting for transfers between devices: 2.85 us -> 0.88 us  [local(): near_back = lax.ppermute(merge(near_part, relayed), AXES, across)]
    pallas_call x1, Pallas kernels: 10.5 us -> 11.9 us  [own(): pl.pallas_call(own_kernel, out_shape=jax.ShapeDtypeStruct((2 * queries +...]
    ppermute x1, starting transfers between devices: 3.75 us -> 4.85 us  [local(): near_back = lax.ppermute(merge(near_part, relayed), AXES, across)]
  transfers between devices with their start and end apart: 6 -> 6, of which waited for: 3 -> 4; matrix products, arithmetic and copies ran while one was open for 0% -> 0% of each run, Pallas kernels for 27% -> 25%
where the time goes in v4:
time: 52 us; the launch traced here: 51.7 us
  Pallas kernels  28.9 us (56%)
  starting transfers between devices  11.6 us (22%)
  waiting for transfers between devices  8.1 us (16%)
  local copies, waits for them, and re-layouts  2.29 us (4%)
  between operations  0.74 us (1%)
    pallas_call x1, Pallas kernels, neighbours(): pl.pallas_call(neighbour_kernel, out_shape=(result, result), in_specs=[SM...  14 us
    pallas_call x1, Pallas kernels, own(): pl.pallas_call(own_kernel, out_shape=jax.ShapeDtypeStruct((2 * queries +...  11.9 us
    ppermute x1, starting transfers between devices, local(): near_back = lax.ppermute(merge(near_part, relayed), AXES, across)  4.85 us
    ppermute x1, waiting for transfers between devices, local(): near = lax.ppermute(message, AXES, across)  4.48 us
    unnamed x10, local copies, waits for them, and re-layouts  2.29 us
    ppermute x1, starting transfers between devices, local(): near = lax.ppermute(message, AXES, across)  2.11 us
    ppermute x1, waiting for transfers between devices, local(): far_b = lax.ppermute(near, AXES, relay)  2.09 us
    ppermute x1, starting transfers between devices, local(): relayed = lax.ppermute(far_part, AXES, relay_back)  2.03 us
  transfers between devices with their start and end apart: 6, of which 4 were waited for; matrix products, arithmetic and copies ran while one was open for 0% of the time, Pallas kernels for 25%

profile of v4, /device:TPU:1, one launch (start us, length us, event | category | flops | bytes accessed | tf_op | source)
XLA Modules:
  0.0 51.7 jit_solution(8359210232033121884)
XLA Ops:
  0.6 0.0 copy-start
  0.6 0.9 %copy-done = bf16[128,768]{1,0:T(8,128)(2,1)S(1)} copy-done((bf16[128,768]{1,0:T(8,128)(2,1)S(1)}, bf16[128,768]{1,0:T(8,128)(2,1)}, u32[]{:S(2)}) %copy-start) | copy-done | bytes 196632
  1.6 0.0 copy-start.1
  1.6 0.7 %copy-done.1 = s32[128,2]{0,1:T(2,128)S(1)} copy-done((s32[128,2]{0,1:T(2,128)S(1)}, s32[128,2]{0,1:T(2,128)}, u32[]{:S(2)}) %copy-start.1) | copy-done | bytes 1048
  2.2 0.0 copy-start.3
  2.2 0.7 %copy-done.3 = s32[128,2]{0,1:T(2,128)S(1)} copy-done((s32[128,2]{0,1:T(2,128)S(1)}, s32[128,2]{0,1:T(2,128)}, u32[]{:S(2)}) %copy-start.3) | copy-done | bytes 1048
  3.0 2.1 %collective-permute-start = (bf16[144,768]{1,0:T(8,128)(2,1)S(1)}, bf16[144,768]{1,0:T(8,128)(2,1)S(1)}, u32[]{:S(2)}, u32[]{:S(2)}) collective-permute-start(bf16[144,768]{1,0:T(8,128)(2,1)S(1)} %pack.1.message), channel_id=1, source_target_pairs={{0,1},{1,0},{2,3},{3,2},{4,5},{5,4},{6,7},{7,6},{8,9},{9,8},{10,11... | collective-permute-start | bytes 663560 | tf_op jit(solution)/shard_map/ppermute | solution.py:528
  5.1 0.7 %collective-permute-start.1 = (bf16[144,768]{1,0:T(8,128)(2,1)S(1)}, bf16[144,768]{1,0:T(8,128)(2,1)S(1)}, u32[]{:S(2)}, u32[]{:S(2)}) collective-permute-start(bf16[144,768]{1,0:T(8,128)(2,1)S(1)} %pack.1.message), channel_id=1, source_target_pairs={{3,4},{7,8},{11,12},{15,16},{19,20},{23,24},{27,28},{4,3},{8,7},{1... | collective-permute-start | bytes 663560 | tf_op jit(solution)/shard_map/ppermute | solution.py:529
  5.7 4.5 %collective-permute-done.near = bf16[144,768]{1,0:T(8,128)(2,1)S(1)} collective-permute-done((bf16[144,768]{1,0:T(8,128)(2,1)S(1)}, bf16[144,768]{1,0:T(8,128)(2,1)S(1)}, u32[]{:S(2)}, u32[]{:S(2)}) %collective-permute-start) | collective-permute-done | bytes 221216 | tf_op jit(solution)/shard_map/ppermute | solution.py:528
  10.2 1.3 %collective-permute-start.2 = (bf16[144,768]{1,0:T(8,128)(2,1)S(1)}, bf16[144,768]{1,0:T(8,128)(2,1)S(1)}, u32[]{:S(2)}, u32[]{:S(2)}) collective-permute-start(bf16[144,768]{1,0:T(8,128)(2,1)S(1)} %collective-permute-done.near), channel_id=1, source_target_pairs={{0,2},{4,6},{8,10},{12,14},{16,18},{20,22},{24,26},{28,30},{3,1},{... | collective-permute-start | bytes 663560 | tf_op jit(solution)/shard_map/ppermute | solution.py:530
  11.5 0.1 pad_add_fusion.shifts
  11.6 0.0 collective-permute-done.1.far_a
  11.6 2.1 %collective-permute-done.2.far_b = bf16[144,768]{1,0:T(8,128)(2,1)S(1)} collective-permute-done((bf16[144,768]{1,0:T(8,128)(2,1)S(1)}, bf16[144,768]{1,0:T(8,128)(2,1)S(1)}, u32[]{:S(2)}, u32[]{:S(2)}) %collective-permute-start.2) | collective-permute-done | bytes 221216 | tf_op jit(solution)/shard_map/ppermute | solution.py:530
  13.7 14.0 %neighbour_blocks.1 = (bf16[272,768]{1,0:T(8,128)(2,1)S(1)}, bf16[272,768]{1,0:T(8,128)(2,1)S(1)}) custom-call(s32[2]{0:T(128)S(1)} %pad_add_fusion.shifts, bf16[144,768]{1,0:T(8,128)(2,1)S(1)} %collective-permute-done.near, bf16[144,768]{1,0:T(8,128)(2,1)S(1)} %collective-permute-done.1.far_a, bf16[144,768]{1,0:T(8,128)(2,1)S(1)} %collective-permute-done.2.far_b, ...), custom_call_target="tpu_custom_call" | custom-call | flops 6442450944 | bytes 12582912 | tf_op jit(solution)/shard_map/neighbour_blocks/pallas_call | solution.py:383
  27.7 0.0 copy-start.2
  27.7 0.0 copy-start.4
  27.7 2.0 %collective-permute-start.3 = (bf16[272,768]{1,0:T(8,128)(2,1)S(1)}, bf16[272,768]{1,0:T(8,128)(2,1)S(1)}, u32[]{:S(2)}, u32[]{:S(2)}) collective-permute-start(bf16[272,768]{1,0:T(8,128)(2,1)S(1)} %get-tuple-element.9), channel_id=1, source_target_pairs={{2,0},{6,4},{10,8},{14,12},{18,16},{22,20},{26,24},{30,28},{1,3},{... | collective-permute-start | bytes 1253384 | tf_op jit(solution)/shard_map/ppermute | solution.py:534
  29.8 0.7 %collective-permute-start.5 = (bf16[272,768]{1,0:T(8,128)(2,1)S(1)}, bf16[272,768]{1,0:T(8,128)(2,1)S(1)}, u32[]{:S(2)}, u32[]{:S(2)}) collective-permute-start(bf16[272,768]{1,0:T(8,128)(2,1)S(1)} %get-tuple-element.9), channel_id=1, source_target_pairs={{3,4},{7,8},{11,12},{15,16},{19,20},{23,24},{27,28},{4,3},{8,7},{1... | collective-permute-start | bytes 1253384 | tf_op jit(solution)/shard_map/ppermute | solution.py:533
  30.5 0.6 %collective-permute-done.3.second = bf16[272,768]{1,0:T(8,128)(2,1)S(1)} collective-permute-done((bf16[272,768]{1,0:T(8,128)(2,1)S(1)}, bf16[272,768]{1,0:T(8,128)(2,1)S(1)}, u32[]{:S(2)}, u32[]{:S(2)}) %collective-permute-start.3) | collective-permute-done | bytes 417824 | tf_op jit(solution)/shard_map/ppermute | solution.py:534
  31.1 1.1 %merge.1 = bf16[272,768]{1,0:T(8,128)(2,1)S(1)} custom-call(bf16[272,768]{1,0:T(8,128)(2,1)S(1)} %get-tuple-element.11.first, bf16[272,768]{1,0:T(8,128)(2,1)S(1)} %collective-permute-done.3.second), custom_call_target="tpu_custom_call" | custom-call | tf_op jit(solution)/shard_map/merge/pallas_call | solution.py:465
  32.3 4.9 %collective-permute-start.4 = (bf16[272,768]{1,0:T(8,128)(2,1)S(1)}, bf16[272,768]{1,0:T(8,128)(2,1)S(1)}, u32[]{:S(2)}, u32[]{:S(2)}) collective-permute-start(bf16[272,768]{1,0:T(8,128)(2,1)S(1)} %merge.1), channel_id=1, source_target_pairs={{0,1},{1,0},{2,3},{3,2},{4,5},{5,4},{6,7},{7,6},{8,9},{9,8},{10,11... | collective-permute-start | bytes 1253384 | tf_op jit(solution)/shard_map/ppermute | solution.py:535
  37.1 11.9 %own_block.1.first = bf16[272,768]{1,0:T(8,128)(2,1)S(1)} custom-call(s32[1]{0:T(128)} %constant.21.clone.1.shift, bf16[144,768]{1,0:T(8,128)(2,1)S(1)} %pack.1.message, bf16[8192,768]{1,0:T(8,128)(2,1)} %corpus.3), custom_call_target="tpu_custom_call" | custom-call | flops 6442450944 | bytes 12582912 | tf_op jit(solution)/shard_map/own_block/pallas_call | solution.py:249
  49.0 0.0 collective-permute-done.5.third
  49.0 0.9 %collective-permute-done.4.second = bf16[272,768]{1,0:T(8,128)(2,1)S(1)} collective-permute-done((bf16[272,768]{1,0:T(8,128)(2,1)S(1)}, bf16[272,768]{1,0:T(8,128)(2,1)S(1)}, u32[]{:S(2)}, u32[]{:S(2)}) %collective-permute-start.4) | collective-permute-done | bytes 417824 | tf_op jit(solution)/shard_map/ppermute | solution.py:535
  49.9 0.0 copy-done.2
  49.9 0.0 copy-done.4
  49.9 1.8 %finish.1 = (bf16[128,2,768]{2,1,0:T(2,128)(2,1)}, f32[2,128]{1,0:T(2,128)}, f32[2,128]{1,0:T(2,128)}) custom-call(s32[2,128]{1,0:T(2,128)S(1)} %bitcast.8, s32[2,128]{1,0:T(2,128)S(1)} %bitcast.10, bf16[272,768]{1,0:T(8,128)(2,1)S(1)} %own_block.1.first, bf16[272,768]{1,0:T(8,128)(2,1)S(1)} %collective-permute-done.4.second, ...), custom_call_target="tpu_custom_call" | custom-call | tf_op jit(solution)/shard_map/finish/pallas_call | solution.py:505
  (1 shorter events, 0.0 us)
Async XLA Ops:
  0.6 0.9 %copy-start = (bf16[128,768]{1,0:T(8,128)(2,1)S(1)}, bf16[128,768]{1,0:T(8,128)(2,1)}, u32[]{:S(2)}) copy-start(bf16[128,768]{1,0:T(8,128)(2,1)} %queries.1) | copy-start | bytes 589828
  1.6 0.7 %copy-start.1 = (s32[128,2]{0,1:T(2,128)S(1)}, s32[128,2]{0,1:T(2,128)}, u32[]{:S(2)}) copy-start(s32[128,2]{0,1:T(2,128)} %param.6) | copy-start | bytes 3076
  2.2 0.7 %copy-start.3 = (s32[128,2]{0,1:T(2,128)S(1)}, s32[128,2]{0,1:T(2,128)}, u32[]{:S(2)}) copy-start(s32[128,2]{0,1:T(2,128)} %param.7) | copy-start | bytes 3076
  3.0 7.3 %collective-permute-start = (bf16[144,768]{1,0:T(8,128)(2,1)S(1)}, bf16[144,768]{1,0:T(8,128)(2,1)S(1)}, u32[]{:S(2)}, u32[]{:S(2)}) collective-permute-start(bf16[144,768]{1,0:T(8,128)(2,1)S(1)} %pack.1.message), channel_id=1, source_target_pairs={{0,1},{1,0},{2,3},{3,2},{4,5},{5,4},{6,7},{7,6},{8,9},{9,8},{10,11... | collective-permute-start | bytes 663560 | tf_op jit(solution)/shard_map/ppermute | solution.py:528
  5.1 6.5 %collective-permute-start.1 = (bf16[144,768]{1,0:T(8,128)(2,1)S(1)}, bf16[144,768]{1,0:T(8,128)(2,1)S(1)}, u32[]{:S(2)}, u32[]{:S(2)}) collective-permute-start(bf16[144,768]{1,0:T(8,128)(2,1)S(1)} %pack.1.message), channel_id=1, source_target_pairs={{3,4},{7,8},{11,12},{15,16},{19,20},{23,24},{27,28},{4,3},{8,7},{1... | collective-permute-start | bytes 663560 | tf_op jit(solution)/shard_map/ppermute | solution.py:529
  10.2 3.5 %collective-permute-start.2 = (bf16[144,768]{1,0:T(8,128)(2,1)S(1)}, bf16[144,768]{1,0:T(8,128)(2,1)S(1)}, u32[]{:S(2)}, u32[]{:S(2)}) collective-permute-start(bf16[144,768]{1,0:T(8,128)(2,1)S(1)} %collective-permute-done.near), channel_id=1, source_target_pairs={{0,2},{4,6},{8,10},{12,14},{16,18},{20,22},{24,26},{28,30},{3,1},{... | collective-permute-start | bytes 663560 | tf_op jit(solution)/shard_map/ppermute | solution.py:530
  27.7 22.2 %copy-start.2 = (s32[128,2]{0,1:T(2,128)S(1)}, s32[128,2]{0,1:T(2,128)}, u32[]{:S(2)}) copy-start(s32[128,2]{0,1:T(2,128)} %param.6) | copy-start | bytes 3076
  27.7 22.2 %copy-start.4 = (s32[128,2]{0,1:T(2,128)S(1)}, s32[128,2]{0,1:T(2,128)}, u32[]{:S(2)}) copy-start(s32[128,2]{0,1:T(2,128)} %param.7) | copy-start | bytes 3076
  27.7 3.4 %collective-permute-start.3 = (bf16[272,768]{1,0:T(8,128)(2,1)S(1)}, bf16[272,768]{1,0:T(8,128)(2,1)S(1)}, u32[]{:S(2)}, u32[]{:S(2)}) collective-permute-start(bf16[272,768]{1,0:T(8,128)(2,1)S(1)} %get-tuple-element.9), channel_id=1, source_target_pairs={{2,0},{6,4},{10,8},{14,12},{18,16},{22,20},{26,24},{30,28},{1,3},{... | collective-permute-start | bytes 1253384 | tf_op jit(solution)/shard_map/ppermute | solution.py:534
  29.8 19.2 %collective-permute-start.5 = (bf16[272,768]{1,0:T(8,128)(2,1)S(1)}, bf16[272,768]{1,0:T(8,128)(2,1)S(1)}, u32[]{:S(2)}, u32[]{:S(2)}) collective-permute-start(bf16[272,768]{1,0:T(8,128)(2,1)S(1)} %get-tuple-element.9), channel_id=1, source_target_pairs={{3,4},{7,8},{11,12},{15,16},{19,20},{23,24},{27,28},{4,3},{8,7},{1... | collective-permute-start | bytes 1253384 | tf_op jit(solution)/shard_map/ppermute | solution.py:533
  32.3 17.7 %collective-permute-start.4 = (bf16[272,768]{1,0:T(8,128)(2,1)S(1)}, bf16[272,768]{1,0:T(8,128)(2,1)S(1)}, u32[]{:S(2)}, u32[]{:S(2)}) collective-permute-start(bf16[272,768]{1,0:T(8,128)(2,1)S(1)} %merge.1), channel_id=1, source_target_pairs={{0,1},{1,0},{2,3},{3,2},{4,5},{5,4},{6,7},{7,6},{8,9},{9,8},{10,11... | collective-permute-start | bytes 1253384 | tf_op jit(solution)/shard_map/ppermute | solution.py:535

commit v5 on v4

--- a/solution.py
+++ b/solution.py
@@ -207,8 +207,9 @@
     bounds[1, at, :] = jnp.broadcast_to(length, shape)
 
 
-def own_kernel(shift, message, corpus, out, *scratch):
+def own_kernel(first_doc, shift, message, corpus, out, *scratch):
     docs, arrived, rows_q, bounds = scratch[:4]
+    corpus = corpus.at[pl.ds(first_doc, docs.shape[0])]
     start_copies(corpus, docs, arrived)
     queries = message.shape[0] - META
     unit = identity(queries)
@@ -218,7 +219,7 @@
 
     def bound(k):
         value = columns[:, 2 * k : 2 * k + 1] * 256.0 + columns[:, 2 * k + 1 : 2 * k + 2]
-        return jnp.clip(value.astype(jnp.int32) - shift[0], 0, docs.shape[0])
+        return jnp.clip(value.astype(jnp.int32) - (shift[0] + first_doc), 0, docs.shape[0])
 
     for w in range(2):
         at = slice(w * queries, (w + 1) * queries)
@@ -242,166 +243,108 @@
         ).astype(BF16)
 
 
-def own(shift, message, corpus):
-    docs, width = corpus.shape
+def own(shift, message, corpus, first_doc, docs):
+    width = corpus.shape[1]
     queries = message.shape[0] - META
     tile = min(DOC_TILE, docs // 2)
     return pl.pallas_call(
-        own_kernel,
+        functools.partial(own_kernel, first_doc),
         out_shape=jax.ShapeDtypeStruct((2 * queries + META, width), BF16),
         in_specs=[SMEM, VMEM, HBM],
         out_specs=VMEM,
         scratch_shapes=row_scratch(2 * queries, 2 * queries, docs // tile, docs, width, tile),
         compiler_params=params(44),
         cost_estimate=pl.CostEstimate(
-            flops=8 * queries * docs * width,
-            bytes_accessed=docs * width * 2,
-            transcendentals=2 * queries * docs,
+            flops=8 * queries * docs * width if first_doc == 0 else 0,
+            bytes_accessed=docs * width * 2 if first_doc == 0 else 0,
+            transcendentals=0,
         ),
         name="own_block",
     )(shift, message, corpus)
 
 
-def neighbour_kernel(
-    shifts, near, far_a, far_b, corpus, near_out, far_out, both_q, pooled, spans, item_spans, items, span_done, *scratch
-):
+def side_kernel(shift, message, corpus, out, pooled, *scratch):
     docs, arrived, rows_q, bounds = scratch[:4]
     start_copies(corpus, docs, arrived)
-    queries = near.shape[0] - META
-    n_docs = docs.shape[0]
-    tiles = arrived.shape[0]
-    tile = n_docs // tiles
-    window = scratch[7].shape[0]
-    both_q[0:queries, :] = near[0:queries, :]
-    both_q[queries:, :] = far_a[0:queries, :] + far_b[0:queries, :]
-    metas = (near[queries:, 0:queries], far_a[queries:, 0:queries] + far_b[queries:, 0:queries])
-
-    lows, highs = [], []
-    for side, meta in enumerate(metas):
-        meta = meta.astype(F32)
-
-        def bound(k):
-            value = meta[2 * k : 2 * k + 1, :] * 256.0 + meta[2 * k + 1 : 2 * k + 2, :]
-            return jnp.clip(value.astype(jnp.int32) - shifts[side], 0, n_docs)
-
-        for w in range(2):
-            lows.append(bound(w))
-            highs.append(jnp.maximum(bound(2 + w), lows[-1]))
-    blocks = len(lows)
-    rows = blocks * queries
-
-    keys = [
-        jnp.where(high > low, jnp.where(low == 0, high, n_docs + low), 2 * n_docs)
-        for low, high in zip(lows, highs)
+    queries = message.shape[0] - META
+    group = rows_q.shape[0]
+    meta = message[queries:, 0:queries].astype(F32)
+
+    def bound(k):
+        value = meta[2 * k : 2 * k + 1, :] * 256.0 + meta[2 * k + 1 : 2 * k + 2, :]
+        return jnp.clip(value.astype(jnp.int32) - shift[0], 0, docs.shape[0])
+
+    lows = [bound(w) for w in range(2)]
+    lengths = [jnp.maximum(bound(2 + w) - low, 0) for w, low in enumerate(lows)]
+    parts = []
+    for low, length in zip(lows, lengths):
+        lines = [*split_int(low), *split_int(length), jnp.zeros((META - 4, queries), F32)]
+        parts.append(jnp.concatenate(lines, axis=0).astype(BF16))
+    flags = [(length > 0).astype(F32) for length in lengths]
+    stacked = jnp.concatenate(flags + [jnp.zeros((META - 2, queries), F32)], axis=0).astype(BF16)
+    before = lax.broadcasted_iota(jnp.int32, (queries, queries), 0) < lax.broadcasted_iota(
+        jnp.int32, (queries, queries), 1
+    )
+    ranks = jnp.dot(stacked, before.astype(F32).astype(BF16), preferred_element_type=F32)
+    held = jnp.sum(flags[0], axis=1, keepdims=True)
+    places = [
+        jnp.where(flag > 0, ranks[w : w + 1, :] + w * held, -1.0).astype(jnp.int32)
+        for w, flag in enumerate(flags)
     ]
-    parts = []
-    for low, high, key in zip(lows, highs, keys):
-        lines = [*split_int(low), *split_int(high - low), *split_int(key)]
-        parts.append(jnp.concatenate(lines + [jnp.zeros((META - 6, queries), F32)], axis=0).astype(BF16))
-    unit = identity(queries)
-    lane = lax.broadcasted_iota(jnp.int32, (1, queries), 1)
-    line = lax.broadcasted_iota(jnp.int32, (queries, 1), 0)
-    places = [jnp.zeros((1, queries), F32)] * blocks
-    ordered = [keys[b] * rows + (lane + b * queries) for b in range(blocks)]
-    for a in range(blocks):
-        columns = lax.dot_general(unit, parts[a], NT, preferred_element_type=F32)
-        key = (columns[:, 4:5] * 256.0 + columns[:, 5:6]).astype(jnp.int32)
-        key = jnp.broadcast_to(key * rows + (line + a * queries), (queries, queries))
-        for b in range(blocks):
-            places[b] = places[b] + jnp.sum((key < ordered[b]).astype(F32), axis=0, keepdims=True)
-    places = [place.astype(jnp.int32) for place in places]
-
-    begin = lax.broadcasted_iota(jnp.int32, (tiles, queries), 0) * tile
-    first = jnp.full((tiles, 1), rows, jnp.int32)
-    last = jnp.zeros((tiles, 1), jnp.int32)
-    for low, high, place in zip(lows, highs, places):
-        met = (high > low) & (low < begin + tile) & (high > begin)
-        first = jnp.minimum(first, jnp.min(jnp.where(met, place, rows), axis=1, keepdims=True))
-        last = jnp.maximum(last, jnp.max(jnp.where(met, place + 1, 0), axis=1, keepdims=True))
-    column = lax.broadcasted_iota(jnp.int32, (tiles, LANES), 1)
-    spans[...] = jnp.where(column == 0, first, last)
-    copy = pltpu.make_async_copy(spans, item_spans, span_done)
-    copy.start()
-
-    pick = []
-    for b in range(blocks):
-        row = lax.broadcasted_iota(jnp.int32, (rows, queries), 0)
-        pick.append((row == places[b]).astype(F32).astype(BF16))
-    of_query = jnp.concatenate([pick[0] + pick[1], pick[2] + pick[3]], axis=1)
-    rows_q[0:rows, :] = jnp.dot(of_query, both_q[...], preferred_element_type=F32).astype(BF16)
-    rows_q[rows:, :] = jnp.zeros((rows_q.shape[0] - rows, rows_q.shape[1]), BF16)
-    columns = jnp.zeros((rows, META), F32)
-    for chosen, part in zip(pick, parts):
-        columns = columns + lax.dot_general(chosen, part, NT, preferred_element_type=F32)
-    low = (columns[:, 0:1] * 256.0 + columns[:, 1:2]).astype(jnp.int32)
-    length = (columns[:, 2:3] * 256.0 + columns[:, 3:4]).astype(jnp.int32)
-    set_bounds(bounds, slice(0, rows), low, length)
-    none = jnp.zeros((bounds.shape[1] - rows, 1), jnp.int32)
-    set_bounds(bounds, slice(rows, bounds.shape[1]), none, none)
-
-    copy.wait()
-    count = jnp.int32(0)
-    for t in range(tiles):
-        head = jnp.minimum(item_spans[t, 0] // ROW_TILE * ROW_TILE, rows - ROW_TILE)
-        for k in range(-(-rows // window)):
-            items[0, count] = t
-            items[1, count] = head + k * window
-            items[2, count] = 1 if k == 0 else 0
-            more = True if k == 0 else head + k * window < item_spans[t, 1]
-            count = count + jnp.where(more, 1, 0)
-    items[0, count] = tiles - 1
-    items[1, count] = rows
-    items[2, count] = 0
-    count = (count + 1) // 2 * 2
-
-    def ready(i):
-        @pl.when(items[2, i] == 1)
-        def _():
-            tile_copy(corpus, docs, arrived, items[0, i]).wait()
-
-    stats = stats_matrix(attend_rows(scratch, count, lambda i: (items[0, i], items[1, i]), ready))[0:rows, :]
-    pooled[...] = scratch[-1][0:rows, :].astype(BF16)
-    for out in (near_out, far_out):
-        out[2 * queries :, :] = jnp.zeros((META, out.shape[1]), BF16)
-    for b, chosen in enumerate(pick):
-        out = (near_out, far_out)[b // 2]
-        at = slice((b % 2) * queries, (b % 2 + 1) * queries)
-        out[at, :] = lax.dot_general(chosen, pooled[...], TN, preferred_element_type=F32).astype(BF16)
-        out[2 * queries :, at] = lax.dot_general(
-            stats, chosen, TN, preferred_element_type=F32
+    active = jnp.sum(flags[0] + flags[1]).astype(jnp.int32)
+    out[...] = jnp.zeros(out.shape, BF16)
+
+    def work(g, carry):
+        row = lax.broadcasted_iota(jnp.int32, (group, queries), 0) + g * group
+        pick = [(row == place).astype(F32).astype(BF16) for place in places]
+        rows_q[...] = jnp.dot(
+            pick[0] + pick[1], message[0:queries, :], preferred_element_type=F32
         ).astype(BF16)
-
-
-def neighbours(shifts, near, far_a, far_b, corpus):
+        columns = sum(
+            lax.dot_general(chosen, part, NT, preferred_element_type=F32) for chosen, part in zip(pick, parts)
+        )
+        low = (columns[:, 0:1] * 256.0 + columns[:, 1:2]).astype(jnp.int32)
+        length = (columns[:, 2:3] * 256.0 + columns[:, 3:4]).astype(jnp.int32)
+        set_bounds(bounds, slice(0, group), low, length)
+
+        def ready(i):
+            @pl.when(g == 0)
+            def _():
+                tile_copy(corpus, docs, arrived, i).wait()
+
+        stats = stats_matrix(attend_rows(scratch, arrived.shape[0], lambda i: (i, 0), ready))
+        pooled[...] = scratch[-1][...].astype(BF16)
+        for w, chosen in enumerate(pick):
+            at = slice(w * queries, (w + 1) * queries)
+            out[at, :] += lax.dot_general(chosen, pooled[...], TN, preferred_element_type=F32).astype(BF16)
+            out[2 * queries :, at] += lax.dot_general(
+                stats, chosen, TN, preferred_element_type=F32
+            ).astype(BF16)
+        return carry
+
+    lax.fori_loop(0, jnp.maximum((active + group - 1) // group, 1), work, 0)
+
+
+def side(shift, message, corpus):
     docs, width = corpus.shape
-    queries = near.shape[0] - META
-    rows = 4 * queries
+    queries = message.shape[0] - META
     tile = min(DOC_TILE, docs // 2)
-    window = min(rows, (queries + 3 * queries // 8) // ROW_TILE * ROW_TILE)
-    most = docs // tile * -(-rows // window) + 2
-    result = jax.ShapeDtypeStruct((2 * queries + META, width), BF16)
+    group = min(2 * queries, (queries + queries // 4) // ROW_TILE * ROW_TILE)
     return pl.pallas_call(
-        neighbour_kernel,
-        out_shape=(result, result),
-        in_specs=[SMEM, VMEM, VMEM, VMEM, HBM],
-        out_specs=(VMEM, VMEM),
-        scratch_shapes=[
-            pltpu.VMEM((2 * queries, width), BF16),
-            pltpu.VMEM((rows, width), BF16),
-            pltpu.VMEM((docs // tile, LANES), jnp.int32),
-            pltpu.SMEM((docs // tile, LANES), jnp.int32),
-            pltpu.SMEM((3, most), jnp.int32),
-            pltpu.SemaphoreType.DMA,
-        ]
-        + row_scratch(rows + window, window, most, docs, width, tile),
+        side_kernel,
+        out_shape=jax.ShapeDtypeStruct((2 * queries + META, width), BF16),
+        in_specs=[SMEM, VMEM, HBM],
+        out_specs=VMEM,
+        scratch_shapes=[pltpu.VMEM((group, width), BF16)]
+        + row_scratch(group, group, docs // tile, docs, width, tile),
         compiler_params=params(44),
         cost_estimate=pl.CostEstimate(
-            flops=8 * queries * docs * width,
+            flops=5 * queries * docs * width,
             bytes_accessed=docs * width * 2,
-            transcendentals=2 * queries * docs,
+            transcendentals=queries * docs,
         ),
-        name="neighbour_blocks",
-    )(shifts, near, far_a, far_b, corpus)
+        name="side_block",
+    )(shift, message, corpus)
 
 
 def pack_kernel(base, queries, starts, ends, out):
@@ -472,10 +415,10 @@
     )(first, second)
 
 
-def finish_kernel(window_start, window_end, first, second, third, pooled, log_mass, mean_score):
+def finish_kernel(window_start, window_end, first, second, third, fourth_a, fourth_b, pooled, log_mass, mean_score):
     queries = window_start.shape[1]
     unit = identity(queries)
-    members = (first, second, third)
+    members = (first[...], second[...], third[...], fourth_a[...] + fourth_b[...])
     for w in range(2):
         at = slice(w * queries, (w + 1) * queries)
         states = [columns_of(member, unit, w) for member in members]
@@ -505,7 +448,7 @@
     return pl.pallas_call(
         finish_kernel,
         out_shape=(jax.ShapeDtypeStruct((queries, 2, width), BF16), line, line),
-        in_specs=[VMEM] * 5,
+        in_specs=[VMEM] * 7,
         out_specs=(VMEM, VMEM, VMEM),
         compiler_params=params(8),
         name="finish",
@@ -517,25 +460,32 @@
     size = lax.axis_size(AXES)
     position = lax.axis_index(AXES)
     across = [(i, i ^ 1) for i in range(size)]
+    past = [(i, i + 1) for i in range(1, size - 1, 2)] + [(i + 1, i) for i in range(1, size - 1, 2)]
     between = [(i, i + 1) for i in range(3, size - 1, 4)] + [(i + 1, i) for i in range(3, size - 1, 4)]
-    relay = [(i, i + 2) for i in range(0, size, 4)] + [(i + 3, i + 1) for i in range(0, size, 4)]
-    relay_back = [(target, source) for source, target in relay]
+    relay = [(i + 2, i) for i in range(0, size, 4)] + [(i + 1, i + 3) for i in range(0, size, 4)]
+    outward = [(i + 1, i) for i in range(0, size, 4)] + [(i + 2, i + 3) for i in range(0, size, 4)]
+    inward = [(target, source) for source, target in outward]
     odd = position % 2
 
     starts, ends = window_start.T, window_end.T
     base = jnp.full((1,), (position - 1) * docs, jnp.int32)
     message = pack(base, queries, starts, ends)
     near = lax.ppermute(message, AXES, across)
-    far_a = lax.ppermute(message, AXES, between)
-    far_b = lax.ppermute(near, AXES, relay)
-    shifts = jnp.stack([2 * docs * odd, 2 * docs * (1 - odd)]).astype(jnp.int32)
-    near_part, far_part = neighbours(shifts, near, far_a, far_b, corpus)
+    far = lax.ppermute(message, AXES, past)
+    shift = jnp.full((1,), docs, jnp.int32)
+    early = docs // 2
+    own_early = own(shift, message, corpus, 0, early)
+    near, _ = lax.optimization_barrier((near, own_early))
+    near_part = side(jnp.full((1,), 2 * docs * odd, jnp.int32), near, corpus)
+    near_back_a = lax.ppermute(near_part, AXES, outward)
+    far, _ = lax.optimization_barrier((far, near_part))
+    far_part = side(jnp.full((1,), 2 * docs * (1 - odd), jnp.int32), far, corpus)
     far_back = lax.ppermute(far_part, AXES, between)
-    relayed = lax.ppermute(far_part, AXES, relay_back)
-    near_back = lax.ppermute(merge(near_part, relayed), AXES, across)
-    message, _ = lax.optimization_barrier((message, far_part))
-    own_part = own(jnp.full((1,), docs, jnp.int32), message, corpus)
-    pooled, log_mass, mean_score = finish(starts, ends, own_part, near_back, far_back)
+    merged = merge(near_part, lax.ppermute(far_part, AXES, relay))
+    near_back_b = lax.ppermute(merged, AXES, inward)
+    message, _ = lax.optimization_barrier((message, merged))
+    own_late = own(shift, message, corpus, early, docs - early)
+    pooled, log_mass, mean_score = finish(starts, ends, own_early, own_late, far_back, near_back_a, near_back_b)
     return pooled, log_mass.T, mean_score.T
 
 

time: 52 us -> 63.6 us (1.22)
  Pallas kernels: 28.9 us -> 40 us
  starting transfers between devices: 11.6 us -> 14.3 us
  waiting for transfers between devices: 8.1 us -> 5.64 us
    pallas_call x2 -> x4, Pallas kernels: 25.9 us -> 36.7 us  [the longest x2 21.7 us: side(): pl.pallas_call(side_kernel, out_shape=jax.ShapeDtypeStruct((2 * queries +...]
    ppermute x4, starting transfers between devices: 8.83 us -> 12.3 us  [the longest x1 4.58 us: local(): near_back_a = lax.ppermute(near_part, AXES, outward)]
    ppermute x1, waiting for transfers between devices: 4.48 us -> 1.95 us  [local(): near = lax.ppermute(message, AXES, across)]
    ppermute x1, starting transfers between devices: 2.11 us -> 1.28 us  [local(): near = lax.ppermute(message, AXES, across)]
  transfers between devices with their start and end apart: 6 -> 6, of which waited for: 4 -> 2; matrix products, arithmetic and copies ran while one was open for 0% -> 0% of each run, Pallas kernels for 25% -> 43%
where the time goes in v5:
time: 63.6 us; the launch traced here: 62.9 us
  Pallas kernels  40 us (63%)
  starting transfers between devices  14.3 us (22%)
  waiting for transfers between devices  5.64 us (9%)
  local copies, waits for them, and re-layouts  2.29 us (4%)
  between operations  0.77 us (1%)
    pallas_call x2, Pallas kernels, side(): pl.pallas_call(side_kernel, out_shape=jax.ShapeDtypeStruct((2 * queries +...  21.7 us
    pallas_call x2, Pallas kernels, own(): pl.pallas_call(functools.partial(own_kernel, first_doc), out_shape=jax.Sh...  15 us
    ppermute x1, starting transfers between devices, local(): near_back_a = lax.ppermute(near_part, AXES, outward)  4.58 us
    ppermute x1, starting transfers between devices, local(): far = lax.ppermute(message, AXES, past)  4.51 us
    ppermute x1, waiting for transfers between devices, local(): near_back_a = lax.ppermute(near_part, AXES, outward)  3.67 us
    unnamed x10, local copies, waits for them, and re-layouts  2.29 us
    pallas_call x1, Pallas kernels, finish(): pl.pallas_call(finish_kernel, out_shape=(jax.ShapeDtypeStruct((queries, 2...  2.16 us
    ppermute x1, waiting for transfers between devices, local(): near = lax.ppermute(message, AXES, across)  1.95 us
  transfers between devices with their start and end apart: 6, of which 2 were waited for; matrix products, arithmetic and copies ran while one was open for 0% of the time, Pallas kernels for 43%

profile of v5, /device:TPU:1, one launch (start us, length us, event | category | flops | bytes accessed | tf_op | source)
XLA Modules:
  0.0 62.9 jit_solution(6243511716766466597)
XLA Ops:
  0.6 0.0 copy-start
  0.6 0.9 %copy-done = bf16[128,768]{1,0:T(8,128)(2,1)S(1)} copy-done((bf16[128,768]{1,0:T(8,128)(2,1)S(1)}, bf16[128,768]{1,0:T(8,128)(2,1)}, u32[]{:S(2)}) %copy-start) | copy-done | bytes 196632
  1.6 0.0 copy-start.1
  1.6 0.7 %copy-done.1 = s32[128,2]{0,1:T(2,128)S(1)} copy-done((s32[128,2]{0,1:T(2,128)S(1)}, s32[128,2]{0,1:T(2,128)}, u32[]{:S(2)}) %copy-start.1) | copy-done | bytes 1048
  2.2 0.0 copy-start.3
  2.2 0.7 %copy-done.3 = s32[128,2]{0,1:T(2,128)S(1)} copy-done((s32[128,2]{0,1:T(2,128)S(1)}, s32[128,2]{0,1:T(2,128)}, u32[]{:S(2)}) %copy-start.3) | copy-done | bytes 1048
  3.0 4.5 %collective-permute-start.1 = (bf16[144,768]{1,0:T(8,128)(2,1)S(1)}, bf16[144,768]{1,0:T(8,128)(2,1)S(1)}, u32[]{:S(2)}, u32[]{:S(2)}) collective-permute-start(bf16[144,768]{1,0:T(8,128)(2,1)S(1)} %pack.1.message), channel_id=1, source_target_pairs={{1,2},{3,4},{5,6},{7,8},{9,10},{11,12},{13,14},{15,16},{17,18},{19... | collective-permute-start | bytes 663560 | tf_op jit(solution)/shard_map/ppermute | solution.py:474
  7.5 1.3 %collective-permute-start = (bf16[144,768]{1,0:T(8,128)(2,1)S(1)}, bf16[144,768]{1,0:T(8,128)(2,1)S(1)}, u32[]{:S(2)}, u32[]{:S(2)}) collective-permute-start(bf16[144,768]{1,0:T(8,128)(2,1)S(1)} %pack.1.message), channel_id=1, source_target_pairs={{0,1},{1,0},{2,3},{3,2},{4,5},{5,4},{6,7},{7,6},{8,9},{9,8},{10,11... | collective-permute-start | bytes 663560 | tf_op jit(solution)/shard_map/ppermute | solution.py:473
  8.7 7.5 %own_block.2.first = bf16[272,768]{1,0:T(8,128)(2,1)S(1)} custom-call(s32[1]{0:T(128)} %constant.21.clone.1.shift, bf16[144,768]{1,0:T(8,128)(2,1)S(1)} %pack.1.message, bf16[8192,768]{1,0:T(8,128)(2,1)} %corpus.7), custom_call_target="tpu_custom_call" | custom-call | flops 3221225472 | bytes 6291456 | tf_op jit(solution)/shard_map/own_block/pallas_call | solution.py:250
  16.2 2.0 %collective-permute-done.message = bf16[144,768]{1,0:T(8,128)(2,1)S(1)} collective-permute-done((bf16[144,768]{1,0:T(8,128)(2,1)S(1)}, bf16[144,768]{1,0:T(8,128)(2,1)S(1)}, u32[]{:S(2)}, u32[]{:S(2)}) %collective-permute-start) | collective-permute-done | bytes 221216 | tf_op jit(solution)/shard_map/ppermute | solution.py:473
  18.2 10.8 %side_block.2.first = bf16[272,768]{1,0:T(8,128)(2,1)S(1)} custom-call(s32[1]{0:T(128)} %bitcast.3.shift, bf16[144,768]{1,0:T(8,128)(2,1)S(1)} %collective-permute-done.message, bf16[8192,768]{1,0:T(8,128)(2,1)} %corpus.7), custom_call_target="tpu_custom_call" | custom-call | flops 4026531840 | bytes 12582912 | tf_op jit(solution)/shard_map/side_block/pallas_call | solution.py:333
  29.0 0.0 collective-permute-done.1.message
  29.0 0.0 copy-start.2
  29.1 0.0 copy-start.4
  29.1 10.9 %side_block.3 = bf16[272,768]{1,0:T(8,128)(2,1)S(1)} custom-call(s32[1]{0:T(128)} %bitcast.4.shift, bf16[144,768]{1,0:T(8,128)(2,1)S(1)} %collective-permute-done.1.message, bf16[8192,768]{1,0:T(8,128)(2,1)} %corpus.7), custom_call_target="tpu_custom_call" | custom-call | flops 4026531840 | bytes 12582912 | tf_op jit(solution)/shard_map/side_block/pallas_call | solution.py:333
  39.9 1.7 %collective-permute-start.2 = (bf16[272,768]{1,0:T(8,128)(2,1)S(1)}, bf16[272,768]{1,0:T(8,128)(2,1)S(1)}, u32[]{:S(2)}, u32[]{:S(2)}) collective-permute-start(bf16[272,768]{1,0:T(8,128)(2,1)S(1)} %side_block.3), channel_id=1, source_target_pairs={{2,0},{6,4},{10,8},{14,12},{18,16},{22,20},{26,24},{30,28},{1,3},{... | collective-permute-start | bytes 1253384 | tf_op jit(solution)/shard_map/ppermute | solution.py:484
  41.7 0.7 %collective-permute-start.3 = (bf16[272,768]{1,0:T(8,128)(2,1)S(1)}, bf16[272,768]{1,0:T(8,128)(2,1)S(1)}, u32[]{:S(2)}, u32[]{:S(2)}) collective-permute-start(bf16[272,768]{1,0:T(8,128)(2,1)S(1)} %side_block.3), channel_id=1, source_target_pairs={{3,4},{7,8},{11,12},{15,16},{19,20},{23,24},{27,28},{4,3},{8,7},{1... | collective-permute-start | bytes 1253384 | tf_op jit(solution)/shard_map/ppermute | solution.py:483
  42.4 4.6 %collective-permute-start.4 = (bf16[272,768]{1,0:T(8,128)(2,1)S(1)}, bf16[272,768]{1,0:T(8,128)(2,1)S(1)}, u32[]{:S(2)}, u32[]{:S(2)}) collective-permute-start(bf16[272,768]{1,0:T(8,128)(2,1)S(1)} %side_block.2.first), channel_id=1, source_target_pairs={{1,0},{5,4},{9,8},{13,12},{17,16},{21,20},{25,24},{29,28},{2,3},{6... | collective-permute-start | bytes 1253384 | tf_op jit(solution)/shard_map/ppermute | solution.py:480
  47.0 0.0 collective-permute-done.2.second
  47.0 1.1 %merge.1 = bf16[272,768]{1,0:T(8,128)(2,1)S(1)} custom-call(bf16[272,768]{1,0:T(8,128)(2,1)S(1)} %side_block.2.first, bf16[272,768]{1,0:T(8,128)(2,1)S(1)} %collective-permute-done.2.second), custom_call_target="tpu_custom_call" | custom-call | tf_op jit(solution)/shard_map/merge/pallas_call | solution.py:408
  48.1 1.5 %collective-permute-start.5 = (bf16[272,768]{1,0:T(8,128)(2,1)S(1)}, bf16[272,768]{1,0:T(8,128)(2,1)S(1)}, u32[]{:S(2)}, u32[]{:S(2)}) collective-permute-start(bf16[272,768]{1,0:T(8,128)(2,1)S(1)} %merge.1), channel_id=1, source_target_pairs={{0,1},{4,5},{8,9},{12,13},{16,17},{20,21},{24,25},{28,29},{3,2},{7... | collective-permute-start | bytes 1253384 | tf_op jit(solution)/shard_map/ppermute | solution.py:485
  49.6 7.5 %own_block.3.second = bf16[272,768]{1,0:T(8,128)(2,1)S(1)} custom-call(s32[1]{0:T(128)} %constant.21.clone.1.shift, bf16[144,768]{1,0:T(8,128)(2,1)S(1)} %pack.1.message, bf16[8192,768]{1,0:T(8,128)(2,1)} %corpus.7), custom_call_target="tpu_custom_call" | custom-call | tf_op jit(solution)/shard_map/own_block/pallas_call | solution.py:250
  57.0 0.0 collective-permute-done.3.third
  57.1 3.7 %collective-permute-done.4.fourth_a = bf16[272,768]{1,0:T(8,128)(2,1)S(1)} collective-permute-done((bf16[272,768]{1,0:T(8,128)(2,1)S(1)}, bf16[272,768]{1,0:T(8,128)(2,1)S(1)}, u32[]{:S(2)}, u32[]{:S(2)}) %collective-permute-start.4) | collective-permute-done | bytes 417824 | tf_op jit(solution)/shard_map/ppermute | solution.py:480
  60.7 0.0 collective-permute-done.5.fourth_b
  60.7 0.0 copy-done.2
  60.7 0.0 copy-done.4
  60.7 2.2 %finish.1 = (bf16[128,2,768]{2,1,0:T(2,128)(2,1)}, f32[2,128]{1,0:T(2,128)}, f32[2,128]{1,0:T(2,128)}) custom-call(s32[2,128]{1,0:T(2,128)S(1)} %bitcast.8, s32[2,128]{1,0:T(2,128)S(1)} %bitcast.10, bf16[272,768]{1,0:T(8,128)(2,1)S(1)} %own_block.2.first, bf16[272,768]{1,0:T(8,128)(2,1)S(1)} %own_block.3.second, ...), custom_call_target="tpu_custom_call" | custom-call | tf_op jit(solution)/shard_map/finish/pallas_call | solution.py:448
  (1 shorter events, 0.0 us)
Async XLA Ops:
  0.6 0.9 %copy-start = (bf16[128,768]{1,0:T(8,128)(2,1)S(1)}, bf16[128,768]{1,0:T(8,128)(2,1)}, u32[]{:S(2)}) copy-start(bf16[128,768]{1,0:T(8,128)(2,1)} %queries.1) | copy-start | bytes 589828
  1.6 0.7 %copy-start.1 = (s32[128,2]{0,1:T(2,128)S(1)}, s32[128,2]{0,1:T(2,128)}, u32[]{:S(2)}) copy-start(s32[128,2]{0,1:T(2,128)} %param.6) | copy-start | bytes 3076
  2.2 0.7 %copy-start.3 = (s32[128,2]{0,1:T(2,128)S(1)}, s32[128,2]{0,1:T(2,128)}, u32[]{:S(2)}) copy-start(s32[128,2]{0,1:T(2,128)} %param.7) | copy-start | bytes 3076
  3.0 26.1 %collective-permute-start.1 = (bf16[144,768]{1,0:T(8,128)(2,1)S(1)}, bf16[144,768]{1,0:T(8,128)(2,1)S(1)}, u32[]{:S(2)}, u32[]{:S(2)}) collective-permute-start(bf16[144,768]{1,0:T(8,128)(2,1)S(1)} %pack.1.message), channel_id=1, source_target_pairs={{1,2},{3,4},{5,6},{7,8},{9,10},{11,12},{13,14},{15,16},{17,18},{19... | collective-permute-start | bytes 663560 | tf_op jit(solution)/shard_map/ppermute | solution.py:474
  7.5 10.7 %collective-permute-start = (bf16[144,768]{1,0:T(8,128)(2,1)S(1)}, bf16[144,768]{1,0:T(8,128)(2,1)S(1)}, u32[]{:S(2)}, u32[]{:S(2)}) collective-permute-start(bf16[144,768]{1,0:T(8,128)(2,1)S(1)} %pack.1.message), channel_id=1, source_target_pairs={{0,1},{1,0},{2,3},{3,2},{4,5},{5,4},{6,7},{7,6},{8,9},{9,8},{10,11... | collective-permute-start | bytes 663560 | tf_op jit(solution)/shard_map/ppermute | solution.py:473
  29.0 31.7 %copy-start.2 = (s32[128,2]{0,1:T(2,128)S(1)}, s32[128,2]{0,1:T(2,128)}, u32[]{:S(2)}) copy-start(s32[128,2]{0,1:T(2,128)} %param.6) | copy-start | bytes 3076
  29.1 31.7 %copy-start.4 = (s32[128,2]{0,1:T(2,128)S(1)}, s32[128,2]{0,1:T(2,128)}, u32[]{:S(2)}) copy-start(s32[128,2]{0,1:T(2,128)} %param.7) | copy-start | bytes 3076
  39.9 7.0 %collective-permute-start.2 = (bf16[272,768]{1,0:T(8,128)(2,1)S(1)}, bf16[272,768]{1,0:T(8,128)(2,1)S(1)}, u32[]{:S(2)}, u32[]{:S(2)}) collective-permute-start(bf16[272,768]{1,0:T(8,128)(2,1)S(1)} %side_block.3), channel_id=1, source_target_pairs={{2,0},{6,4},{10,8},{14,12},{18,16},{22,20},{26,24},{30,28},{1,3},{... | collective-permute-start | bytes 1253384 | tf_op jit(solution)/shard_map/ppermute | solution.py:484
  41.7 15.4 %collective-permute-start.3 = (bf16[272,768]{1,0:T(8,128)(2,1)S(1)}, bf16[272,768]{1,0:T(8,128)(2,1)S(1)}, u32[]{:S(2)}, u32[]{:S(2)}) collective-permute-start(bf16[272,768]{1,0:T(8,128)(2,1)S(1)} %side_block.3), channel_id=1, source_target_pairs={{3,4},{7,8},{11,12},{15,16},{19,20},{23,24},{27,28},{4,3},{8,7},{1... | collective-permute-start | bytes 1253384 | tf_op jit(solution)/shard_map/ppermute | solution.py:483
  42.4 18.4 %collective-permute-start.4 = (bf16[272,768]{1,0:T(8,128)(2,1)S(1)}, bf16[272,768]{1,0:T(8,128)(2,1)S(1)}, u32[]{:S(2)}, u32[]{:S(2)}) collective-permute-start(bf16[272,768]{1,0:T(8,128)(2,1)S(1)} %side_block.2.first), channel_id=1, source_target_pairs={{1,0},{5,4},{9,8},{13,12},{17,16},{21,20},{25,24},{29,28},{2,3},{6... | collective-permute-start | bytes 1253384 | tf_op jit(solution)/shard_map/ppermute | solution.py:480
  48.1 12.6 %collective-permute-start.5 = (bf16[272,768]{1,0:T(8,128)(2,1)S(1)}, bf16[272,768]{1,0:T(8,128)(2,1)S(1)}, u32[]{:S(2)}, u32[]{:S(2)}) collective-permute-start(bf16[272,768]{1,0:T(8,128)(2,1)S(1)} %merge.1), channel_id=1, source_target_pairs={{0,1},{4,5},{8,9},{12,13},{16,17},{20,21},{24,25},{28,29},{3,2},{7... | collective-permute-start | bytes 1253384 | tf_op jit(solution)/shard_map/ppermute | solution.py:485

commit v6 on v3

v6 whole, which is shorter than its diff:
```python
import functools
import math

import jax
import jax.numpy as jnp
from jax import lax
from jax.experimental import pallas as pl
from jax.experimental.pallas import tpu as pltpu
from jax.sharding import PartitionSpec as P

SCORE_SCALE = 3.0
NEG = -1e30
LOG2E = math.log2(math.e)
AXES = ("tm", "pb")
BF16 = jnp.bfloat16
F32 = jnp.float32
NT = (((1,), (1,)), ((), ()))
TN = (((0,), (0,)), ((), ()))
META = 16
LANES = 128
DOC_TILE = 1024
SUBLANES = 8
CHUNK = 32

VMEM = pl.BlockSpec(memory_space=pltpu.VMEM)
SMEM = pl.BlockSpec(memory_space=pltpu.SMEM)
HBM = pl.BlockSpec(memory_space=pltpu.HBM)


def params(mebibytes):
    return pltpu.CompilerParams(vmem_limit_bytes=mebibytes * 2**20)


def identity(n):
    rows = lax.broadcasted_iota(jnp.int32, (n, n), 0)
    return (rows == lax.broadcasted_iota(jnp.int32, (n, n), 1)).astype(BF16)


def split_int(value):
    return (value >> 8).astype(F32), (value & 255).astype(F32)


def split_float(value):
    high = value.astype(BF16).astype(F32)
    rest = value - high
    middle = rest.astype(BF16).astype(F32)
    return high, middle, rest - middle


def row_scratch(rows, docs, width, tile):
    groups = rows // LANES
    return [
        pltpu.VMEM((docs, width), BF16),
        pltpu.SemaphoreType.DMA((docs // tile,)),
        pltpu.VMEM((rows, width), BF16),
        pltpu.VMEM((groups, SUBLANES, LANES), jnp.int32),
        pltpu.VMEM((groups, SUBLANES, LANES), jnp.int32),
        pltpu.VMEM((groups, SUBLANES, LANES), F32),
        pltpu.VMEM((groups, SUBLANES, LANES), F32),
        pltpu.VMEM((groups, SUBLANES, LANES), F32),
        pltpu.VMEM((tile, 2 * LANES), F32),
        pltpu.VMEM((tile, 2 * LANES), F32),
        pltpu.VMEM((docs, 2 * LANES), F32),
        pltpu.VMEM((tile, 2 * LANES), BF16),
        pltpu.VMEM((tile, 2 * LANES), BF16),
        pltpu.VMEM((rows, width), F32),
    ]


def tile_copy(corpus, docs, arrived, t):
    tile = docs.shape[0] // arrived.shape[0]
    at = pl.ds(t * tile, tile)
    return pltpu.make_async_copy(corpus.at[at], docs.at[at], arrived.at[t])


def start_copies(corpus, docs, arrived):
    for t in range(arrived.shape[0]):
        tile_copy(corpus, docs, arrived, t).start()


def fold(values, op):
    return op(values.reshape(values.shape[0] // SUBLANES, SUBLANES, values.shape[1]), axis=0)


def set_bounds(scratch, low, length):
    lows, lengths = scratch[3:5]
    for g in range(lows.shape[0]):
        at = slice(g * LANES, (g + 1) * LANES)
        lows[g] = jnp.broadcast_to(low[:, at], (SUBLANES, LANES))
        lengths[g] = jnp.broadcast_to(length[:, at], (SUBLANES, LANES))


def attend_rows(scratch, corpus, step):
    docs, arrived, rows_q, lows, lengths, peak, score_sum, mass, s_a, s_b, masked, p_a, p_b, acc = scratch
    n_docs, width = docs.shape
    tile = s_a.shape[0]
    tiles = n_docs // tile
    scale = SCORE_SCALE / math.sqrt(width)

    def first_group(t):
        if isinstance(t, int):
            return step if t >= tiles // 2 else 0
        return jnp.where(t >= tiles // 2, step, 0)

    def met_rows(t):
        first = first_group(t)
        if isinstance(first, int):
            return slice(first * LANES, (first + 2) * LANES)
        return pl.ds(pl.multiple_of(first * LANES, LANES), 2 * LANES)

    def wide(ref, g):
        return jnp.broadcast_to(ref[g][0:1, :], (CHUNK, LANES))

    def score(t):
        tile_copy(corpus, docs, arrived, t).wait()
        (s_a, s_b)[t % 2][...] = lax.dot_general(
            docs[t * tile : (t + 1) * tile, :], rows_q[met_rows(t), :], NT, preferred_element_type=F32
        )

    def scan(t):
        scores = (s_a, s_b)[t % 2]
        down = lax.broadcasted_iota(jnp.int32, (CHUNK, LANES), 0)
        for side in range(2):
            g = first_group(t) + side
            at = slice(side * LANES, (side + 1) * LANES)
            offset = down - wide(lows, g)
            length = wide(lengths, g).astype(jnp.uint32)
            top, total = peak[g], score_sum[g]
            for c in range(0, tile, CHUNK):
                value = scores[c : c + CHUNK, at]
                inside = (offset + (t * tile + c)).astype(jnp.uint32) < length
                kept = jnp.where(inside, value, NEG)
                top = jnp.maximum(top, fold(kept, jnp.max))
                total = total + fold(jnp.where(inside, value, 0.0), jnp.sum)
                masked[t * tile + c : t * tile + c + CHUNK, at] = kept
            peak[g] = top
            score_sum[g] = total

    peak[...] = jnp.full(peak.shape, NEG, F32)
    score_sum[...] = jnp.zeros(score_sum.shape, F32)
    mass[...] = jnp.zeros(mass.shape, F32)
    acc[...] = jnp.zeros(acc.shape, F32)
    score(0)
    for t in range(tiles):
        if t + 1 < tiles:
            score(t + 1)
        scan(t)
    groups = range(peak.shape[0])
    tops = [jnp.max(peak[g], axis=0, keepdims=True) for g in groups]
    for g in groups:
        peak[g] = jnp.broadcast_to(jnp.maximum(tops[g], 0.5 * NEG), (SUBLANES, LANES))

    def weigh(t, out):
        for side in range(2):
            g = first_group(t) + side
            at = slice(side * LANES, (side + 1) * LANES)
            shift, total = wide(peak, g), mass[g]
            for c in range(0, tile, CHUNK):
                value = masked[pl.ds(pl.multiple_of(t * tile + c, CHUNK), CHUNK), at]
                p = jnp.exp2((value - shift) * (scale * LOG2E))
                total = total + fold(p, jnp.sum)
                out[c : c + CHUNK, at] = p.astype(BF16)
            mass[g] = total

    def pool(t, weights):
        block = docs[pl.ds(pl.multiple_of(t * tile, tile), tile), :]
        acc[met_rows(t), :] += lax.dot_general(weights[...], block, TN, preferred_element_type=F32)

    weigh(0, p_a)

    def second_step(k, carry):
        t = 2 * k + 1
        pool(t - 1, p_a)
        weigh(t, p_b)
        pool(t, p_b)
        weigh(t + 1, p_a)
        return carry

    lax.fori_loop(0, tiles // 2 - 1, second_step, 0)
    pool(tiles - 2, p_a)
    weigh(tiles - 1, p_b)
    pool(tiles - 1, p_b)

    def line(parts):
        return jnp.concatenate(parts, axis=1)

    return (
        line(tops) * scale,
        line([jnp.sum(mass[g], axis=0, keepdims=True) for g in groups]),
        line([jnp.sum(score_sum[g], axis=0, keepdims=True) for g in groups]) * scale,
    )


def stats_lines(stats):
    lines = [part for value in stats for part in split_float(value)]
    lines.append(jnp.zeros((META - len(lines), stats[0].shape[1]), F32))
    return jnp.concatenate(lines, axis=0).astype(BF16)


def bound_lines(meta, shift, n_docs):
    meta = meta.astype(F32)

    def bound(k):
        value = meta[2 * k : 2 * k + 1, :] * 256.0 + meta[2 * k + 1 : 2 * k + 2, :]
        return jnp.clip(value.astype(jnp.int32) - shift, 0, n_docs)

    lows = [bound(w) for w in range(2)]
    return lows, [jnp.maximum(bound(2 + w) - low, 0) for w, low in enumerate(lows)]


def own_kernel(shift, message, corpus, out, *scratch):
    docs, arrived, rows_q = scratch[:3]
    start_copies(corpus, docs, arrived)
    queries = message.shape[0] - META
    lows, lengths = bound_lines(message[queries:, 0:queries], shift[0], docs.shape[0])
    set_bounds(scratch, jnp.concatenate(lows, axis=1), jnp.concatenate(lengths, axis=1))
    for w in range(2):
        rows_q[w * queries : (w + 1) * queries, :] = message[0:queries, :]
    stats = attend_rows(scratch, corpus, 0)
    out[0 : 2 * queries, :] = scratch[-1][...].astype(BF16)
    out[2 * queries :, :] = jnp.zeros((META, out.shape[1]), BF16)
    out[2 * queries :, 0 : 2 * queries] = stats_lines(stats)


def own(shift, message, corpus):
    docs, width = corpus.shape
    queries = message.shape[0] - META
    tile = min(DOC_TILE, docs // 2)
    return pl.pallas_call(
        own_kernel,
        out_shape=jax.ShapeDtypeStruct((2 * queries + META, width), BF16),
        in_specs=[SMEM, VMEM, HBM],
        out_specs=VMEM,
        scratch_shapes=row_scratch(2 * queries, docs, width, tile),
        compiler_params=params(44),
        cost_estimate=pl.CostEstimate(
            flops=8 * queries * docs * width,
            bytes_accessed=docs * width * 2,
            transcendentals=2 * queries * docs,
        ),
        name="own_block",
    )(shift, message, corpus)


def neighbour_kernel(shifts, near, far_a, far_b, corpus, near_out, far_out, both_q, pooled, *scratch):
    docs, arrived, rows_q = scratch[:3]
    start_copies(corpus, docs, arrived)
    queries = near.shape[0] - META
    n_docs = docs.shape[0]
    held = rows_q.shape[0]
    centre = held // 2
    both_q[0:queries, :] = near[0:queries, :]
    both_q[queries:, :] = far_a[0:queries, :] + far_b[0:queries, :]
    metas = (near[queries:, 0:queries], far_a[queries:, 0:queries] + far_b[queries:, 0:queries])
    lows, lengths = [], []
    for side, meta in enumerate(metas):
        low, length = bound_lines(meta, shifts[side], n_docs)
        lows += low
        lengths += length
    blocks = len(lows)
    rows = blocks * queries

    keys = [
        jnp.where(length > 0, jnp.where(low == 0, length, n_docs + low), 2 * n_docs)
        for low, length in zip(lows, lengths)
    ]
    parts = []
    for low, length, key in zip(lows, lengths, keys):
        lines = [*split_int(low), *split_int(length), *split_int(key), jnp.zeros((META - 6, queries), F32)]
        parts.append(jnp.concatenate(lines, axis=0).astype(BF16))
    unit = identity(queries)
    lane = lax.broadcasted_iota(jnp.int32, (1, queries), 1)
    line = lax.broadcasted_iota(jnp.int32, (queries, 1), 0)
    ordered = [keys[b] * rows + (lane + b * queries) for b in range(blocks)]
    ranks = [jnp.zeros((1, queries), F32)] * blocks
    for a in range(blocks):
        columns = lax.dot_general(unit, parts[a], NT, preferred_element_type=F32)
        key = (columns[:, 4:5] * 256.0 + columns[:, 5:6]).astype(jnp.int32)
        key = jnp.broadcast_to(key * rows + (line + a * queries), (queries, queries))
        for b in range(blocks):
            ranks[b] = ranks[b] + jnp.sum((key < ordered[b]).astype(F32), axis=0, keepdims=True)
    opened = jnp.zeros((1, 1), F32)
    for low, length in zip(lows, lengths):
        opened = opened + jnp.sum(((length > 0) & (low == 0)).astype(F32), axis=1, keepdims=True)
    places, misfits = [], jnp.zeros((1, 1), F32)
    half = n_docs // 2
    for low, length, rank in zip(lows, lengths, ranks):
        place = (rank + (centre - opened)).astype(jnp.int32)
        bad = (place < 0) | (place >= held)
        bad = bad | ((place < LANES) & (low + length > half)) | ((place >= 2 * LANES) & (low < half))
        misfits = misfits + jnp.sum(((length > 0) & bad).astype(F32), axis=1, keepdims=True)
        places.append(jnp.where(length > 0, place, -1))
    fits = jnp.max(misfits) == 0.0
    passes = jnp.where(fits, 1, 2)
    step = jnp.where(fits, held // LANES - 2, 0)

    near_out[...] = jnp.zeros(near_out.shape, BF16)
    far_out[...] = jnp.zeros(far_out.shape, BF16)

    def work(turn, carry):
        row = lax.broadcasted_iota(jnp.int32, (held, queries), 0)
        pick = []
        for b in range(blocks):
            plain = jnp.where(turn == b // 2, lane + (b % 2) * queries, -1)
            place = jnp.where(fits, places[b], plain)
            pick.append((row == place).astype(F32).astype(BF16))
        of_query = jnp.concatenate([pick[0] + pick[1], pick[2] + pick[3]], axis=1)
        rows_q[...] = jnp.dot(of_query, both_q[...], preferred_element_type=F32).astype(BF16)
        lines = sum(
            lax.dot_general(part, chosen, NT, preferred_element_type=F32) for part, chosen in zip(parts, pick)
        )
        set_bounds(
            scratch,
            (lines[0:1, :] * 256.0 + lines[1:2, :]).astype(jnp.int32),
            (lines[2:3, :] * 256.0 + lines[3:4, :]).astype(jnp.int32),
        )
        stats = stats_lines(attend_rows(scratch, corpus, step))
        pooled[...] = scratch[-1][...].astype(BF16)
        for b, chosen in enumerate(pick):
            out = (near_out, far_out)[b // 2]
            at = slice((b % 2) * queries, (b % 2 + 1) * queries)
            out[at, :] += lax.dot_general(chosen, pooled[...], TN, preferred_element_type=F32).astype(BF16)
            out[2 * queries :, at] += jnp.dot(stats, chosen, preferred_element_type=F32).astype(BF16)

        @pl.when(turn + 1 < passes)
        def _():
            start_copies(corpus, docs, arrived)

        return carry

    lax.fori_loop(0, passes, work, 0)


def neighbours(shifts, near, far_a, far_b, corpus):
    docs, width = corpus.shape
    queries = near.shape[0] - META
    held = 3 * LANES
    tile = min(DOC_TILE, docs // 2)
    result = jax.ShapeDtypeStruct((2 * queries + META, width), BF16)
    return pl.pallas_call(
        neighbour_kernel,
        out_shape=(result, result),
        in_specs=[SMEM, VMEM, VMEM, VMEM, HBM],
        out_specs=(VMEM, VMEM),
        scratch_shapes=[pltpu.VMEM((2 * queries, width), BF16), pltpu.VMEM((held, width), BF16)]
        + row_scratch(held, docs, width, tile),
        compiler_params=params(44),
        cost_estimate=pl.CostEstimate(
            flops=8 * queries * docs * width,
            bytes_accessed=docs * width * 2,
            transcendentals=2 * queries * docs,
        ),
        name="neighbour_blocks",
    )(shifts, near, far_a, far_b, corpus)


def pack_kernel(base, queries, starts, ends, out):
    rows, width = queries.shape
    out[0:rows, :] = queries[...]
    out[rows:, :] = jnp.zeros((META, width), BF16)
    parts = [split_int(lines[...] - base[0]) for lines in (starts, ends)]
    lines = [part[w : w + 1, :] for pair in parts for w in range(2) for part in pair]
    lines.append(jnp.zeros((META - 8, rows), F32))
    out[rows:, 0:rows] = jnp.concatenate(lines, axis=0).astype(BF16)


def pack(base, queries, starts, ends):
    rows, width = queries.shape
    return pl.pallas_call(
        pack_kernel,
        out_shape=jax.ShapeDtypeStruct((rows + META, width), BF16),
        in_specs=[SMEM, VMEM, VMEM, VMEM],
        out_specs=VMEM,
        compiler_params=params(4),
        name="pack",
    )(base, queries, starts, ends)


def columns_of(state, unit, w):
    queries = unit.shape[0]
    lines = state[2 * queries :, w * queries : (w + 1) * queries]
    columns = lax.dot_general(unit, lines, NT, preferred_element_type=F32)
    top, total, score_sum = (
        columns[:, 3 * k : 3 * k + 1] + columns[:, 3 * k + 1 : 3 * k + 2] + columns[:, 3 * k + 2 : 3 * k + 3]
        for k in range(3)
    )
    return jnp.where(total > 0, top, NEG), total, score_sum


def weigh_states(tops):
    best = functools.reduce(jnp.maximum, tops)
    return best, [jnp.exp(top - best) for top in tops]


def stats_matrix(stats):
    rows = stats[0].shape[0]
    lane = lax.broadcasted_iota(jnp.int32, (rows, META), 1)
    matrix = jnp.zeros((rows, META), F32)
    for k, value in enumerate(stats):
        for j, part in enumerate(split_float(value)):
            matrix = jnp.where(lane == 3 * k + j, part, matrix)
    return matrix.astype(BF16)


def merge_kernel(first, second, out):
    queries = (first.shape[0] - META) // 2
    unit = identity(queries)
    out[2 * queries :, :] = jnp.zeros((META, out.shape[1]), BF16)
    for w in range(2):
        at = slice(w * queries, (w + 1) * queries)
        states = [columns_of(state, unit, w) for state in (first, second)]
        best, factors = weigh_states([state[0] for state in states])
        total = functools.reduce(jnp.add, [f * state[1] for f, state in zip(factors, states)])
        score_sum = states[0][2] + states[1][2]
        out[at, :] = (
            factors[0] * first[at, :].astype(F32) + factors[1] * second[at, :].astype(F32)
        ).astype(BF16)
        stats = stats_matrix((best, total, score_sum))
        out[2 * queries :, at] = lax.dot_general(
            stats, unit, TN, preferred_element_type=F32
        ).astype(BF16)


def merge(first, second):
    return pl.pallas_call(
        merge_kernel,
        out_shape=jax.ShapeDtypeStruct(first.shape, BF16),
        in_specs=[VMEM, VMEM],
        out_specs=VMEM,
        compiler_params=params(8),
        name="merge",
    )(first, second)


def finish_kernel(window_start, window_end, first, second, third, pooled, log_mass, mean_score):
    queries = window_start.shape[1]
    unit = identity(queries)
    members = (first, second, third)
    for w in range(2):
        at = slice(w * queries, (w + 1) * queries)
        states = [columns_of(member, unit, w) for member in members]
        _, factors = weigh_states([state[0] for state in states])
        total = functools.reduce(jnp.add, [f * state[1] for f, state in zip(factors, states)])
        weighted = functools.reduce(
            jnp.add, [f * member[at, :].astype(F32) for f, member in zip(factors, members)]
        )
        pooled[:, w, :] = (weighted / total).astype(BF16)

        lines = [member[2 * queries :, at].astype(F32) for member in members]
        tops, totals, sums = (
            [line[3 * k : 3 * k + 1, :] + line[3 * k + 1 : 3 * k + 2, :] + line[3 * k + 2 : 3 * k + 3, :] for line in lines]
            for k in range(3)
        )
        best, factors = weigh_states([jnp.where(t > 0, top, NEG) for top, t in zip(tops, totals)])
        total = functools.reduce(jnp.add, [f * t for f, t in zip(factors, totals)])
        log_mass[w : w + 1, :] = best + jnp.log(total)
        count = (window_end[w : w + 1, :] - window_start[w : w + 1, :]).astype(F32)
        mean_score[w : w + 1, :] = functools.reduce(jnp.add, sums) / count


def finish(window_start, window_end, *members):
    queries = window_start.shape[1]
    width = members[0].shape[1]
    line = jax.ShapeDtypeStruct((2, queries), F32)
    return pl.pallas_call(
        finish_kernel,
        out_shape=(jax.ShapeDtypeStruct((queries, 2, width), BF16), line, line),
        in_specs=[VMEM] * 5,
        out_specs=(VMEM, VMEM, VMEM),
        compiler_params=params(8),
        name="finish",
    )(window_start, window_end, *members)


def local(queries, corpus, window_start, window_end):
    docs = corpus.shape[0]
    size = lax.axis_size(AXES)
    position = lax.axis_index(AXES)
    across = [(i, i ^ 1) for i in range(size)]
    between = [(i, i + 1) for i in range(3, size - 1, 4)] + [(i + 1, i) for i in range(3, size - 1, 4)]
    relay = [(i, i + 2) for i in range(0, size, 4)] + [(i + 3, i + 1) for i in range(0, size, 4)]
    relay_back = [(target, source) for source, target in relay]
    odd = position % 2

    starts, ends = window_start.T, window_end.T
    base = jnp.full((1,), (position - 1) * docs, jnp.int32)
    message = pack(base, queries, starts, ends)
    near = lax.ppermute(message, AXES, across)
    far_a = lax.ppermute(message, AXES, between)
    far_b = lax.ppermute(near, AXES, relay)
    shifts = jnp.stack([2 * docs * odd, 2 * docs * (1 - odd)]).astype(jnp.int32)
    near_part, far_part = neighbours(shifts, near, far_a, far_b, corpus)
    far_back = lax.ppermute(far_part, AXES, between)
    relayed = lax.ppermute(far_part, AXES, relay_back)
    near_back = lax.ppermute(merge(near_part, relayed), AXES, across)
    message, _ = lax.optimization_barrier((message, far_part))
    own_part = own(jnp.full((1,), docs, jnp.int32), message, corpus)
    pooled, log_mass, mean_score = finish(starts, ends, own_part, near_back, far_back)
    return pooled, log_mass.T, mean_score.T


def solution(mesh):
    placed = P(AXES, None)
    return jax.shard_map(
        local,
        mesh=mesh,
        in_specs=(placed,) * 4,
        out_specs=(P(AXES, None, None), placed, placed),
        check_vma=False,
    )
```

time: 61.2 us -> 56.5 us (0.923)
  local copies, waits for them, and re-layouts: 11.4 us -> 2.29 us
  Pallas kernels: 31.8 us -> 33.9 us
  waiting for transfers between devices: 5.49 us -> 7.04 us
  starting transfers between devices: 10.6 us -> 11.8 us
    unnamed x16 -> x10, local copies, waits for them, and re-layouts: 11.4 us -> 2.29 us
    pallas_call x1 -> x0, Pallas kernels: 4.7 us -> none  [load(): pl.pallas_call(load_kernel, out_shape=jax.ShapeDtypeStruct(corpus.shape,...]
    ppermute x1, waiting for transfers between devices: 0.01 us -> 4.48 us  [local(): near = lax.ppermute(message, AXES, across)]
    pallas_call x1, Pallas kernels: 10.5 us -> 14.5 us  [own(): pl.pallas_call(own_kernel, out_shape=jax.ShapeDtypeStruct((2 * queries +...]
    ppermute x1, waiting for transfers between devices: 2.85 us -> 0.01 us  [local(): near_back = lax.ppermute(merge(near_part, relayed), AXES, across)]
    pallas_call x1, Pallas kernels: 13.6 us -> 16.5 us  [neighbours(): pl.pallas_call(neighbour_kernel, out_shape=(result, result), in_specs=[SM...]
    ppermute x1, starting transfers between devices: 3.75 us -> 4.82 us  [local(): near_back = lax.ppermute(merge(near_part, relayed), AXES, across)]
  transfers between devices with their start and end apart: 6 -> 6, of which waited for: 3 -> 3; matrix products, arithmetic and copies ran while one was open for 0% -> 0% of each run, Pallas kernels for 27% -> 28%
where the time goes in v6:
time: 56.5 us; the launch traced here: 55.9 us
  Pallas kernels  33.9 us (60%)
  starting transfers between devices  11.8 us (21%)
  waiting for transfers between devices  7.04 us (12%)
  local copies, waits for them, and re-layouts  2.29 us (4%)
  between operations  0.76 us (1%)
    pallas_call x1, Pallas kernels, neighbours(): pl.pallas_call(neighbour_kernel, out_shape=(result, result), in_specs=[SM...  16.5 us
    pallas_call x1, Pallas kernels, own(): pl.pallas_call(own_kernel, out_shape=jax.ShapeDtypeStruct((2 * queries +...  14.5 us
    ppermute x1, starting transfers between devices, local(): near_back = lax.ppermute(merge(near_part, relayed), AXES, across)  4.82 us
    ppermute x1, waiting for transfers between devices, local(): near = lax.ppermute(message, AXES, across)  4.48 us
    unnamed x10, local copies, waits for them, and re-layouts  2.29 us
    ppermute x1, starting transfers between devices, local(): near = lax.ppermute(message, AXES, across)  2.11 us
    ppermute x1, waiting for transfers between devices, local(): far_b = lax.ppermute(near, AXES, relay)  2.09 us
    ppermute x1, starting transfers between devices, local(): relayed = lax.ppermute(far_part, AXES, relay_back)  2.06 us
  transfers between devices with their start and end apart: 6, of which 3 were waited for; matrix products, arithmetic and copies ran while one was open for 0% of the time, Pallas kernels for 28%

profile of v6, /device:TPU:1, one launch (start us, length us, event | category | flops | bytes accessed | tf_op | source)
XLA Modules:
  0.0 55.9 jit_solution(13633131898342017874)
XLA Ops:
  0.6 0.0 copy-start
  0.6 0.9 %copy-done = bf16[128,768]{1,0:T(8,128)(2,1)S(1)} copy-done((bf16[128,768]{1,0:T(8,128)(2,1)S(1)}, bf16[128,768]{1,0:T(8,128)(2,1)}, u32[]{:S(2)}) %copy-start) | copy-done | bytes 196632
  1.6 0.0 copy-start.1
  1.6 0.7 %copy-done.1 = s32[128,2]{0,1:T(2,128)S(1)} copy-done((s32[128,2]{0,1:T(2,128)S(1)}, s32[128,2]{0,1:T(2,128)}, u32[]{:S(2)}) %copy-start.1) | copy-done | bytes 1048
  2.2 0.0 copy-start.3
  2.2 0.7 %copy-done.3 = s32[128,2]{0,1:T(2,128)S(1)} copy-done((s32[128,2]{0,1:T(2,128)S(1)}, s32[128,2]{0,1:T(2,128)}, u32[]{:S(2)}) %copy-start.3) | copy-done | bytes 1048
  3.0 2.1 %collective-permute-start = (bf16[144,768]{1,0:T(8,128)(2,1)S(1)}, bf16[144,768]{1,0:T(8,128)(2,1)S(1)}, u32[]{:S(2)}, u32[]{:S(2)}) collective-permute-start(bf16[144,768]{1,0:T(8,128)(2,1)S(1)} %pack.1.message), channel_id=1, source_target_pairs={{0,1},{1,0},{2,3},{3,2},{4,5},{5,4},{6,7},{7,6},{8,9},{9,8},{10,11... | collective-permute-start | bytes 663560 | tf_op jit(solution)/shard_map/ppermute | solution.py:488
  5.1 0.7 %collective-permute-start.1 = (bf16[144,768]{1,0:T(8,128)(2,1)S(1)}, bf16[144,768]{1,0:T(8,128)(2,1)S(1)}, u32[]{:S(2)}, u32[]{:S(2)}) collective-permute-start(bf16[144,768]{1,0:T(8,128)(2,1)S(1)} %pack.1.message), channel_id=1, source_target_pairs={{3,4},{7,8},{11,12},{15,16},{19,20},{23,24},{27,28},{4,3},{8,7},{1... | collective-permute-start | bytes 663560 | tf_op jit(solution)/shard_map/ppermute | solution.py:489
  5.7 4.5 %collective-permute-done.near = bf16[144,768]{1,0:T(8,128)(2,1)S(1)} collective-permute-done((bf16[144,768]{1,0:T(8,128)(2,1)S(1)}, bf16[144,768]{1,0:T(8,128)(2,1)S(1)}, u32[]{:S(2)}, u32[]{:S(2)}) %collective-permute-start) | collective-permute-done | bytes 221216 | tf_op jit(solution)/shard_map/ppermute | solution.py:488
  10.2 1.3 %collective-permute-start.2 = (bf16[144,768]{1,0:T(8,128)(2,1)S(1)}, bf16[144,768]{1,0:T(8,128)(2,1)S(1)}, u32[]{:S(2)}, u32[]{:S(2)}) collective-permute-start(bf16[144,768]{1,0:T(8,128)(2,1)S(1)} %collective-permute-done.near), channel_id=1, source_target_pairs={{0,2},{4,6},{8,10},{12,14},{16,18},{20,22},{24,26},{28,30},{3,1},{... | collective-permute-start | bytes 663560 | tf_op jit(solution)/shard_map/ppermute | solution.py:490
  11.5 0.1 pad_add_fusion.shifts
  11.6 0.0 collective-permute-done.1.far_a
  11.6 2.1 %collective-permute-done.2.far_b = bf16[144,768]{1,0:T(8,128)(2,1)S(1)} collective-permute-done((bf16[144,768]{1,0:T(8,128)(2,1)S(1)}, bf16[144,768]{1,0:T(8,128)(2,1)S(1)}, u32[]{:S(2)}, u32[]{:S(2)}) %collective-permute-start.2) | collective-permute-done | bytes 221216 | tf_op jit(solution)/shard_map/ppermute | solution.py:490
  13.7 16.5 %neighbour_blocks.1 = (bf16[272,768]{1,0:T(8,128)(2,1)S(1)}, bf16[272,768]{1,0:T(8,128)(2,1)S(1)}) custom-call(s32[2]{0:T(128)S(1)} %pad_add_fusion.shifts, bf16[144,768]{1,0:T(8,128)(2,1)S(1)} %collective-permute-done.near, bf16[144,768]{1,0:T(8,128)(2,1)S(1)} %collective-permute-done.1.far_a, bf16[144,768]{1,0:T(8,128)(2,1)S(1)} %collective-permute-done.2.far_b, ...), custom_call_target="tpu_custom_call" | custom-call | flops 6442450944 | bytes 12582912 | tf_op jit(solution)/shard_map/neighbour_blocks/pallas_call | solution.py:340
  30.1 0.0 copy-start.2
  30.1 0.0 copy-start.4
  30.2 2.1 %collective-permute-start.3 = (bf16[272,768]{1,0:T(8,128)(2,1)S(1)}, bf16[272,768]{1,0:T(8,128)(2,1)S(1)}, u32[]{:S(2)}, u32[]{:S(2)}) collective-permute-start(bf16[272,768]{1,0:T(8,128)(2,1)S(1)} %get-tuple-element.9), channel_id=1, source_target_pairs={{2,0},{6,4},{10,8},{14,12},{18,16},{22,20},{26,24},{30,28},{1,3},{... | collective-permute-start | bytes 1253384 | tf_op jit(solution)/shard_map/ppermute | solution.py:494
  32.2 0.9 %collective-permute-start.5 = (bf16[272,768]{1,0:T(8,128)(2,1)S(1)}, bf16[272,768]{1,0:T(8,128)(2,1)S(1)}, u32[]{:S(2)}, u32[]{:S(2)}) collective-permute-start(bf16[272,768]{1,0:T(8,128)(2,1)S(1)} %get-tuple-element.9), channel_id=1, source_target_pairs={{3,4},{7,8},{11,12},{15,16},{19,20},{23,24},{27,28},{4,3},{8,7},{1... | collective-permute-start | bytes 1253384 | tf_op jit(solution)/shard_map/ppermute | solution.py:493
  33.1 0.5 collective-permute-done.3.second
  33.6 1.1 %merge.1 = bf16[272,768]{1,0:T(8,128)(2,1)S(1)} custom-call(bf16[272,768]{1,0:T(8,128)(2,1)S(1)} %get-tuple-element.11.first, bf16[272,768]{1,0:T(8,128)(2,1)S(1)} %collective-permute-done.3.second), custom_call_target="tpu_custom_call" | custom-call | tf_op jit(solution)/shard_map/merge/pallas_call | solution.py:425
  34.7 4.8 %collective-permute-start.4 = (bf16[272,768]{1,0:T(8,128)(2,1)S(1)}, bf16[272,768]{1,0:T(8,128)(2,1)S(1)}, u32[]{:S(2)}, u32[]{:S(2)}) collective-permute-start(bf16[272,768]{1,0:T(8,128)(2,1)S(1)} %merge.1), channel_id=1, source_target_pairs={{0,1},{1,0},{2,3},{3,2},{4,5},{5,4},{6,7},{7,6},{8,9},{9,8},{10,11... | collective-permute-start | bytes 1253384 | tf_op jit(solution)/shard_map/ppermute | solution.py:495
  39.5 14.5 %own_block.1.first = bf16[272,768]{1,0:T(8,128)(2,1)S(1)} custom-call(s32[1]{0:T(128)} %constant.21.clone.1.shift, bf16[144,768]{1,0:T(8,128)(2,1)S(1)} %pack.1.message, bf16[8192,768]{1,0:T(8,128)(2,1)} %corpus.3), custom_call_target="tpu_custom_call" | custom-call | flops 6442450944 | bytes 12582912 | tf_op jit(solution)/shard_map/own_block/pallas_call | solution.py:229
  54.0 0.0 collective-permute-done.5.third
  54.1 0.0 collective-permute-done.4.second
  54.1 0.0 copy-done.2
  54.1 0.0 copy-done.4
  54.1 1.8 %finish.1 = (bf16[128,2,768]{2,1,0:T(2,128)(2,1)}, f32[2,128]{1,0:T(2,128)}, f32[2,128]{1,0:T(2,128)}) custom-call(s32[2,128]{1,0:T(2,128)S(1)} %bitcast.8, s32[2,128]{1,0:T(2,128)S(1)} %bitcast.10, bf16[272,768]{1,0:T(8,128)(2,1)S(1)} %own_block.1.first, bf16[272,768]{1,0:T(8,128)(2,1)S(1)} %collective-permute-done.4.second, ...), custom_call_target="tpu_custom_call" | custom-call | tf_op jit(solution)/shard_map/finish/pallas_call | solution.py:465
  (1 shorter events, 0.0 us)
Async XLA Ops:
  0.6 0.9 %copy-start = (bf16[128,768]{1,0:T(8,128)(2,1)S(1)}, bf16[128,768]{1,0:T(8,128)(2,1)}, u32[]{:S(2)}) copy-start(bf16[128,768]{1,0:T(8,128)(2,1)} %queries.1) | copy-start | bytes 589828
  1.6 0.7 %copy-start.1 = (s32[128,2]{0,1:T(2,128)S(1)}, s32[128,2]{0,1:T(2,128)}, u32[]{:S(2)}) copy-start(s32[128,2]{0,1:T(2,128)} %param.6) | copy-start | bytes 3076
  2.2 0.7 %copy-start.3 = (s32[128,2]{0,1:T(2,128)S(1)}, s32[128,2]{0,1:T(2,128)}, u32[]{:S(2)}) copy-start(s32[128,2]{0,1:T(2,128)} %param.7) | copy-start | bytes 3076
  3.0 7.3 %collective-permute-start = (bf16[144,768]{1,0:T(8,128)(2,1)S(1)}, bf16[144,768]{1,0:T(8,128)(2,1)S(1)}, u32[]{:S(2)}, u32[]{:S(2)}) collective-permute-start(bf16[144,768]{1,0:T(8,128)(2,1)S(1)} %pack.1.message), channel_id=1, source_target_pairs={{0,1},{1,0},{2,3},{3,2},{4,5},{5,4},{6,7},{7,6},{8,9},{9,8},{10,11... | collective-permute-start | bytes 663560 | tf_op jit(solution)/shard_map/ppermute | solution.py:488
  5.1 6.5 %collective-permute-start.1 = (bf16[144,768]{1,0:T(8,128)(2,1)S(1)}, bf16[144,768]{1,0:T(8,128)(2,1)S(1)}, u32[]{:S(2)}, u32[]{:S(2)}) collective-permute-start(bf16[144,768]{1,0:T(8,128)(2,1)S(1)} %pack.1.message), channel_id=1, source_target_pairs={{3,4},{7,8},{11,12},{15,16},{19,20},{23,24},{27,28},{4,3},{8,7},{1... | collective-permute-start | bytes 663560 | tf_op jit(solution)/shard_map/ppermute | solution.py:489
  10.2 3.5 %collective-permute-start.2 = (bf16[144,768]{1,0:T(8,128)(2,1)S(1)}, bf16[144,768]{1,0:T(8,128)(2,1)S(1)}, u32[]{:S(2)}, u32[]{:S(2)}) collective-permute-start(bf16[144,768]{1,0:T(8,128)(2,1)S(1)} %collective-permute-done.near), channel_id=1, source_target_pairs={{0,2},{4,6},{8,10},{12,14},{16,18},{20,22},{24,26},{28,30},{3,1},{... | collective-permute-start | bytes 663560 | tf_op jit(solution)/shard_map/ppermute | solution.py:490
  30.1 23.9 %copy-start.2 = (s32[128,2]{0,1:T(2,128)S(1)}, s32[128,2]{0,1:T(2,128)}, u32[]{:S(2)}) copy-start(s32[128,2]{0,1:T(2,128)} %param.6) | copy-start | bytes 3076
  30.1 23.9 %copy-start.4 = (s32[128,2]{0,1:T(2,128)S(1)}, s32[128,2]{0,1:T(2,128)}, u32[]{:S(2)}) copy-start(s32[128,2]{0,1:T(2,128)} %param.7) | copy-start | bytes 3076
  30.2 3.4 %collective-permute-start.3 = (bf16[272,768]{1,0:T(8,128)(2,1)S(1)}, bf16[272,768]{1,0:T(8,128)(2,1)S(1)}, u32[]{:S(2)}, u32[]{:S(2)}) collective-permute-start(bf16[272,768]{1,0:T(8,128)(2,1)S(1)} %get-tuple-element.9), channel_id=1, source_target_pairs={{2,0},{6,4},{10,8},{14,12},{18,16},{22,20},{26,24},{30,28},{1,3},{... | collective-permute-start | bytes 1253384 | tf_op jit(solution)/shard_map/ppermute | solution.py:494
  32.2 21.8 %collective-permute-start.5 = (bf16[272,768]{1,0:T(8,128)(2,1)S(1)}, bf16[272,768]{1,0:T(8,128)(2,1)S(1)}, u32[]{:S(2)}, u32[]{:S(2)}) collective-permute-start(bf16[272,768]{1,0:T(8,128)(2,1)S(1)} %get-tuple-element.9), channel_id=1, source_target_pairs={{3,4},{7,8},{11,12},{15,16},{19,20},{23,24},{27,28},{4,3},{8,7},{1... | collective-permute-start | bytes 1253384 | tf_op jit(solution)/shard_map/ppermute | solution.py:493
  34.7 19.4 %collective-permute-start.4 = (bf16[272,768]{1,0:T(8,128)(2,1)S(1)}, bf16[272,768]{1,0:T(8,128)(2,1)S(1)}, u32[]{:S(2)}, u32[]{:S(2)}) collective-permute-start(bf16[272,768]{1,0:T(8,128)(2,1)S(1)} %merge.1), channel_id=1, source_target_pairs={{0,1},{1,0},{2,3},{3,2},{4,5},{5,4},{6,7},{7,6},{8,9},{9,8},{10,11... | collective-permute-start | bytes 1253384 | tf_op jit(solution)/shard_map/ppermute | solution.py:495

commit v7 on v6

--- a/solution.py
+++ b/solution.py
@@ -50,8 +50,6 @@
 def row_scratch(rows, docs, width, tile):
     groups = rows // LANES
     return [
-        pltpu.VMEM((docs, width), BF16),
-        pltpu.SemaphoreType.DMA((docs // tile,)),
         pltpu.VMEM((rows, width), BF16),
         pltpu.VMEM((groups, SUBLANES, LANES), jnp.int32),
         pltpu.VMEM((groups, SUBLANES, LANES), jnp.int32),
@@ -83,15 +81,15 @@
 
 
 def set_bounds(scratch, low, length):
-    lows, lengths = scratch[3:5]
+    lows, lengths = scratch[1:3]
     for g in range(lows.shape[0]):
         at = slice(g * LANES, (g + 1) * LANES)
         lows[g] = jnp.broadcast_to(low[:, at], (SUBLANES, LANES))
         lengths[g] = jnp.broadcast_to(length[:, at], (SUBLANES, LANES))
 
 
-def attend_rows(scratch, corpus, step):
-    docs, arrived, rows_q, lows, lengths, peak, score_sum, mass, s_a, s_b, masked, p_a, p_b, acc = scratch
+def attend_rows(docs, scratch, step, corpus=None, arrived=None):
+    rows_q, lows, lengths, peak, score_sum, mass, s_a, s_b, masked, p_a, p_b, acc = scratch
     n_docs, width = docs.shape
     tile = s_a.shape[0]
     tiles = n_docs // tile
@@ -112,7 +110,9 @@
         return jnp.broadcast_to(ref[g][0:1, :], (CHUNK, LANES))
 
     def score(t):
-        tile_copy(corpus, docs, arrived, t).wait()
+        if corpus is not None and t % (tiles // 2) == 0:
+            for k in range(t, t + tiles // 2):
+                tile_copy(corpus, docs, arrived, k).wait()
         (s_a, s_b)[t % 2][...] = lax.dot_general(
             docs[t * tile : (t + 1) * tile, :], rows_q[met_rows(t), :], NT, preferred_element_type=F32
         )
@@ -208,15 +208,14 @@
     return lows, [jnp.maximum(bound(2 + w) - low, 0) for w, low in enumerate(lows)]
 
 
-def own_kernel(shift, message, corpus, out, *scratch):
-    docs, arrived, rows_q = scratch[:3]
-    start_copies(corpus, docs, arrived)
+def own_kernel(shift, message, docs, out, *scratch):
+    rows_q = scratch[0]
     queries = message.shape[0] - META
     lows, lengths = bound_lines(message[queries:, 0:queries], shift[0], docs.shape[0])
     set_bounds(scratch, jnp.concatenate(lows, axis=1), jnp.concatenate(lengths, axis=1))
     for w in range(2):
         rows_q[w * queries : (w + 1) * queries, :] = message[0:queries, :]
-    stats = attend_rows(scratch, corpus, 0)
+    stats = attend_rows(docs, scratch, 0)
     out[0 : 2 * queries, :] = scratch[-1][...].astype(BF16)
     out[2 * queries :, :] = jnp.zeros((META, out.shape[1]), BF16)
     out[2 * queries :, 0 : 2 * queries] = stats_lines(stats)
@@ -229,10 +228,10 @@
     return pl.pallas_call(
         own_kernel,
         out_shape=jax.ShapeDtypeStruct((2 * queries + META, width), BF16),
-        in_specs=[SMEM, VMEM, HBM],
+        in_specs=[SMEM, VMEM, VMEM],
         out_specs=VMEM,
         scratch_shapes=row_scratch(2 * queries, docs, width, tile),
-        compiler_params=params(44),
+        compiler_params=params(16),
         cost_estimate=pl.CostEstimate(
             flops=8 * queries * docs * width,
             bytes_accessed=docs * width * 2,
@@ -242,8 +241,8 @@
     )(shift, message, corpus)
 
 
-def neighbour_kernel(shifts, near, far_a, far_b, corpus, near_out, far_out, both_q, pooled, *scratch):
-    docs, arrived, rows_q = scratch[:3]
+def neighbour_kernel(shifts, near, far_a, far_b, corpus, near_out, far_out, docs, arrived, both_q, pooled, *scratch):
+    rows_q = scratch[0]
     start_copies(corpus, docs, arrived)
     queries = near.shape[0] - META
     n_docs = docs.shape[0]
@@ -314,7 +313,7 @@
             (lines[0:1, :] * 256.0 + lines[1:2, :]).astype(jnp.int32),
             (lines[2:3, :] * 256.0 + lines[3:4, :]).astype(jnp.int32),
         )
-        stats = stats_lines(attend_rows(scratch, corpus, step))
+        stats = stats_lines(attend_rows(docs, scratch, step, corpus, arrived))
         pooled[...] = scratch[-1][...].astype(BF16)
         for b, chosen in enumerate(pick):
             out = (near_out, far_out)[b // 2]
@@ -342,9 +341,14 @@
         out_shape=(result, result),
         in_specs=[SMEM, VMEM, VMEM, VMEM, HBM],
         out_specs=(VMEM, VMEM),
-        scratch_shapes=[pltpu.VMEM((2 * queries, width), BF16), pltpu.VMEM((held, width), BF16)]
+        scratch_shapes=[
+            pltpu.VMEM((docs, width), BF16),
+            pltpu.SemaphoreType.DMA((docs // tile,)),
+            pltpu.VMEM((2 * queries, width), BF16),
+            pltpu.VMEM((held, width), BF16),
+        ]
         + row_scratch(held, docs, width, tile),
-        compiler_params=params(44),
+        compiler_params=params(30),
         cost_estimate=pl.CostEstimate(
             flops=8 * queries * docs * width,
             bytes_accessed=docs * width * 2,

time: 56.5 us -> 55.7 us (0.986)
  Pallas kernels: 33.9 us -> 25 us
  local copies, waits for them, and re-layouts: 2.29 us -> 6.87 us
  waiting for transfers between devices: 7.04 us -> 11 us
    pallas_call x1, Pallas kernels: 14.5 us -> 8.83 us  [own(): pl.pallas_call(own_kernel, out_shape=jax.ShapeDtypeStruct((2 * queries +...]
    unnamed x10 -> x12, local copies, waits for them, and re-layouts: 2.29 us -> 6.87 us
    ppermute x1, waiting for transfers between devices: 0.01 us -> 3.95 us  [local(): near_back = lax.ppermute(merge(near_part, relayed), AXES, across)]
    pallas_call x1, Pallas kernels: 16.5 us -> 13.2 us  [neighbours(): pl.pallas_call(neighbour_kernel, out_shape=(result, result), in_specs=[SM...]
  transfers between devices with their start and end apart: 6 -> 6, of which waited for: 3 -> 4; matrix products, arithmetic and copies ran while one was open for 0% -> 0% of each run, Pallas kernels for 28% -> 18%
where the time goes in v7:
time: 55.7 us; the launch traced here: 55.4 us
  Pallas kernels  25 us (45%)
  starting transfers between devices  11.8 us (21%)
  waiting for transfers between devices  11 us (20%)
  local copies, waits for them, and re-layouts  6.87 us (12%)
  between operations  0.74 us (1%)
    pallas_call x1, Pallas kernels, neighbours(): pl.pallas_call(neighbour_kernel, out_shape=(result, result), in_specs=[SM...  13.2 us
    pallas_call x1, Pallas kernels, own(): pl.pallas_call(own_kernel, out_shape=jax.ShapeDtypeStruct((2 * queries +...  8.83 us
    unnamed x12, local copies, waits for them, and re-layouts  6.87 us
    ppermute x1, starting transfers between devices, local(): near_back = lax.ppermute(merge(near_part, relayed), AXES, across)  4.83 us
    ppermute x1, waiting for transfers between devices, local(): near = lax.ppermute(message, AXES, across)  4.48 us
    ppermute x1, waiting for transfers between devices, local(): near_back = lax.ppermute(merge(near_part, relayed), AXES, across)  3.95 us
    ppermute x1, starting transfers between devices, local(): near = lax.ppermute(message, AXES, across)  2.11 us
    ppermute x1, waiting for transfers between devices, local(): far_b = lax.ppermute(near, AXES, relay)  2.09 us
  transfers between devices with their start and end apart: 6, of which 4 were waited for; matrix products, arithmetic and copies ran while one was open for 0% of the time, Pallas kernels for 18%

profile of v7, /device:TPU:1, one launch (start us, length us, event | category | flops | bytes accessed | tf_op | source)
XLA Modules:
  0.0 55.4 jit_solution(9010791563395619676)
XLA Ops:
  0.6 0.0 copy-start
  0.6 0.9 %copy-done = bf16[128,768]{1,0:T(8,128)(2,1)S(1)} copy-done((bf16[128,768]{1,0:T(8,128)(2,1)S(1)}, bf16[128,768]{1,0:T(8,128)(2,1)}, u32[]{:S(2)}) %copy-start) | copy-done | bytes 196632
  1.6 0.0 copy-start.1
  1.6 0.7 %copy-done.1 = s32[128,2]{0,1:T(2,128)S(1)} copy-done((s32[128,2]{0,1:T(2,128)S(1)}, s32[128,2]{0,1:T(2,128)}, u32[]{:S(2)}) %copy-start.1) | copy-done | bytes 1048
  2.2 0.0 copy-start.3
  2.2 0.7 %copy-done.3 = s32[128,2]{0,1:T(2,128)S(1)} copy-done((s32[128,2]{0,1:T(2,128)S(1)}, s32[128,2]{0,1:T(2,128)}, u32[]{:S(2)}) %copy-start.3) | copy-done | bytes 1048
  3.0 2.1 %collective-permute-start = (bf16[144,768]{1,0:T(8,128)(2,1)S(1)}, bf16[144,768]{1,0:T(8,128)(2,1)S(1)}, u32[]{:S(2)}, u32[]{:S(2)}) collective-permute-start(bf16[144,768]{1,0:T(8,128)(2,1)S(1)} %pack.1.message), channel_id=1, source_target_pairs={{0,1},{1,0},{2,3},{3,2},{4,5},{5,4},{6,7},{7,6},{8,9},{9,8},{10,11... | collective-permute-start | bytes 663560 | tf_op jit(solution)/shard_map/ppermute | solution.py:492
  5.1 0.7 %collective-permute-start.1 = (bf16[144,768]{1,0:T(8,128)(2,1)S(1)}, bf16[144,768]{1,0:T(8,128)(2,1)S(1)}, u32[]{:S(2)}, u32[]{:S(2)}) collective-permute-start(bf16[144,768]{1,0:T(8,128)(2,1)S(1)} %pack.1.message), channel_id=1, source_target_pairs={{3,4},{7,8},{11,12},{15,16},{19,20},{23,24},{27,28},{4,3},{8,7},{1... | collective-permute-start | bytes 663560 | tf_op jit(solution)/shard_map/ppermute | solution.py:493
  5.7 4.5 %collective-permute-done.near = bf16[144,768]{1,0:T(8,128)(2,1)S(1)} collective-permute-done((bf16[144,768]{1,0:T(8,128)(2,1)S(1)}, bf16[144,768]{1,0:T(8,128)(2,1)S(1)}, u32[]{:S(2)}, u32[]{:S(2)}) %collective-permute-start) | collective-permute-done | bytes 221216 | tf_op jit(solution)/shard_map/ppermute | solution.py:492
  10.2 1.3 %collective-permute-start.2 = (bf16[144,768]{1,0:T(8,128)(2,1)S(1)}, bf16[144,768]{1,0:T(8,128)(2,1)S(1)}, u32[]{:S(2)}, u32[]{:S(2)}) collective-permute-start(bf16[144,768]{1,0:T(8,128)(2,1)S(1)} %collective-permute-done.near), channel_id=1, source_target_pairs={{0,2},{4,6},{8,10},{12,14},{16,18},{20,22},{24,26},{28,30},{3,1},{... | collective-permute-start | bytes 663560 | tf_op jit(solution)/shard_map/ppermute | solution.py:494
  11.5 0.1 pad_add_fusion.shifts
  11.6 0.0 collective-permute-done.1.far_a
  11.6 2.1 %collective-permute-done.2.far_b = bf16[144,768]{1,0:T(8,128)(2,1)S(1)} collective-permute-done((bf16[144,768]{1,0:T(8,128)(2,1)S(1)}, bf16[144,768]{1,0:T(8,128)(2,1)S(1)}, u32[]{:S(2)}, u32[]{:S(2)}) %collective-permute-start.2) | collective-permute-done | bytes 221216 | tf_op jit(solution)/shard_map/ppermute | solution.py:494
  13.7 0.0 copy-start.5
  13.7 4.6 %copy-done.5 = bf16[8192,768]{1,0:T(8,128)(2,1)S(1)} copy-done((bf16[8192,768]{1,0:T(8,128)(2,1)S(1)}, bf16[8192,768]{1,0:T(8,128)(2,1)}, u32[]{:S(2)}) %copy-start.5) | copy-done | bytes 12582936
  18.3 13.2 %neighbour_blocks.1 = (bf16[272,768]{1,0:T(8,128)(2,1)S(1)}, bf16[272,768]{1,0:T(8,128)(2,1)S(1)}) custom-call(s32[2]{0:T(128)S(1)} %pad_add_fusion.shifts, bf16[144,768]{1,0:T(8,128)(2,1)S(1)} %collective-permute-done.near, bf16[144,768]{1,0:T(8,128)(2,1)S(1)} %collective-permute-done.1.far_a, bf16[144,768]{1,0:T(8,128)(2,1)S(1)} %collective-permute-done.2.far_b, ...), custom_call_target="tpu_custom_call" | custom-call | flops 6442450944 | bytes 12582912 | tf_op jit(solution)/shard_map/neighbour_blocks/pallas_call | solution.py:339
  31.4 0.0 copy-start.2
  31.4 0.0 copy-start.4
  31.4 2.1 %collective-permute-start.3 = (bf16[272,768]{1,0:T(8,128)(2,1)S(1)}, bf16[272,768]{1,0:T(8,128)(2,1)S(1)}, u32[]{:S(2)}, u32[]{:S(2)}) collective-permute-start(bf16[272,768]{1,0:T(8,128)(2,1)S(1)} %get-tuple-element.9), channel_id=1, source_target_pairs={{2,0},{6,4},{10,8},{14,12},{18,16},{22,20},{26,24},{30,28},{1,3},{... | collective-permute-start | bytes 1253384 | tf_op jit(solution)/shard_map/ppermute | solution.py:498
  33.5 0.9 %collective-permute-start.5 = (bf16[272,768]{1,0:T(8,128)(2,1)S(1)}, bf16[272,768]{1,0:T(8,128)(2,1)S(1)}, u32[]{:S(2)}, u32[]{:S(2)}) collective-permute-start(bf16[272,768]{1,0:T(8,128)(2,1)S(1)} %get-tuple-element.9), channel_id=1, source_target_pairs={{3,4},{7,8},{11,12},{15,16},{19,20},{23,24},{27,28},{4,3},{8,7},{1... | collective-permute-start | bytes 1253384 | tf_op jit(solution)/shard_map/ppermute | solution.py:497
  34.4 0.5 collective-permute-done.3.second
  34.9 1.1 %merge.1 = bf16[272,768]{1,0:T(8,128)(2,1)S(1)} custom-call(bf16[272,768]{1,0:T(8,128)(2,1)S(1)} %get-tuple-element.11.first, bf16[272,768]{1,0:T(8,128)(2,1)S(1)} %collective-permute-done.3.second), custom_call_target="tpu_custom_call" | custom-call | tf_op jit(solution)/shard_map/merge/pallas_call | solution.py:429
  36.0 4.8 %collective-permute-start.4 = (bf16[272,768]{1,0:T(8,128)(2,1)S(1)}, bf16[272,768]{1,0:T(8,128)(2,1)S(1)}, u32[]{:S(2)}, u32[]{:S(2)}) collective-permute-start(bf16[272,768]{1,0:T(8,128)(2,1)S(1)} %merge.1), channel_id=1, source_target_pairs={{0,1},{1,0},{2,3},{3,2},{4,5},{5,4},{6,7},{7,6},{8,9},{9,8},{10,11... | collective-permute-start | bytes 1253384 | tf_op jit(solution)/shard_map/ppermute | solution.py:499
  40.8 8.8 %own_block.1.first = bf16[272,768]{1,0:T(8,128)(2,1)S(1)} custom-call(s32[1]{0:T(128)} %constant.21.clone.1.shift, bf16[144,768]{1,0:T(8,128)(2,1)S(1)} %pack.1.message, bf16[8192,768]{1,0:T(8,128)(2,1)S(1)} %copy-done.5), custom_call_target="tpu_custom_call" | custom-call | flops 6442450944 | bytes 12582912 | tf_op jit(solution)/shard_map/own_block/pallas_call | solution.py:228
  49.7 0.0 collective-permute-done.5.third
  49.7 4.0 %collective-permute-done.4.second = bf16[272,768]{1,0:T(8,128)(2,1)S(1)} collective-permute-done((bf16[272,768]{1,0:T(8,128)(2,1)S(1)}, bf16[272,768]{1,0:T(8,128)(2,1)S(1)}, u32[]{:S(2)}, u32[]{:S(2)}) %collective-permute-start.4) | collective-permute-done | bytes 417824 | tf_op jit(solution)/shard_map/ppermute | solution.py:499
  53.6 0.0 copy-done.2
  53.6 0.0 copy-done.4
  53.6 1.8 %finish.1 = (bf16[128,2,768]{2,1,0:T(2,128)(2,1)}, f32[2,128]{1,0:T(2,128)}, f32[2,128]{1,0:T(2,128)}) custom-call(s32[2,128]{1,0:T(2,128)S(1)} %bitcast.8, s32[2,128]{1,0:T(2,128)S(1)} %bitcast.10, bf16[272,768]{1,0:T(8,128)(2,1)S(1)} %own_block.1.first, bf16[272,768]{1,0:T(8,128)(2,1)S(1)} %collective-permute-done.4.second, ...), custom_call_target="tpu_custom_call" | custom-call | tf_op jit(solution)/shard_map/finish/pallas_call | solution.py:469
  (1 shorter events, 0.0 us)
Async XLA Ops:
  0.6 0.9 %copy-start = (bf16[128,768]{1,0:T(8,128)(2,1)S(1)}, bf16[128,768]{1,0:T(8,128)(2,1)}, u32[]{:S(2)}) copy-start(bf16[128,768]{1,0:T(8,128)(2,1)} %queries.1) | copy-start | bytes 589828
  1.6 0.7 %copy-start.1 = (s32[128,2]{0,1:T(2,128)S(1)}, s32[128,2]{0,1:T(2,128)}, u32[]{:S(2)}) copy-start(s32[128,2]{0,1:T(2,128)} %param.6) | copy-start | bytes 3076
  2.2 0.7 %copy-start.3 = (s32[128,2]{0,1:T(2,128)S(1)}, s32[128,2]{0,1:T(2,128)}, u32[]{:S(2)}) copy-start(s32[128,2]{0,1:T(2,128)} %param.7) | copy-start | bytes 3076
  3.0 7.3 %collective-permute-start = (bf16[144,768]{1,0:T(8,128)(2,1)S(1)}, bf16[144,768]{1,0:T(8,128)(2,1)S(1)}, u32[]{:S(2)}, u32[]{:S(2)}) collective-permute-start(bf16[144,768]{1,0:T(8,128)(2,1)S(1)} %pack.1.message), channel_id=1, source_target_pairs={{0,1},{1,0},{2,3},{3,2},{4,5},{5,4},{6,7},{7,6},{8,9},{9,8},{10,11... | collective-permute-start | bytes 663560 | tf_op jit(solution)/shard_map/ppermute | solution.py:492
  5.1 6.5 %collective-permute-start.1 = (bf16[144,768]{1,0:T(8,128)(2,1)S(1)}, bf16[144,768]{1,0:T(8,128)(2,1)S(1)}, u32[]{:S(2)}, u32[]{:S(2)}) collective-permute-start(bf16[144,768]{1,0:T(8,128)(2,1)S(1)} %pack.1.message), channel_id=1, source_target_pairs={{3,4},{7,8},{11,12},{15,16},{19,20},{23,24},{27,28},{4,3},{8,7},{1... | collective-permute-start | bytes 663560 | tf_op jit(solution)/shard_map/ppermute | solution.py:493
  10.2 3.5 %collective-permute-start.2 = (bf16[144,768]{1,0:T(8,128)(2,1)S(1)}, bf16[144,768]{1,0:T(8,128)(2,1)S(1)}, u32[]{:S(2)}, u32[]{:S(2)}) collective-permute-start(bf16[144,768]{1,0:T(8,128)(2,1)S(1)} %collective-permute-done.near), channel_id=1, source_target_pairs={{0,2},{4,6},{8,10},{12,14},{16,18},{20,22},{24,26},{28,30},{3,1},{... | collective-permute-start | bytes 663560 | tf_op jit(solution)/shard_map/ppermute | solution.py:494
  13.7 4.6 %copy-start.5 = (bf16[8192,768]{1,0:T(8,128)(2,1)S(1)}, bf16[8192,768]{1,0:T(8,128)(2,1)}, u32[]{:S(2)}) copy-start(bf16[8192,768]{1,0:T(8,128)(2,1)} %docs.1) | copy-start | bytes 37748740
  31.4 22.2 %copy-start.2 = (s32[128,2]{0,1:T(2,128)S(1)}, s32[128,2]{0,1:T(2,128)}, u32[]{:S(2)}) copy-start(s32[128,2]{0,1:T(2,128)} %param.6) | copy-start | bytes 3076
  31.4 22.2 %copy-start.4 = (s32[128,2]{0,1:T(2,128)S(1)}, s32[128,2]{0,1:T(2,128)}, u32[]{:S(2)}) copy-start(s32[128,2]{0,1:T(2,128)} %param.7) | copy-start | bytes 3076
  31.4 3.4 %collective-permute-start.3 = (bf16[272,768]{1,0:T(8,128)(2,1)S(1)}, bf16[272,768]{1,0:T(8,128)(2,1)S(1)}, u32[]{:S(2)}, u32[]{:S(2)}) collective-permute-start(bf16[272,768]{1,0:T(8,128)(2,1)S(1)} %get-tuple-element.9), channel_id=1, source_target_pairs={{2,0},{6,4},{10,8},{14,12},{18,16},{22,20},{26,24},{30,28},{1,3},{... | collective-permute-start | bytes 1253384 | tf_op jit(solution)/shard_map/ppermute | solution.py:498
  33.5 16.1 %collective-permute-start.5 = (bf16[272,768]{1,0:T(8,128)(2,1)S(1)}, bf16[272,768]{1,0:T(8,128)(2,1)S(1)}, u32[]{:S(2)}, u32[]{:S(2)}) collective-permute-start(bf16[272,768]{1,0:T(8,128)(2,1)S(1)} %get-tuple-element.9), channel_id=1, source_target_pairs={{3,4},{7,8},{11,12},{15,16},{19,20},{23,24},{27,28},{4,3},{8,7},{1... | collective-permute-start | bytes 1253384 | tf_op jit(solution)/shard_map/ppermute | solution.py:497
  36.0 17.6 %collective-permute-start.4 = (bf16[272,768]{1,0:T(8,128)(2,1)S(1)}, bf16[272,768]{1,0:T(8,128)(2,1)S(1)}, u32[]{:S(2)}, u32[]{:S(2)}) collective-permute-start(bf16[272,768]{1,0:T(8,128)(2,1)S(1)} %merge.1), channel_id=1, source_target_pairs={{0,1},{1,0},{2,3},{3,2},{4,5},{5,4},{6,7},{7,6},{8,9},{9,8},{10,11... | collective-permute-start | bytes 1253384 | tf_op jit(solution)/shard_map/ppermute | solution.py:499

commit v8 on v7

--- a/solution.py
+++ b/solution.py
@@ -24,7 +24,6 @@
 
 VMEM = pl.BlockSpec(memory_space=pltpu.VMEM)
 SMEM = pl.BlockSpec(memory_space=pltpu.SMEM)
-HBM = pl.BlockSpec(memory_space=pltpu.HBM)
 
 
 def params(mebibytes):
@@ -65,17 +64,6 @@
     ]
 
 
-def tile_copy(corpus, docs, arrived, t):
-    tile = docs.shape[0] // arrived.shape[0]
-    at = pl.ds(t * tile, tile)
-    return pltpu.make_async_copy(corpus.at[at], docs.at[at], arrived.at[t])
-
-
-def start_copies(corpus, docs, arrived):
-    for t in range(arrived.shape[0]):
-        tile_copy(corpus, docs, arrived, t).start()
-
-
 def fold(values, op):
     return op(values.reshape(values.shape[0] // SUBLANES, SUBLANES, values.shape[1]), axis=0)
 
@@ -88,7 +76,7 @@
         lengths[g] = jnp.broadcast_to(length[:, at], (SUBLANES, LANES))
 
 
-def attend_rows(docs, scratch, step, corpus=None, arrived=None):
+def attend_rows(docs, scratch, step):
     rows_q, lows, lengths, peak, score_sum, mass, s_a, s_b, masked, p_a, p_b, acc = scratch
     n_docs, width = docs.shape
     tile = s_a.shape[0]
@@ -110,9 +98,6 @@
         return jnp.broadcast_to(ref[g][0:1, :], (CHUNK, LANES))
 
     def score(t):
-        if corpus is not None and t % (tiles // 2) == 0:
-            for k in range(t, t + tiles // 2):
-                tile_copy(corpus, docs, arrived, k).wait()
         (s_a, s_b)[t % 2][...] = lax.dot_general(
             docs[t * tile : (t + 1) * tile, :], rows_q[met_rows(t), :], NT, preferred_element_type=F32
         )
@@ -241,9 +226,8 @@
     )(shift, message, corpus)
 
 
-def neighbour_kernel(shifts, near, far_a, far_b, corpus, near_out, far_out, docs, arrived, both_q, pooled, *scratch):
+def neighbour_kernel(shifts, near, far_a, far_b, docs, near_out, far_out, both_q, pooled, *scratch):
     rows_q = scratch[0]
-    start_copies(corpus, docs, arrived)
     queries = near.shape[0] - META
     n_docs = docs.shape[0]
     held = rows_q.shape[0]
@@ -313,18 +297,13 @@
             (lines[0:1, :] * 256.0 + lines[1:2, :]).astype(jnp.int32),
             (lines[2:3, :] * 256.0 + lines[3:4, :]).astype(jnp.int32),
         )
-        stats = stats_lines(attend_rows(docs, scratch, step, corpus, arrived))
+        stats = stats_lines(attend_rows(docs, scratch, step))
         pooled[...] = scratch[-1][...].astype(BF16)
         for b, chosen in enumerate(pick):
             out = (near_out, far_out)[b // 2]
             at = slice((b % 2) * queries, (b % 2 + 1) * queries)
             out[at, :] += lax.dot_general(chosen, pooled[...], TN, preferred_element_type=F32).astype(BF16)
             out[2 * queries :, at] += jnp.dot(stats, chosen, preferred_element_type=F32).astype(BF16)
-
-        @pl.when(turn + 1 < passes)
-        def _():
-            start_copies(corpus, docs, arrived)
-
         return carry
 
     lax.fori_loop(0, passes, work, 0)
@@ -339,16 +318,14 @@
     return pl.pallas_call(
         neighbour_kernel,
         out_shape=(result, result),
-        in_specs=[SMEM, VMEM, VMEM, VMEM, HBM],
+        in_specs=[SMEM, VMEM, VMEM, VMEM, VMEM],
         out_specs=(VMEM, VMEM),
         scratch_shapes=[
-            pltpu.VMEM((docs, width), BF16),
-            pltpu.SemaphoreType.DMA((docs // tile,)),
             pltpu.VMEM((2 * queries, width), BF16),
             pltpu.VMEM((held, width), BF16),
         ]
         + row_scratch(held, docs, width, tile),
-        compiler_params=params(30),
+        compiler_params=params(18),
         cost_estimate=pl.CostEstimate(
             flops=8 * queries * docs * width,
             bytes_accessed=docs * width * 2,
@@ -368,7 +345,7 @@
     out[rows:, 0:rows] = jnp.concatenate(lines, axis=0).astype(BF16)
 
 
-def pack(base, queries, starts, ends):
+def pack(base, queries, starts, ends, waiting):
     rows, width = queries.shape
     return pl.pallas_call(
         pack_kernel,
@@ -376,6 +353,7 @@
         in_specs=[SMEM, VMEM, VMEM, VMEM],
         out_specs=VMEM,
         compiler_params=params(4),
+        cost_estimate=pl.CostEstimate(flops=waiting, bytes_accessed=0, transcendentals=0),
         name="pack",
     )(base, queries, starts, ends)
 
@@ -477,6 +455,7 @@
 
 
 def local(queries, corpus, window_start, window_end):
+    rows, width = queries.shape
     docs = corpus.shape[0]
     size = lax.axis_size(AXES)
     position = lax.axis_index(AXES)
@@ -488,7 +467,7 @@
 
     starts, ends = window_start.T, window_end.T
     base = jnp.full((1,), (position - 1) * docs, jnp.int32)
-    message = pack(base, queries, starts, ends)
+    message = pack(base, queries, starts, ends, 8 * rows * docs * width)
     near = lax.ppermute(message, AXES, across)
     far_a = lax.ppermute(message, AXES, between)
     far_b = lax.ppermute(near, AXES, relay)

time: 55.7 us -> 54.5 us (0.978)
  Pallas kernels: 25 us -> 24 us
    pallas_call x1, Pallas kernels: 13.2 us -> 11.9 us  [neighbours(): pl.pallas_call(neighbour_kernel, out_shape=(result, result), in_specs=[SM...]
    unnamed x12 -> x14, local copies, waits for them, and re-layouts: 6.87 us -> 6.87 us
  transfers between devices with their start and end apart: 6 -> 6, of which waited for: 4 -> 4; matrix products, arithmetic and copies ran while one was open for 0% -> 0% of each run, Pallas kernels for 18% -> 19%
where the time goes in v8:
time: 54.5 us; the launch traced here: 54.2 us
  Pallas kernels  24 us (44%)
  starting transfers between devices  11.8 us (22%)
  waiting for transfers between devices  10.8 us (20%)
  local copies, waits for them, and re-layouts  6.87 us (13%)
  between operations  0.74 us (1%)
    pallas_call x1, Pallas kernels, neighbours(): pl.pallas_call(neighbour_kernel, out_shape=(result, result), in_specs=[SM...  11.9 us
    pallas_call x1, Pallas kernels, own(): pl.pallas_call(own_kernel, out_shape=jax.ShapeDtypeStruct((2 * queries +...  9.06 us
    unnamed x14, local copies, waits for them, and re-layouts  6.87 us
    ppermute x1, starting transfers between devices, local(): near_back = lax.ppermute(merge(near_part, relayed), AXES, across)  4.82 us
    ppermute x1, waiting for transfers between devices, local(): near = lax.ppermute(message, AXES, across)  4.48 us
    ppermute x1, waiting for transfers between devices, local(): near_back = lax.ppermute(merge(near_part, relayed), AXES, across)  3.72 us
    ppermute x1, starting transfers between devices, local(): near = lax.ppermute(message, AXES, across)  2.11 us
    ppermute x1, waiting for transfers between devices, local(): far_b = lax.ppermute(near, AXES, relay)  2.09 us
  transfers between devices with their start and end apart: 6, of which 4 were waited for; matrix products, arithmetic and copies ran while one was open for 0% of the time, Pallas kernels for 19%

profile of v8, /device:TPU:1, one launch (start us, length us, event | category | flops | bytes accessed | tf_op | source)
XLA Modules:
  0.0 54.2 jit_solution(5696129692252458975)
XLA Ops:
  0.6 0.0 copy-start
  0.6 0.7 %copy-done = s32[128,2]{0,1:T(2,128)S(1)} copy-done((s32[128,2]{0,1:T(2,128)S(1)}, s32[128,2]{0,1:T(2,128)}, u32[]{:S(2)}) %copy-start) | copy-done | bytes 1048
  1.3 0.0 copy-start.2
  1.3 0.7 %copy-done.2 = s32[128,2]{0,1:T(2,128)S(1)} copy-done((s32[128,2]{0,1:T(2,128)S(1)}, s32[128,2]{0,1:T(2,128)}, u32[]{:S(2)}) %copy-start.2) | copy-done | bytes 1048
  2.0 0.0 copy-start.6
  2.0 0.9 %copy-done.6 = bf16[128,768]{1,0:T(8,128)(2,1)S(1)} copy-done((bf16[128,768]{1,0:T(8,128)(2,1)S(1)}, bf16[128,768]{1,0:T(8,128)(2,1)}, u32[]{:S(2)}) %copy-start.6) | copy-done | bytes 196632
  3.0 2.1 %collective-permute-start = (bf16[144,768]{1,0:T(8,128)(2,1)S(1)}, bf16[144,768]{1,0:T(8,128)(2,1)S(1)}, u32[]{:S(2)}, u32[]{:S(2)}) collective-permute-start(bf16[144,768]{1,0:T(8,128)(2,1)S(1)} %pack.1.message), channel_id=1, source_target_pairs={{0,1},{1,0},{2,3},{3,2},{4,5},{5,4},{6,7},{7,6},{8,9},{9,8},{10,11... | collective-permute-start | bytes 663560 | tf_op jit(solution)/shard_map/ppermute | solution.py:471
  5.1 0.7 %collective-permute-start.1 = (bf16[144,768]{1,0:T(8,128)(2,1)S(1)}, bf16[144,768]{1,0:T(8,128)(2,1)S(1)}, u32[]{:S(2)}, u32[]{:S(2)}) collective-permute-start(bf16[144,768]{1,0:T(8,128)(2,1)S(1)} %pack.1.message), channel_id=1, source_target_pairs={{3,4},{7,8},{11,12},{15,16},{19,20},{23,24},{27,28},{4,3},{8,7},{1... | collective-permute-start | bytes 663560 | tf_op jit(solution)/shard_map/ppermute | solution.py:472
  5.7 4.5 %collective-permute-done.near = bf16[144,768]{1,0:T(8,128)(2,1)S(1)} collective-permute-done((bf16[144,768]{1,0:T(8,128)(2,1)S(1)}, bf16[144,768]{1,0:T(8,128)(2,1)S(1)}, u32[]{:S(2)}, u32[]{:S(2)}) %collective-permute-start) | collective-permute-done | bytes 221216 | tf_op jit(solution)/shard_map/ppermute | solution.py:471
  10.2 1.3 %collective-permute-start.2 = (bf16[144,768]{1,0:T(8,128)(2,1)S(1)}, bf16[144,768]{1,0:T(8,128)(2,1)S(1)}, u32[]{:S(2)}, u32[]{:S(2)}) collective-permute-start(bf16[144,768]{1,0:T(8,128)(2,1)S(1)} %collective-permute-done.near), channel_id=1, source_target_pairs={{0,2},{4,6},{8,10},{12,14},{16,18},{20,22},{24,26},{28,30},{3,1},{... | collective-permute-start | bytes 663560 | tf_op jit(solution)/shard_map/ppermute | solution.py:473
  11.5 0.1 pad_add_fusion.shifts
  11.6 0.0 collective-permute-done.1.far_a
  11.6 2.1 %collective-permute-done.2.far_b = bf16[144,768]{1,0:T(8,128)(2,1)S(1)} collective-permute-done((bf16[144,768]{1,0:T(8,128)(2,1)S(1)}, bf16[144,768]{1,0:T(8,128)(2,1)S(1)}, u32[]{:S(2)}, u32[]{:S(2)}) %collective-permute-start.2) | collective-permute-done | bytes 221216 | tf_op jit(solution)/shard_map/ppermute | solution.py:473
  13.7 0.0 copy-start.4
  13.7 4.6 %copy-done.4 = bf16[8192,768]{1,0:T(8,128)(2,1)S(1)} copy-done((bf16[8192,768]{1,0:T(8,128)(2,1)S(1)}, bf16[8192,768]{1,0:T(8,128)(2,1)}, u32[]{:S(2)}) %copy-start.4) | copy-done | bytes 12582936
  18.3 0.0 copy-start.5
  18.3 11.9 %neighbour_blocks.1 = (bf16[272,768]{1,0:T(8,128)(2,1)S(1)}, bf16[272,768]{1,0:T(8,128)(2,1)S(1)}) custom-call(s32[2]{0:T(128)S(1)} %pad_add_fusion.shifts, bf16[144,768]{1,0:T(8,128)(2,1)S(1)} %collective-permute-done.near, bf16[144,768]{1,0:T(8,128)(2,1)S(1)} %collective-permute-done.1.far_a, bf16[144,768]{1,0:T(8,128)(2,1)S(1)} %collective-permute-done.2.far_b, ...), custom_call_target="tpu_custom_call" | custom-call | flops 6442450944 | bytes 12582912 | tf_op jit(solution)/shard_map/neighbour_blocks/pallas_call | solution.py:318
  30.2 0.0 copy-start.1
  30.2 0.0 copy-start.3
  30.2 2.1 %collective-permute-start.3 = (bf16[272,768]{1,0:T(8,128)(2,1)S(1)}, bf16[272,768]{1,0:T(8,128)(2,1)S(1)}, u32[]{:S(2)}, u32[]{:S(2)}) collective-permute-start(bf16[272,768]{1,0:T(8,128)(2,1)S(1)} %get-tuple-element.9), channel_id=1, source_target_pairs={{2,0},{6,4},{10,8},{14,12},{18,16},{22,20},{26,24},{30,28},{1,3},{... | collective-permute-start | bytes 1253384 | tf_op jit(solution)/shard_map/ppermute | solution.py:477
  32.3 0.9 %collective-permute-start.5 = (bf16[272,768]{1,0:T(8,128)(2,1)S(1)}, bf16[272,768]{1,0:T(8,128)(2,1)S(1)}, u32[]{:S(2)}, u32[]{:S(2)}) collective-permute-start(bf16[272,768]{1,0:T(8,128)(2,1)S(1)} %get-tuple-element.9), channel_id=1, source_target_pairs={{3,4},{7,8},{11,12},{15,16},{19,20},{23,24},{27,28},{4,3},{8,7},{1... | collective-permute-start | bytes 1253384 | tf_op jit(solution)/shard_map/ppermute | solution.py:476
  33.2 0.5 collective-permute-done.3.second
  33.6 1.1 %merge.1 = bf16[272,768]{1,0:T(8,128)(2,1)S(1)} custom-call(bf16[272,768]{1,0:T(8,128)(2,1)S(1)} %get-tuple-element.11.first, bf16[272,768]{1,0:T(8,128)(2,1)S(1)} %collective-permute-done.3.second), custom_call_target="tpu_custom_call" | custom-call | tf_op jit(solution)/shard_map/merge/pallas_call | solution.py:407
  34.8 4.8 %collective-permute-start.4 = (bf16[272,768]{1,0:T(8,128)(2,1)S(1)}, bf16[272,768]{1,0:T(8,128)(2,1)S(1)}, u32[]{:S(2)}, u32[]{:S(2)}) collective-permute-start(bf16[272,768]{1,0:T(8,128)(2,1)S(1)} %merge.1), channel_id=1, source_target_pairs={{0,1},{1,0},{2,3},{3,2},{4,5},{5,4},{6,7},{7,6},{8,9},{9,8},{10,11... | collective-permute-start | bytes 1253384 | tf_op jit(solution)/shard_map/ppermute | solution.py:478
  39.6 0.0 copy-done.5
  39.6 9.1 %own_block.1.first = bf16[272,768]{1,0:T(8,128)(2,1)S(1)} custom-call(s32[1]{0:T(128)} %constant.21.clone.1.shift, bf16[144,768]{1,0:T(8,128)(2,1)S(1)} %pack.1.message, bf16[8192,768]{1,0:T(8,128)(2,1)S(1)} %copy-done.5), custom_call_target="tpu_custom_call" | custom-call | flops 6442450944 | bytes 12582912 | tf_op jit(solution)/shard_map/own_block/pallas_call | solution.py:213
  48.7 0.0 collective-permute-done.5.third
  48.7 3.7 %collective-permute-done.4.second = bf16[272,768]{1,0:T(8,128)(2,1)S(1)} collective-permute-done((bf16[272,768]{1,0:T(8,128)(2,1)S(1)}, bf16[272,768]{1,0:T(8,128)(2,1)S(1)}, u32[]{:S(2)}, u32[]{:S(2)}) %collective-permute-start.4) | collective-permute-done | bytes 417824 | tf_op jit(solution)/shard_map/ppermute | solution.py:478
  52.4 0.0 copy-done.1
  52.4 0.0 copy-done.3
  52.4 1.8 %finish.1 = (bf16[128,2,768]{2,1,0:T(2,128)(2,1)}, f32[2,128]{1,0:T(2,128)}, f32[2,128]{1,0:T(2,128)}) custom-call(s32[2,128]{1,0:T(2,128)S(1)} %bitcast.8, s32[2,128]{1,0:T(2,128)S(1)} %bitcast.10, bf16[272,768]{1,0:T(8,128)(2,1)S(1)} %own_block.1.first, bf16[272,768]{1,0:T(8,128)(2,1)S(1)} %collective-permute-done.4.second, ...), custom_call_target="tpu_custom_call" | custom-call | tf_op jit(solution)/shard_map/finish/pallas_call | solution.py:447
  (1 shorter events, 0.0 us)
Async XLA Ops:
  0.6 0.7 %copy-start = (s32[128,2]{0,1:T(2,128)S(1)}, s32[128,2]{0,1:T(2,128)}, u32[]{:S(2)}) copy-start(s32[128,2]{0,1:T(2,128)} %param.6) | copy-start | bytes 3076
  1.3 0.7 %copy-start.2 = (s32[128,2]{0,1:T(2,128)S(1)}, s32[128,2]{0,1:T(2,128)}, u32[]{:S(2)}) copy-start(s32[128,2]{0,1:T(2,128)} %param.7) | copy-start | bytes 3076
  2.0 0.9 %copy-start.6 = (bf16[128,768]{1,0:T(8,128)(2,1)S(1)}, bf16[128,768]{1,0:T(8,128)(2,1)}, u32[]{:S(2)}) copy-start(bf16[128,768]{1,0:T(8,128)(2,1)} %queries.1) | copy-start | bytes 589828
  3.0 7.3 %collective-permute-start = (bf16[144,768]{1,0:T(8,128)(2,1)S(1)}, bf16[144,768]{1,0:T(8,128)(2,1)S(1)}, u32[]{:S(2)}, u32[]{:S(2)}) collective-permute-start(bf16[144,768]{1,0:T(8,128)(2,1)S(1)} %pack.1.message), channel_id=1, source_target_pairs={{0,1},{1,0},{2,3},{3,2},{4,5},{5,4},{6,7},{7,6},{8,9},{9,8},{10,11... | collective-permute-start | bytes 663560 | tf_op jit(solution)/shard_map/ppermute | solution.py:471
  5.1 6.5 %collective-permute-start.1 = (bf16[144,768]{1,0:T(8,128)(2,1)S(1)}, bf16[144,768]{1,0:T(8,128)(2,1)S(1)}, u32[]{:S(2)}, u32[]{:S(2)}) collective-permute-start(bf16[144,768]{1,0:T(8,128)(2,1)S(1)} %pack.1.message), channel_id=1, source_target_pairs={{3,4},{7,8},{11,12},{15,16},{19,20},{23,24},{27,28},{4,3},{8,7},{1... | collective-permute-start | bytes 663560 | tf_op jit(solution)/shard_map/ppermute | solution.py:472
  10.2 3.5 %collective-permute-start.2 = (bf16[144,768]{1,0:T(8,128)(2,1)S(1)}, bf16[144,768]{1,0:T(8,128)(2,1)S(1)}, u32[]{:S(2)}, u32[]{:S(2)}) collective-permute-start(bf16[144,768]{1,0:T(8,128)(2,1)S(1)} %collective-permute-done.near), channel_id=1, source_target_pairs={{0,2},{4,6},{8,10},{12,14},{16,18},{20,22},{24,26},{28,30},{3,1},{... | collective-permute-start | bytes 663560 | tf_op jit(solution)/shard_map/ppermute | solution.py:473
  13.7 4.6 %copy-start.4 = (bf16[8192,768]{1,0:T(8,128)(2,1)S(1)}, bf16[8192,768]{1,0:T(8,128)(2,1)}, u32[]{:S(2)}) copy-start(bf16[8192,768]{1,0:T(8,128)(2,1)} %docs.3) | copy-start | bytes 37748740
  18.3 21.3 %copy-start.5 = (bf16[8192,768]{1,0:T(8,128)(2,1)S(1)}, bf16[8192,768]{1,0:T(8,128)(2,1)}, u32[]{:S(2)}) copy-start(bf16[8192,768]{1,0:T(8,128)(2,1)} %docs.3) | copy-start | bytes 37748740
  30.2 22.2 %copy-start.1 = (s32[128,2]{0,1:T(2,128)S(1)}, s32[128,2]{0,1:T(2,128)}, u32[]{:S(2)}) copy-start(s32[128,2]{0,1:T(2,128)} %param.6) | copy-start | bytes 3076
  30.2 22.2 %copy-start.3 = (s32[128,2]{0,1:T(2,128)S(1)}, s32[128,2]{0,1:T(2,128)}, u32[]{:S(2)}) copy-start(s32[128,2]{0,1:T(2,128)} %param.7) | copy-start | bytes 3076
  30.2 3.4 %collective-permute-start.3 = (bf16[272,768]{1,0:T(8,128)(2,1)S(1)}, bf16[272,768]{1,0:T(8,128)(2,1)S(1)}, u32[]{:S(2)}, u32[]{:S(2)}) collective-permute-start(bf16[272,768]{1,0:T(8,128)(2,1)S(1)} %get-tuple-element.9), channel_id=1, source_target_pairs={{2,0},{6,4},{10,8},{14,12},{18,16},{22,20},{26,24},{30,28},{1,3},{... | collective-permute-start | bytes 1253384 | tf_op jit(solution)/shard_map/ppermute | solution.py:477
  32.3 16.4 %collective-permute-start.5 = (bf16[272,768]{1,0:T(8,128)(2,1)S(1)}, bf16[272,768]{1,0:T(8,128)(2,1)S(1)}, u32[]{:S(2)}, u32[]{:S(2)}) collective-permute-start(bf16[272,768]{1,0:T(8,128)(2,1)S(1)} %get-tuple-element.9), channel_id=1, source_target_pairs={{3,4},{7,8},{11,12},{15,16},{19,20},{23,24},{27,28},{4,3},{8,7},{1... | collective-permute-start | bytes 1253384 | tf_op jit(solution)/shard_map/ppermute | solution.py:476
  34.8 17.6 %collective-permute-start.4 = (bf16[272,768]{1,0:T(8,128)(2,1)S(1)}, bf16[272,768]{1,0:T(8,128)(2,1)S(1)}, u32[]{:S(2)}, u32[]{:S(2)}) collective-permute-start(bf16[272,768]{1,0:T(8,128)(2,1)S(1)} %merge.1), channel_id=1, source_target_pairs={{0,1},{1,0},{2,3},{3,2},{4,5},{5,4},{6,7},{7,6},{8,9},{9,8},{10,11... | collective-permute-start | bytes 1253384 | tf_op jit(solution)/shard_map/ppermute | solution.py:478

commit v9 on v8

--- a/solution.py
+++ b/solution.py
@@ -24,6 +24,7 @@
 
 VMEM = pl.BlockSpec(memory_space=pltpu.VMEM)
 SMEM = pl.BlockSpec(memory_space=pltpu.SMEM)
+HBM = pl.BlockSpec(memory_space=pltpu.HBM)
 
 
 def params(mebibytes):
@@ -64,6 +65,16 @@
     ]
 
 
+def part_copies(corpus, docs, arrived, tile):
+    tiles = docs.shape[0] // tile
+    firsts = sorted({0, tiles // 4, tiles // 2})
+    copies = {}
+    for k, (first, end) in enumerate(zip(firsts, firsts[1:] + [tiles])):
+        at = pl.ds(first * tile, (end - first) * tile)
+        copies[first] = pltpu.make_async_copy(corpus.at[at], docs.at[at], arrived.at[k])
+    return copies
+
+
 def fold(values, op):
     return op(values.reshape(values.shape[0] // SUBLANES, SUBLANES, values.shape[1]), axis=0)
 
@@ -76,7 +87,7 @@
         lengths[g] = jnp.broadcast_to(length[:, at], (SUBLANES, LANES))
 
 
-def attend_rows(docs, scratch, step):
+def attend_rows(docs, scratch, step, copies):
     rows_q, lows, lengths, peak, score_sum, mass, s_a, s_b, masked, p_a, p_b, acc = scratch
     n_docs, width = docs.shape
     tile = s_a.shape[0]
@@ -98,6 +109,8 @@
         return jnp.broadcast_to(ref[g][0:1, :], (CHUNK, LANES))
 
     def score(t):
+        if t in copies:
+            copies[t].wait()
         (s_a, s_b)[t % 2][...] = lax.dot_general(
             docs[t * tile : (t + 1) * tile, :], rows_q[met_rows(t), :], NT, preferred_element_type=F32
         )
@@ -193,14 +206,17 @@
     return lows, [jnp.maximum(bound(2 + w) - low, 0) for w, low in enumerate(lows)]
 
 
-def own_kernel(shift, message, docs, out, *scratch):
+def own_kernel(shift, message, corpus, out, docs, arrived, *scratch):
     rows_q = scratch[0]
+    copies = part_copies(corpus, docs, arrived, scratch[6].shape[0])
+    for copy in copies.values():
+        copy.start()
     queries = message.shape[0] - META
     lows, lengths = bound_lines(message[queries:, 0:queries], shift[0], docs.shape[0])
     set_bounds(scratch, jnp.concatenate(lows, axis=1), jnp.concatenate(lengths, axis=1))
     for w in range(2):
         rows_q[w * queries : (w + 1) * queries, :] = message[0:queries, :]
-    stats = attend_rows(docs, scratch, 0)
+    stats = attend_rows(docs, scratch, 0, copies)
     out[0 : 2 * queries, :] = scratch[-1][...].astype(BF16)
     out[2 * queries :, :] = jnp.zeros((META, out.shape[1]), BF16)
     out[2 * queries :, 0 : 2 * queries] = stats_lines(stats)
@@ -213,10 +229,11 @@
     return pl.pallas_call(
         own_kernel,
         out_shape=jax.ShapeDtypeStruct((2 * queries + META, width), BF16),
-        in_specs=[SMEM, VMEM, VMEM],
+        in_specs=[SMEM, VMEM, HBM],
         out_specs=VMEM,
-        scratch_shapes=row_scratch(2 * queries, docs, width, tile),
-        compiler_params=params(16),
+        scratch_shapes=[pltpu.VMEM((docs, width), BF16), pltpu.SemaphoreType.DMA((3,))]
+        + row_scratch(2 * queries, docs, width, tile),
+        compiler_params=params(44),
         cost_estimate=pl.CostEstimate(
             flops=8 * queries * docs * width,
             bytes_accessed=docs * width * 2,
@@ -226,15 +243,18 @@
     )(shift, message, corpus)
 
 
-def neighbour_kernel(shifts, near, far_a, far_b, docs, near_out, far_out, both_q, pooled, *scratch):
+def neighbour_kernel(shifts, near, far, corpus, near_out, far_out, docs, arrived, both_q, pooled, *scratch):
     rows_q = scratch[0]
+    copies = part_copies(corpus, docs, arrived, scratch[6].shape[0])
+    for copy in copies.values():
+        copy.start()
     queries = near.shape[0] - META
     n_docs = docs.shape[0]
     held = rows_q.shape[0]
     centre = held // 2
     both_q[0:queries, :] = near[0:queries, :]
-    both_q[queries:, :] = far_a[0:queries, :] + far_b[0:queries, :]
-    metas = (near[queries:, 0:queries], far_a[queries:, 0:queries] + far_b[queries:, 0:queries])
+    both_q[queries:, :] = far[0:queries, :]
+    metas = (near[queries:, 0:queries], far[queries:, 0:queries])
     lows, lengths = [], []
     for side, meta in enumerate(metas):
         low, length = bound_lines(meta, shifts[side], n_docs)
@@ -297,19 +317,25 @@
             (lines[0:1, :] * 256.0 + lines[1:2, :]).astype(jnp.int32),
             (lines[2:3, :] * 256.0 + lines[3:4, :]).astype(jnp.int32),
         )
-        stats = stats_lines(attend_rows(docs, scratch, step))
+        stats = stats_lines(attend_rows(docs, scratch, step, copies))
         pooled[...] = scratch[-1][...].astype(BF16)
         for b, chosen in enumerate(pick):
             out = (near_out, far_out)[b // 2]
             at = slice((b % 2) * queries, (b % 2 + 1) * queries)
             out[at, :] += lax.dot_general(chosen, pooled[...], TN, preferred_element_type=F32).astype(BF16)
             out[2 * queries :, at] += jnp.dot(stats, chosen, preferred_element_type=F32).astype(BF16)
+
+        @pl.when(turn + 1 < passes)
+        def _():
+            for copy in copies.values():
+                copy.start()
+
         return carry
 
     lax.fori_loop(0, passes, work, 0)
 
 
-def neighbours(shifts, near, far_a, far_b, corpus):
+def neighbours(shifts, near, far, corpus):
     docs, width = corpus.shape
     queries = near.shape[0] - META
     held = 3 * LANES
@@ -318,21 +344,23 @@
     return pl.pallas_call(
         neighbour_kernel,
         out_shape=(result, result),
-        in_specs=[SMEM, VMEM, VMEM, VMEM, VMEM],
+        in_specs=[SMEM, VMEM, VMEM, HBM],
         out_specs=(VMEM, VMEM),
         scratch_shapes=[
+            pltpu.VMEM((docs, width), BF16),
+            pltpu.SemaphoreType.DMA((3,)),
             pltpu.VMEM((2 * queries, width), BF16),
             pltpu.VMEM((held, width), BF16),
         ]
         + row_scratch(held, docs, width, tile),
-        compiler_params=params(18),
+        compiler_params=params(44),
         cost_estimate=pl.CostEstimate(
             flops=8 * queries * docs * width,
             bytes_accessed=docs * width * 2,
             transcendentals=2 * queries * docs,
         ),
         name="neighbour_blocks",
-    )(shifts, near, far_a, far_b, corpus)
+    )(shifts, near, far, corpus)
 
 
 def pack_kernel(base, queries, starts, ends, out):
@@ -345,15 +373,13 @@
     out[rows:, 0:rows] = jnp.concatenate(lines, axis=0).astype(BF16)
 
 
-def pack(base, queries, starts, ends, waiting):
+def pack(base, queries, starts, ends):
     rows, width = queries.shape
     return pl.pallas_call(
         pack_kernel,
         out_shape=jax.ShapeDtypeStruct((rows + META, width), BF16),
         in_specs=[SMEM, VMEM, VMEM, VMEM],
         out_specs=VMEM,
-        compiler_params=params(4),
-        cost_estimate=pl.CostEstimate(flops=waiting, bytes_accessed=0, transcendentals=0),
         name="pack",
     )(base, queries, starts, ends)
 
@@ -455,26 +481,24 @@
 
 
 def local(queries, corpus, window_start, window_end):
-    rows, width = queries.shape
     docs = corpus.shape[0]
     size = lax.axis_size(AXES)
     position = lax.axis_index(AXES)
     across = [(i, i ^ 1) for i in range(size)]
     between = [(i, i + 1) for i in range(3, size - 1, 4)] + [(i + 1, i) for i in range(3, size - 1, 4)]
-    relay = [(i, i + 2) for i in range(0, size, 4)] + [(i + 3, i + 1) for i in range(0, size, 4)]
-    relay_back = [(target, source) for source, target in relay]
+    past = [(i, i + 1) for i in range(1, size - 1, 2)] + [(i + 1, i) for i in range(1, size - 1, 2)]
+    relay = [(i + 2, i) for i in range(0, size, 4)] + [(i + 1, i + 3) for i in range(0, size, 4)]
     odd = position % 2
 
     starts, ends = window_start.T, window_end.T
     base = jnp.full((1,), (position - 1) * docs, jnp.int32)
-    message = pack(base, queries, starts, ends, 8 * rows * docs * width)
+    message = pack(base, queries, starts, ends)
     near = lax.ppermute(message, AXES, across)
-    far_a = lax.ppermute(message, AXES, between)
-    far_b = lax.ppermute(near, AXES, relay)
+    far = lax.ppermute(message, AXES, past)
     shifts = jnp.stack([2 * docs * odd, 2 * docs * (1 - odd)]).astype(jnp.int32)
-    near_part, far_part = neighbours(shifts, near, far_a, far_b, corpus)
+    near_part, far_part = neighbours(shifts, near, far, corpus)
     far_back = lax.ppermute(far_part, AXES, between)
-    relayed = lax.ppermute(far_part, AXES, relay_back)
+    relayed = lax.ppermute(far_part, AXES, relay)
     near_back = lax.ppermute(merge(near_part, relayed), AXES, across)
     message, _ = lax.optimization_barrier((message, far_part))
     own_part = own(jnp.full((1,), docs, jnp.int32), message, corpus)

time: 54.5 us -> 51.4 us (0.943)
  local copies, waits for them, and re-layouts: 6.87 us -> 0.02 us
  Pallas kernels: 24 us -> 30.3 us
  waiting for transfers between devices: 10.8 us -> 9.19 us
  starting transfers between devices: 11.8 us -> 10.9 us
    unnamed x14 -> x6, local copies, waits for them, and re-layouts: 6.87 us -> 0.02 us
    pallas_call x1, Pallas kernels: 9.06 us -> 11.9 us  [own(): pl.pallas_call(own_kernel, out_shape=jax.ShapeDtypeStruct((2 * queries +...]
    ppermute x3 -> x2, waiting for transfers between devices: 2.55 us -> 5.34 us  [the longest x1 4.88 us: local(): far = lax.ppermute(message, AXES, past)]
    ppermute x1, waiting for transfers between devices: 3.72 us -> 1.1 us  [local(): near_back = lax.ppermute(merge(near_part, relayed), AXES, across)]
    pallas_call x1, Pallas kernels: 11.9 us -> 13.8 us  [neighbours(): pl.pallas_call(neighbour_kernel, out_shape=(result, result), in_specs=[SM...]
    ppermute x1, waiting for transfers between devices: 4.48 us -> 2.75 us  [local(): near = lax.ppermute(message, AXES, across)]
    pallas_call x1, Pallas kernels: 0.02 us -> 1.65 us  [pack(): pl.pallas_call(pack_kernel, out_shape=jax.ShapeDtypeStruct((rows + META,...]
    ppermute x1, starting transfers between devices: 4.82 us -> 4.09 us  [local(): near_back = lax.ppermute(merge(near_part, relayed), AXES, across)]
  transfers between devices with their start and end apart: 6 -> 5, of which waited for: 4 -> 4; matrix products, arithmetic and copies ran while one was open for 0% -> 0% of each run, Pallas kernels for 19% -> 25%
where the time goes in v9:
time: 51.4 us; the launch traced here: 51.2 us
  Pallas kernels  30.3 us (59%)
  starting transfers between devices  10.9 us (21%)
  waiting for transfers between devices  9.19 us (18%)
  between operations  0.72 us (1%)
    pallas_call x1, Pallas kernels, neighbours(): pl.pallas_call(neighbour_kernel, out_shape=(result, result), in_specs=[SM...  13.8 us
    pallas_call x1, Pallas kernels, own(): pl.pallas_call(own_kernel, out_shape=jax.ShapeDtypeStruct((2 * queries +...  11.9 us
    ppermute x1, waiting for transfers between devices, local(): far = lax.ppermute(message, AXES, past)  4.88 us
    ppermute x1, starting transfers between devices, local(): near_back = lax.ppermute(merge(near_part, relayed), AXES, across)  4.09 us
    ppermute x1, waiting for transfers between devices, local(): near = lax.ppermute(message, AXES, across)  2.75 us
    ppermute x1, starting transfers between devices, local(): far = lax.ppermute(message, AXES, past)  2.59 us
    ppermute x1, starting transfers between devices, local(): near = lax.ppermute(message, AXES, across)  2.04 us
    pallas_call x1, Pallas kernels, finish(): pl.pallas_call(finish_kernel, out_shape=(jax.ShapeDtypeStruct((queries, 2...  1.81 us
  transfers between devices with their start and end apart: 5, of which 4 were waited for; matrix products, arithmetic and copies ran while one was open for 0% of the time, Pallas kernels for 25%

profile of v9, /device:TPU:1, one launch (start us, length us, event | category | flops | bytes accessed | tf_op | source)
XLA Modules:
  0.0 51.2 jit_solution(382060209789303369)
XLA Ops:
  0.6 1.7 %pack.1.message = bf16[144,768]{1,0:T(8,128)(2,1)} custom-call(s32[1]{0:T(128)} %bitcast.2.base, bf16[128,768]{1,0:T(8,128)(2,1)} %queries.1, s32[2,128]{1,0:T(2,128)} %bitcast.7, s32[2,128]{1,0:T(2,128)} %bitcast.9), custom_call_target="tpu_custom_call" | custom-call | tf_op jit(solution)/shard_map/pack/pallas_call | solution.py:378
  2.3 0.0 copy-start
  2.3 2.0 %collective-permute-start = (bf16[144,768]{1,0:T(8,128)(2,1)}, bf16[144,768]{1,0:T(8,128)(2,1)S(1)}, u32[]{:S(2)}, u32[]{:S(2)}) collective-permute-start(bf16[144,768]{1,0:T(8,128)(2,1)} %pack.1.message), channel_id=1, source_target_pairs={{0,1},{1,0},{2,3},{3,2},{4,5},{5,4},{6,7},{7,6},{8,9},{9,8},{10,11... | collective-permute-start | bytes 663560 | tf_op jit(solution)/shard_map/ppermute | solution.py:496
  4.3 2.6 %collective-permute-start.1 = (bf16[144,768]{1,0:T(8,128)(2,1)}, bf16[144,768]{1,0:T(8,128)(2,1)S(1)}, u32[]{:S(2)}, u32[]{:S(2)}) collective-permute-start(bf16[144,768]{1,0:T(8,128)(2,1)} %pack.1.message), channel_id=1, source_target_pairs={{1,2},{3,4},{5,6},{7,8},{9,10},{11,12},{13,14},{15,16},{17,18},{19... | collective-permute-start | bytes 663560 | tf_op jit(solution)/shard_map/ppermute | solution.py:497
  6.9 0.1 pad_add_fusion.shifts
  7.0 2.7 %collective-permute-done.near = bf16[144,768]{1,0:T(8,128)(2,1)S(1)} collective-permute-done((bf16[144,768]{1,0:T(8,128)(2,1)}, bf16[144,768]{1,0:T(8,128)(2,1)S(1)}, u32[]{:S(2)}, u32[]{:S(2)}) %collective-permute-start) | collective-permute-done | bytes 221216 | tf_op jit(solution)/shard_map/ppermute | solution.py:496
  9.8 4.9 %collective-permute-done.1.far = bf16[144,768]{1,0:T(8,128)(2,1)S(1)} collective-permute-done((bf16[144,768]{1,0:T(8,128)(2,1)}, bf16[144,768]{1,0:T(8,128)(2,1)S(1)}, u32[]{:S(2)}, u32[]{:S(2)}) %collective-permute-start.1) | collective-permute-done | bytes 221216 | tf_op jit(solution)/shard_map/ppermute | solution.py:497
  14.6 13.8 %neighbour_blocks.1 = (bf16[272,768]{1,0:T(8,128)(2,1)S(1)}, bf16[272,768]{1,0:T(8,128)(2,1)S(1)}) custom-call(s32[2]{0:T(128)S(1)} %pad_add_fusion.shifts, bf16[144,768]{1,0:T(8,128)(2,1)S(1)} %collective-permute-done.near, bf16[144,768]{1,0:T(8,128)(2,1)S(1)} %collective-permute-done.1.far, bf16[8192,768]{1,0:T(8,128)(2,1)} %corpus.3), custom_call_target="tpu_custom_call" | custom-call | flops 6442450944 | bytes 12582912 | tf_op jit(solution)/shard_map/neighbour_blocks/pallas_call | solution.py:344
  28.5 0.0 copy-start.1
  28.5 0.0 copy-start.2
  28.5 1.3 %collective-permute-start.2 = (bf16[272,768]{1,0:T(8,128)(2,1)S(1)}, bf16[272,768]{1,0:T(8,128)(2,1)S(1)}, u32[]{:S(2)}, u32[]{:S(2)}) collective-permute-start(bf16[272,768]{1,0:T(8,128)(2,1)S(1)} %get-tuple-element.9), channel_id=1, source_target_pairs={{2,0},{6,4},{10,8},{14,12},{18,16},{22,20},{26,24},{30,28},{1,3},{... | collective-permute-start | bytes 1253384 | tf_op jit(solution)/shard_map/ppermute | solution.py:501
  29.8 0.9 %collective-permute-start.4 = (bf16[272,768]{1,0:T(8,128)(2,1)S(1)}, bf16[272,768]{1,0:T(8,128)(2,1)S(1)}, u32[]{:S(2)}, u32[]{:S(2)}) collective-permute-start(bf16[272,768]{1,0:T(8,128)(2,1)S(1)} %get-tuple-element.9), channel_id=1, source_target_pairs={{3,4},{7,8},{11,12},{15,16},{19,20},{23,24},{27,28},{4,3},{8,7},{1... | collective-permute-start | bytes 1253384 | tf_op jit(solution)/shard_map/ppermute | solution.py:500
  30.7 0.5 collective-permute-done.2.second
  31.2 1.1 %merge.1 = bf16[272,768]{1,0:T(8,128)(2,1)S(1)} custom-call(bf16[272,768]{1,0:T(8,128)(2,1)S(1)} %get-tuple-element.11.first, bf16[272,768]{1,0:T(8,128)(2,1)S(1)} %collective-permute-done.2.second), custom_call_target="tpu_custom_call" | custom-call | tf_op jit(solution)/shard_map/merge/pallas_call | solution.py:433
  32.3 4.1 %collective-permute-start.3 = (bf16[272,768]{1,0:T(8,128)(2,1)S(1)}, bf16[272,768]{1,0:T(8,128)(2,1)S(1)}, u32[]{:S(2)}, u32[]{:S(2)}) collective-permute-start(bf16[272,768]{1,0:T(8,128)(2,1)S(1)} %merge.1), channel_id=1, source_target_pairs={{0,1},{1,0},{2,3},{3,2},{4,5},{5,4},{6,7},{7,6},{8,9},{9,8},{10,11... | collective-permute-start | bytes 1253384 | tf_op jit(solution)/shard_map/ppermute | solution.py:502
  36.4 0.0 copy-done
  36.4 11.9 %own_block.1.first = bf16[272,768]{1,0:T(8,128)(2,1)S(1)} custom-call(s32[1]{0:T(128)} %constant.21.clone.1.shift, bf16[144,768]{1,0:T(8,128)(2,1)S(1)} %copy-done, bf16[8192,768]{1,0:T(8,128)(2,1)} %corpus.3), custom_call_target="tpu_custom_call" | custom-call | flops 6442450944 | bytes 12582912 | tf_op jit(solution)/shard_map/own_block/pallas_call | solution.py:229
  48.3 0.0 collective-permute-done.4.third
  48.3 1.1 %collective-permute-done.3.second = bf16[272,768]{1,0:T(8,128)(2,1)S(1)} collective-permute-done((bf16[272,768]{1,0:T(8,128)(2,1)S(1)}, bf16[272,768]{1,0:T(8,128)(2,1)S(1)}, u32[]{:S(2)}, u32[]{:S(2)}) %collective-permute-start.3) | collective-permute-done | bytes 417824 | tf_op jit(solution)/shard_map/ppermute | solution.py:502
  49.4 0.0 copy-done.1
  49.4 0.0 copy-done.2
  49.4 1.8 %finish.1 = (bf16[128,2,768]{2,1,0:T(2,128)(2,1)}, f32[2,128]{1,0:T(2,128)}, f32[2,128]{1,0:T(2,128)}) custom-call(s32[2,128]{1,0:T(2,128)S(1)} %bitcast.8, s32[2,128]{1,0:T(2,128)S(1)} %bitcast.10, bf16[272,768]{1,0:T(8,128)(2,1)S(1)} %own_block.1.first, bf16[272,768]{1,0:T(8,128)(2,1)S(1)} %collective-permute-done.3.second, ...), custom_call_target="tpu_custom_call" | custom-call | tf_op jit(solution)/shard_map/finish/pallas_call | solution.py:473
Async XLA Ops:
  2.3 34.1 %copy-start = (bf16[144,768]{1,0:T(8,128)(2,1)S(1)}, bf16[144,768]{1,0:T(8,128)(2,1)}, u32[]{:S(2)}) copy-start(bf16[144,768]{1,0:T(8,128)(2,1)} %pack.1.message) | copy-start | bytes 663556
  2.3 7.5 %collective-permute-start = (bf16[144,768]{1,0:T(8,128)(2,1)}, bf16[144,768]{1,0:T(8,128)(2,1)S(1)}, u32[]{:S(2)}, u32[]{:S(2)}) collective-permute-start(bf16[144,768]{1,0:T(8,128)(2,1)} %pack.1.message), channel_id=1, source_target_pairs={{0,1},{1,0},{2,3},{3,2},{4,5},{5,4},{6,7},{7,6},{8,9},{9,8},{10,11... | collective-permute-start | bytes 663560 | tf_op jit(solution)/shard_map/ppermute | solution.py:496
  4.3 10.3 %collective-permute-start.1 = (bf16[144,768]{1,0:T(8,128)(2,1)}, bf16[144,768]{1,0:T(8,128)(2,1)S(1)}, u32[]{:S(2)}, u32[]{:S(2)}) collective-permute-start(bf16[144,768]{1,0:T(8,128)(2,1)} %pack.1.message), channel_id=1, source_target_pairs={{1,2},{3,4},{5,6},{7,8},{9,10},{11,12},{13,14},{15,16},{17,18},{19... | collective-permute-start | bytes 663560 | tf_op jit(solution)/shard_map/ppermute | solution.py:497
  28.5 20.9 %copy-start.1 = (s32[128,2]{0,1:T(2,128)S(1)}, s32[128,2]{0,1:T(2,128)}, u32[]{:S(2)}) copy-start(s32[128,2]{0,1:T(2,128)} %param.6) | copy-start | bytes 3076
  28.5 20.9 %copy-start.2 = (s32[128,2]{0,1:T(2,128)S(1)}, s32[128,2]{0,1:T(2,128)}, u32[]{:S(2)}) copy-start(s32[128,2]{0,1:T(2,128)} %param.7) | copy-start | bytes 3076
  28.5 2.7 %collective-permute-start.2 = (bf16[272,768]{1,0:T(8,128)(2,1)S(1)}, bf16[272,768]{1,0:T(8,128)(2,1)S(1)}, u32[]{:S(2)}, u32[]{:S(2)}) collective-permute-start(bf16[272,768]{1,0:T(8,128)(2,1)S(1)} %get-tuple-element.9), channel_id=1, source_target_pairs={{2,0},{6,4},{10,8},{14,12},{18,16},{22,20},{26,24},{30,28},{1,3},{... | collective-permute-start | bytes 1253384 | tf_op jit(solution)/shard_map/ppermute | solution.py:501
  29.8 18.5 %collective-permute-start.4 = (bf16[272,768]{1,0:T(8,128)(2,1)S(1)}, bf16[272,768]{1,0:T(8,128)(2,1)S(1)}, u32[]{:S(2)}, u32[]{:S(2)}) collective-permute-start(bf16[272,768]{1,0:T(8,128)(2,1)S(1)} %get-tuple-element.9), channel_id=1, source_target_pairs={{3,4},{7,8},{11,12},{15,16},{19,20},{23,24},{27,28},{4,3},{8,7},{1... | collective-permute-start | bytes 1253384 | tf_op jit(solution)/shard_map/ppermute | solution.py:500
  32.3 17.1 %collective-permute-start.3 = (bf16[272,768]{1,0:T(8,128)(2,1)S(1)}, bf16[272,768]{1,0:T(8,128)(2,1)S(1)}, u32[]{:S(2)}, u32[]{:S(2)}) collective-permute-start(bf16[272,768]{1,0:T(8,128)(2,1)S(1)} %merge.1), channel_id=1, source_target_pairs={{0,1},{1,0},{2,3},{3,2},{4,5},{5,4},{6,7},{7,6},{8,9},{9,8},{10,11... | collective-permute-start | bytes 1253384 | tf_op jit(solution)/shard_map/ppermute | solution.py:502

commit v10 on v9

--- a/solution.py
+++ b/solution.py
@@ -444,6 +444,7 @@
     queries = window_start.shape[1]
     unit = identity(queries)
     members = (first, second, third)
+    means = []
     for w in range(2):
         at = slice(w * queries, (w + 1) * queries)
         states = [columns_of(member, unit, w) for member in members]
@@ -452,7 +453,7 @@
         weighted = functools.reduce(
             jnp.add, [f * member[at, :].astype(F32) for f, member in zip(factors, members)]
         )
-        pooled[:, w, :] = (weighted / total).astype(BF16)
+        means.append(weighted / total)
 
         lines = [member[2 * queries :, at].astype(F32) for member in members]
         tops, totals, sums = (
@@ -464,6 +465,7 @@
         log_mass[w : w + 1, :] = best + jnp.log(total)
         count = (window_end[w : w + 1, :] - window_start[w : w + 1, :]).astype(F32)
         mean_score[w : w + 1, :] = functools.reduce(jnp.add, sums) / count
+    pooled[...] = jnp.stack(means, axis=1).astype(BF16)
 
 
 def finish(window_start, window_end, *members):

time: 51.4 us -> 51.9 us (level)
  no operation moved by 1% of the time
where the time goes in v10:
time: 51.9 us; the launch traced here: 51.7 us
  Pallas kernels  30.8 us (59%)
  starting transfers between devices  10.9 us (21%)
  waiting for transfers between devices  9.19 us (18%)
  between operations  0.72 us (1%)
    pallas_call x1, Pallas kernels, neighbours(): pl.pallas_call(neighbour_kernel, out_shape=(result, result), in_specs=[SM...  13.8 us
    pallas_call x1, Pallas kernels, own(): pl.pallas_call(own_kernel, out_shape=jax.ShapeDtypeStruct((2 * queries +...  11.9 us
    ppermute x1, waiting for transfers between devices, local(): far = lax.ppermute(message, AXES, past)  4.88 us
    ppermute x1, starting transfers between devices, local(): near_back = lax.ppermute(merge(near_part, relayed), AXES, across)  4.09 us
    ppermute x1, waiting for transfers between devices, local(): near = lax.ppermute(message, AXES, across)  2.75 us
    ppermute x1, starting transfers between devices, local(): far = lax.ppermute(message, AXES, past)  2.59 us
    pallas_call x1, Pallas kernels, finish(): pl.pallas_call(finish_kernel, out_shape=(jax.ShapeDtypeStruct((queries, 2...  2.27 us
    ppermute x1, starting transfers between devices, local(): near = lax.ppermute(message, AXES, across)  2.04 us
  transfers between devices with their start and end apart: 5, of which 4 were waited for; matrix products, arithmetic and copies ran while one was open for 0% of the time, Pallas kernels for 25%

profile of v10, /device:TPU:1, one launch (start us, length us, event | category | flops | bytes accessed | tf_op | source)
XLA Modules:
  0.0 51.7 jit_solution(979626539481087467)
XLA Ops:
  0.6 1.7 %pack.1.message = bf16[144,768]{1,0:T(8,128)(2,1)} custom-call(s32[1]{0:T(128)} %bitcast.2.base, bf16[128,768]{1,0:T(8,128)(2,1)} %queries.1, s32[2,128]{1,0:T(2,128)} %bitcast.7, s32[2,128]{1,0:T(2,128)} %bitcast.9), custom_call_target="tpu_custom_call" | custom-call | tf_op jit(solution)/shard_map/pack/pallas_call | solution.py:378
  2.3 0.0 copy-start
  2.3 2.0 %collective-permute-start = (bf16[144,768]{1,0:T(8,128)(2,1)}, bf16[144,768]{1,0:T(8,128)(2,1)S(1)}, u32[]{:S(2)}, u32[]{:S(2)}) collective-permute-start(bf16[144,768]{1,0:T(8,128)(2,1)} %pack.1.message), channel_id=1, source_target_pairs={{0,1},{1,0},{2,3},{3,2},{4,5},{5,4},{6,7},{7,6},{8,9},{9,8},{10,11... | collective-permute-start | bytes 663560 | tf_op jit(solution)/shard_map/ppermute | solution.py:498
  4.3 2.6 %collective-permute-start.1 = (bf16[144,768]{1,0:T(8,128)(2,1)}, bf16[144,768]{1,0:T(8,128)(2,1)S(1)}, u32[]{:S(2)}, u32[]{:S(2)}) collective-permute-start(bf16[144,768]{1,0:T(8,128)(2,1)} %pack.1.message), channel_id=1, source_target_pairs={{1,2},{3,4},{5,6},{7,8},{9,10},{11,12},{13,14},{15,16},{17,18},{19... | collective-permute-start | bytes 663560 | tf_op jit(solution)/shard_map/ppermute | solution.py:499
  6.9 0.1 pad_add_fusion.shifts
  7.0 2.7 %collective-permute-done.near = bf16[144,768]{1,0:T(8,128)(2,1)S(1)} collective-permute-done((bf16[144,768]{1,0:T(8,128)(2,1)}, bf16[144,768]{1,0:T(8,128)(2,1)S(1)}, u32[]{:S(2)}, u32[]{:S(2)}) %collective-permute-start) | collective-permute-done | bytes 221216 | tf_op jit(solution)/shard_map/ppermute | solution.py:498
  9.8 4.9 %collective-permute-done.1.far = bf16[144,768]{1,0:T(8,128)(2,1)S(1)} collective-permute-done((bf16[144,768]{1,0:T(8,128)(2,1)}, bf16[144,768]{1,0:T(8,128)(2,1)S(1)}, u32[]{:S(2)}, u32[]{:S(2)}) %collective-permute-start.1) | collective-permute-done | bytes 221216 | tf_op jit(solution)/shard_map/ppermute | solution.py:499
  14.6 13.8 %neighbour_blocks.1 = (bf16[272,768]{1,0:T(8,128)(2,1)S(1)}, bf16[272,768]{1,0:T(8,128)(2,1)S(1)}) custom-call(s32[2]{0:T(128)S(1)} %pad_add_fusion.shifts, bf16[144,768]{1,0:T(8,128)(2,1)S(1)} %collective-permute-done.near, bf16[144,768]{1,0:T(8,128)(2,1)S(1)} %collective-permute-done.1.far, bf16[8192,768]{1,0:T(8,128)(2,1)} %corpus.3), custom_call_target="tpu_custom_call" | custom-call | flops 6442450944 | bytes 12582912 | tf_op jit(solution)/shard_map/neighbour_blocks/pallas_call | solution.py:344
  28.5 0.0 copy-start.1
  28.5 0.0 copy-start.2
  28.5 1.3 %collective-permute-start.2 = (bf16[272,768]{1,0:T(8,128)(2,1)S(1)}, bf16[272,768]{1,0:T(8,128)(2,1)S(1)}, u32[]{:S(2)}, u32[]{:S(2)}) collective-permute-start(bf16[272,768]{1,0:T(8,128)(2,1)S(1)} %get-tuple-element.9), channel_id=1, source_target_pairs={{2,0},{6,4},{10,8},{14,12},{18,16},{22,20},{26,24},{30,28},{1,3},{... | collective-permute-start | bytes 1253384 | tf_op jit(solution)/shard_map/ppermute | solution.py:503
  29.8 0.9 %collective-permute-start.4 = (bf16[272,768]{1,0:T(8,128)(2,1)S(1)}, bf16[272,768]{1,0:T(8,128)(2,1)S(1)}, u32[]{:S(2)}, u32[]{:S(2)}) collective-permute-start(bf16[272,768]{1,0:T(8,128)(2,1)S(1)} %get-tuple-element.9), channel_id=1, source_target_pairs={{3,4},{7,8},{11,12},{15,16},{19,20},{23,24},{27,28},{4,3},{8,7},{1... | collective-permute-start | bytes 1253384 | tf_op jit(solution)/shard_map/ppermute | solution.py:502
  30.7 0.5 collective-permute-done.2.second
  31.2 1.1 %merge.1 = bf16[272,768]{1,0:T(8,128)(2,1)S(1)} custom-call(bf16[272,768]{1,0:T(8,128)(2,1)S(1)} %get-tuple-element.11.first, bf16[272,768]{1,0:T(8,128)(2,1)S(1)} %collective-permute-done.2.second), custom_call_target="tpu_custom_call" | custom-call | tf_op jit(solution)/shard_map/merge/pallas_call | solution.py:433
  32.3 4.1 %collective-permute-start.3 = (bf16[272,768]{1,0:T(8,128)(2,1)S(1)}, bf16[272,768]{1,0:T(8,128)(2,1)S(1)}, u32[]{:S(2)}, u32[]{:S(2)}) collective-permute-start(bf16[272,768]{1,0:T(8,128)(2,1)S(1)} %merge.1), channel_id=1, source_target_pairs={{0,1},{1,0},{2,3},{3,2},{4,5},{5,4},{6,7},{7,6},{8,9},{9,8},{10,11... | collective-permute-start | bytes 1253384 | tf_op jit(solution)/shard_map/ppermute | solution.py:504
  36.4 0.0 copy-done
  36.4 11.9 %own_block.1.first = bf16[272,768]{1,0:T(8,128)(2,1)S(1)} custom-call(s32[1]{0:T(128)} %constant.21.clone.1.shift, bf16[144,768]{1,0:T(8,128)(2,1)S(1)} %copy-done, bf16[8192,768]{1,0:T(8,128)(2,1)} %corpus.3), custom_call_target="tpu_custom_call" | custom-call | flops 6442450944 | bytes 12582912 | tf_op jit(solution)/shard_map/own_block/pallas_call | solution.py:229
  48.3 0.0 collective-permute-done.4.third
  48.3 1.1 %collective-permute-done.3.second = bf16[272,768]{1,0:T(8,128)(2,1)S(1)} collective-permute-done((bf16[272,768]{1,0:T(8,128)(2,1)S(1)}, bf16[272,768]{1,0:T(8,128)(2,1)S(1)}, u32[]{:S(2)}, u32[]{:S(2)}) %collective-permute-start.3) | collective-permute-done | bytes 417824 | tf_op jit(solution)/shard_map/ppermute | solution.py:504
  49.4 0.0 copy-done.1
  49.4 0.0 copy-done.2
  49.4 2.3 %finish.1 = (bf16[128,2,768]{2,1,0:T(2,128)(2,1)}, f32[2,128]{1,0:T(2,128)}, f32[2,128]{1,0:T(2,128)}) custom-call(s32[2,128]{1,0:T(2,128)S(1)} %bitcast.8, s32[2,128]{1,0:T(2,128)S(1)} %bitcast.10, bf16[272,768]{1,0:T(8,128)(2,1)S(1)} %own_block.1.first, bf16[272,768]{1,0:T(8,128)(2,1)S(1)} %collective-permute-done.3.second, ...), custom_call_target="tpu_custom_call" | custom-call | tf_op jit(solution)/shard_map/finish/pallas_call | solution.py:475
Async XLA Ops:
  2.3 34.1 %copy-start = (bf16[144,768]{1,0:T(8,128)(2,1)S(1)}, bf16[144,768]{1,0:T(8,128)(2,1)}, u32[]{:S(2)}) copy-start(bf16[144,768]{1,0:T(8,128)(2,1)} %pack.1.message) | copy-start | bytes 663556
  2.3 7.5 %collective-permute-start = (bf16[144,768]{1,0:T(8,128)(2,1)}, bf16[144,768]{1,0:T(8,128)(2,1)S(1)}, u32[]{:S(2)}, u32[]{:S(2)}) collective-permute-start(bf16[144,768]{1,0:T(8,128)(2,1)} %pack.1.message), channel_id=1, source_target_pairs={{0,1},{1,0},{2,3},{3,2},{4,5},{5,4},{6,7},{7,6},{8,9},{9,8},{10,11... | collective-permute-start | bytes 663560 | tf_op jit(solution)/shard_map/ppermute | solution.py:498
  4.3 10.3 %collective-permute-start.1 = (bf16[144,768]{1,0:T(8,128)(2,1)}, bf16[144,768]{1,0:T(8,128)(2,1)S(1)}, u32[]{:S(2)}, u32[]{:S(2)}) collective-permute-start(bf16[144,768]{1,0:T(8,128)(2,1)} %pack.1.message), channel_id=1, source_target_pairs={{1,2},{3,4},{5,6},{7,8},{9,10},{11,12},{13,14},{15,16},{17,18},{19... | collective-permute-start | bytes 663560 | tf_op jit(solution)/shard_map/ppermute | solution.py:499
  28.5 20.9 %copy-start.1 = (s32[128,2]{0,1:T(2,128)S(1)}, s32[128,2]{0,1:T(2,128)}, u32[]{:S(2)}) copy-start(s32[128,2]{0,1:T(2,128)} %param.6) | copy-start | bytes 3076
  28.5 20.9 %copy-start.2 = (s32[128,2]{0,1:T(2,128)S(1)}, s32[128,2]{0,1:T(2,128)}, u32[]{:S(2)}) copy-start(s32[128,2]{0,1:T(2,128)} %param.7) | copy-start | bytes 3076
  28.5 2.7 %collective-permute-start.2 = (bf16[272,768]{1,0:T(8,128)(2,1)S(1)}, bf16[272,768]{1,0:T(8,128)(2,1)S(1)}, u32[]{:S(2)}, u32[]{:S(2)}) collective-permute-start(bf16[272,768]{1,0:T(8,128)(2,1)S(1)} %get-tuple-element.9), channel_id=1, source_target_pairs={{2,0},{6,4},{10,8},{14,12},{18,16},{22,20},{26,24},{30,28},{1,3},{... | collective-permute-start | bytes 1253384 | tf_op jit(solution)/shard_map/ppermute | solution.py:503
  29.8 18.5 %collective-permute-start.4 = (bf16[272,768]{1,0:T(8,128)(2,1)S(1)}, bf16[272,768]{1,0:T(8,128)(2,1)S(1)}, u32[]{:S(2)}, u32[]{:S(2)}) collective-permute-start(bf16[272,768]{1,0:T(8,128)(2,1)S(1)} %get-tuple-element.9), channel_id=1, source_target_pairs={{3,4},{7,8},{11,12},{15,16},{19,20},{23,24},{27,28},{4,3},{8,7},{1... | collective-permute-start | bytes 1253384 | tf_op jit(solution)/shard_map/ppermute | solution.py:502
  32.3 17.1 %collective-permute-start.3 = (bf16[272,768]{1,0:T(8,128)(2,1)S(1)}, bf16[272,768]{1,0:T(8,128)(2,1)S(1)}, u32[]{:S(2)}, u32[]{:S(2)}) collective-permute-start(bf16[272,768]{1,0:T(8,128)(2,1)S(1)} %merge.1), channel_id=1, source_target_pairs={{0,1},{1,0},{2,3},{3,2},{4,5},{5,4},{6,7},{7,6},{8,9},{9,8},{10,11... | collective-permute-start | bytes 1253384 | tf_op jit(solution)/shard_map/ppermute | solution.py:504
